TPU v7x, 32 devices: a whole 2x2x4 slice. The times are simulated.
32 devices in a mesh: seq: 8 (over y, x, core), tp: 4 (over z).
Axes of the slice: x: 2, y: 2, z: 4, core: 2. Of those that a mesh axis runs over, the one named last changes fastest.
Arguments:
- hidden_in: bfloat16 [6144, 2048], P('seq'), may hold values from -6 to 6
- gain_in: bfloat16 [2048], replicated, may hold values from 0.5 to 1.5
- w_input: bfloat16 [2048, 2048], P('seq', 'tp'), may hold values from -0.125 to 0.125
- w_forget: bfloat16 [2048, 2048], P('seq', 'tp'), may hold values from -0.125 to 0.125
- forget_bias: float32 [2048], replicated, may hold values from -1 to 11
- w_outgate: bfloat16 [2048, 2048], P('seq', 'tp'), may hold values from -0.125 to 0.125
- state_gain: bfloat16 [2048], replicated, may hold values from 0.5 to 1.5
- w_output: bfloat16 [2048, 2048], P('tp', 'seq'), may hold values from -0.125 to 0.125
- gain_mid: bfloat16 [2048], replicated, may hold values from 0.5 to 1.5
- w_gate: bfloat16 [2048, 5632], P('seq', 'tp'), may hold values from -0.125 to 0.125
- w_up: bfloat16 [2048, 5632], P('seq', 'tp'), may hold values from -0.125 to 0.125
- w_down: bfloat16 [5632, 2048], P('tp', 'seq'), may hold values from -0.078125 to 0.078125
- lengths: int32 [2], replicated, may hold values from 1152 to 4992, as said below
- layer_index: int32 [1], replicated, may hold values from 0 to 23
- cotangent: bfloat16 [6144, 2048], P('seq'), may hold values from -6 to 6
Outputs:
- block_out: bfloat16 [6144, 2048], P('seq', 'tp')
- grad_in: float32 [6144, 2048], P('seq', 'tp')
- grad_gain_in: float32 [2048], replicated
- grad_w_input: float32 [2048, 2048], P('seq', 'tp')
- grad_w_forget: float32 [2048, 2048], P('seq', 'tp')
- grad_forget_bias: float32 [2048], replicated
- grad_w_outgate: float32 [2048, 2048], P('seq', 'tp')
- grad_state_gain: float32 [2048], replicated
- grad_w_output: float32 [2048, 2048], P('tp', 'seq')
- grad_gain_mid: float32 [2048], replicated
- grad_w_gate: float32 [2048, 5632], P('seq', 'tp')
- grad_w_up: float32 [2048, 5632], P('seq', 'tp')
- grad_w_down: float32 [5632, 2048], P('tp', 'seq')
- rms_stats: float32 [3], replicated
Inputs may be any that keep to these rules, and one draw needn't show every extreme that they name: The first sequence fills slots from 0, the second follows it directly, padding fills the rest; fewer than 384 slots are padding; lengths[1] lies from 1152 to 1535.
All inputs are finite; a program needn't handle non-finite values.
Results may differ from a plain program's by a relative error of at most 0.0081.
Values may be sent and summed in bfloat16 or wider, within the bound.
A program may use at most 256 MiB of HBM per device.

v0:
```python
import jax
import jax.numpy as jnp
from jax import lax
from jax.sharding import PartitionSpec as P

LAYERS = 24


norm_epsilon = 1e-06


def entering(value, axis, join, neutral, backward):
    count, mine = (lax.axis_size(axis), lax.axis_index(axis))
    pieces = jax.tree.map(lambda part: lax.all_gather(part, axis), value)
    if backward:
        pieces = jax.tree.map(lambda part: part[::-1], pieces)
        mine = count - 1 - mine
    total = jax.tree.map(
        lambda part, zero: jnp.full_like(part, 0) + jnp.asarray(zero, part.dtype), value, neutral
    )

    def hop(position, total):
        longer = join(total, jax.tree.map(lambda part: part[position], pieces))
        return jax.tree.map(lambda new, old: jnp.where(position < mine, new, old), longer, total)

    return lax.fori_loop(0, count - 1, hop, total)


def plain_dot(left, right):
    return jnp.dot(left, right, preferred_element_type=jnp.float32)


def outer_dot(left, right):
    return lax.dot_general(
        left, right, (((0,), (0,)), ((), ())), preferred_element_type=jnp.float32
    )


def inner_dot(left, right):
    return lax.dot_general(
        left, right, (((1,), (1,)), ((), ())), preferred_element_type=jnp.float32
    )


def chain(earlier, later):
    return (earlier[0] * later[0], later[0] * earlier[1] + later[1])


def silu_slope(values):
    sig = jax.nn.sigmoid(values)
    return sig * (1.0 + values * (1.0 - sig))


def place(values, offset, width):
    return lax.dynamic_update_slice(jnp.zeros((width,), jnp.float32), values, (offset,))


def on_device(
    hidden_in,
    gain_in,
    w_input,
    w_forget,
    forget_bias,
    w_outgate,
    state_gain,
    w_output,
    gain_mid,
    w_gate,
    w_up,
    w_down,
    lengths,
    layer_index,
    cotangent,
):
    rows_here = hidden_in.shape[0]
    width = hidden_in.shape[1]
    channels = w_input.shape[1]
    offset = lax.axis_index("tp") * channels
    positions = lax.axis_index("seq") * rows_here + jnp.arange(rows_here, dtype=jnp.int32)
    total = lengths[0] + lengths[1]
    valid = (positions < total).astype(jnp.float32)[:, None]
    starts = ((positions == 0) | (positions == lengths[0])).astype(jnp.float32)[:, None]
    bound = layer_index[0].astype(jnp.float32) / LAYERS
    ones_row = jnp.ones((channels,), jnp.float32)
    zero_row = jnp.zeros((channels,), jnp.float32)
    wide_input, wide_forget, wide_outgate, wide_output, wide_gate, wide_up, wide_down = (
        lax.all_gather(w_input, "seq", axis=0, tiled=True),
        lax.all_gather(w_forget, "seq", axis=0, tiled=True),
        lax.all_gather(w_outgate, "seq", axis=0, tiled=True),
        lax.all_gather(w_output, "seq", axis=1, tiled=True),
        lax.all_gather(w_gate, "seq", axis=0, tiled=True),
        lax.all_gather(w_up, "seq", axis=0, tiled=True),
        lax.all_gather(w_down, "seq", axis=1, tiled=True),
    )
    inputs_f = hidden_in.astype(jnp.float32)
    inv_in = lax.rsqrt(jnp.mean(inputs_f * inputs_f, axis=-1, keepdims=True) + norm_epsilon)
    hat_in = inputs_f * inv_in
    gain_in_f = gain_in.astype(jnp.float32)
    normed_in = (hat_in * gain_in_f).astype(jnp.bfloat16)
    bias_local = lax.dynamic_slice_in_dim(forget_bias, offset, channels, 0)
    input_pre = plain_dot(normed_in, wide_input)
    forget_pre = plain_dot(normed_in, wide_forget) + bias_local
    outgate_pre = plain_dot(normed_in, wide_outgate)
    forget_sig = jax.nn.sigmoid(forget_pre)
    forget_gate = bound + (1.0 - bound) * forget_sig
    forget_eff = forget_gate * (1.0 - starts)
    input_act = jax.nn.silu(input_pre)
    drive = input_act * (1.0 - forget_gate) * valid
    prod_local, state_local = lax.associative_scan(chain, (forget_eff, drive), axis=0)
    scanned = entering((prod_local[-1], state_local[-1]), "seq", chain, (ones_row, zero_row), False)
    state_in = scanned[1]
    drive_first = jnp.concatenate(
        [drive[:1] + forget_eff[:1] * state_in[None, :], drive[1:]], axis=0
    )
    states = lax.associative_scan(chain, (forget_eff, drive_first), axis=0)[1]
    state_total = lax.psum(jnp.sum(states * states, axis=-1), "tp")
    inv_state = lax.rsqrt(state_total / width + norm_epsilon)[:, None]
    hat_state = states * inv_state
    gain_state = lax.dynamic_slice_in_dim(state_gain, offset, channels, 0).astype(jnp.float32)
    outgate_act = jax.nn.silu(outgate_pre)
    gated_out = (hat_state * gain_state * outgate_act).astype(jnp.bfloat16)
    mixed_part = plain_dot(gated_out, wide_output)
    gain_mid_f = gain_mid.astype(jnp.float32)
    mixed = lax.psum(mixed_part, "tp")
    resid_mid = inputs_f + mixed
    inv_mid = lax.rsqrt(jnp.mean(resid_mid * resid_mid, axis=-1, keepdims=True) + norm_epsilon)
    hat_mid = resid_mid * inv_mid
    normed_mid = (hat_mid * gain_mid_f).astype(jnp.bfloat16)
    mixed_cols = lax.dynamic_slice_in_dim(mixed, offset, channels, 1)
    resid_cols = lax.dynamic_slice_in_dim(resid_mid, offset, channels, 1)
    hat_mid_cols = lax.dynamic_slice_in_dim(hat_mid, offset, channels, 1)
    gate_pre = plain_dot(normed_mid, wide_gate)
    up_pre = plain_dot(normed_mid, wide_up)
    gate_act = jax.nn.silu(gate_pre)
    hidden_glu = (gate_act * up_pre).astype(jnp.bfloat16)
    glu_cols = lax.psum_scatter(
        plain_dot(hidden_glu, wide_down), "tp", scatter_dimension=1, tiled=True
    )
    out_cols = resid_cols + glu_cols
    cot_f = cotangent.astype(jnp.float32)
    grad_w_down = outer_dot(hidden_glu, cotangent)
    grad_hidden = inner_dot(cotangent, wide_down)
    grad_gate = (grad_hidden * up_pre * silu_slope(gate_pre)).astype(jnp.bfloat16)
    grad_up = (grad_hidden * gate_act).astype(jnp.bfloat16)
    grad_w_gate = outer_dot(normed_mid, grad_gate)
    grad_w_up = outer_dot(normed_mid, grad_up)
    normed_part = inner_dot(grad_gate, wide_gate) + inner_dot(grad_up, wide_up)
    grad_normed_mid = lax.psum(normed_part, "tp")
    scaled_mid = grad_normed_mid * gain_mid_f
    grad_resid = cot_f + inv_mid * (
        scaled_mid - hat_mid * jnp.mean(scaled_mid * hat_mid, axis=-1, keepdims=True)
    )
    grad_nm_cols = lax.dynamic_slice_in_dim(grad_normed_mid, offset, channels, 1)
    grad_resid_cols = lax.dynamic_slice_in_dim(grad_resid, offset, channels, 1)
    grad_mixed = grad_resid.astype(jnp.bfloat16)
    grad_gain_mid = jnp.sum(grad_nm_cols * hat_mid_cols, axis=0)
    grad_w_output = outer_dot(gated_out, grad_mixed)
    grad_gated = inner_dot(grad_mixed, wide_output)
    grad_gain_state = jnp.sum(grad_gated * hat_state * outgate_act, axis=0)
    grad_outgate = (grad_gated * hat_state * gain_state * silu_slope(outgate_pre)).astype(
        jnp.bfloat16
    )
    weighted = grad_gated * outgate_act * gain_state
    state_inner = lax.psum(jnp.sum(weighted * hat_state, axis=-1), "tp")
    grad_states_out = inv_state * (weighted - hat_state * (state_inner / width)[:, None])
    forget_next = jnp.concatenate([forget_eff[1:], ones_row[None, :]], axis=0)
    prod_back, local_back = lax.associative_scan(
        chain, (forget_next[::-1], grad_states_out[::-1]), axis=0
    )
    prod_back = prod_back[::-1]
    local_back = local_back[::-1]
    arriving = entering(
        (prod_local[-1], forget_eff[0] * local_back[0]), "seq", chain, (ones_row, zero_row), True
    )[1]
    grad_last = jnp.concatenate(
        [grad_states_out[:-1], grad_states_out[-1:] + arriving[None, :]], axis=0
    )
    grad_states = lax.associative_scan(chain, (forget_next[::-1], grad_last[::-1]), axis=0)[1][::-1]
    states_prev = jnp.concatenate([state_in[None, :], states[:-1]], axis=0)
    grad_input = (grad_states * (1.0 - forget_gate) * valid * silu_slope(input_pre)).astype(
        jnp.bfloat16
    )
    grad_gate_f = grad_states * states_prev * (1.0 - starts) - grad_states * input_act * valid
    grad_forget = (grad_gate_f * (1.0 - bound) * forget_sig * (1.0 - forget_sig)).astype(
        jnp.bfloat16
    )
    grad_forget_bias = jnp.sum(grad_forget.astype(jnp.float32), axis=0)
    grad_w_input = outer_dot(normed_in, grad_input)
    grad_w_forget = outer_dot(normed_in, grad_forget)
    grad_w_outgate = outer_dot(normed_in, grad_outgate)
    input_part = (
        inner_dot(grad_input, wide_input)
        + inner_dot(grad_forget, wide_forget)
        + inner_dot(grad_outgate, wide_outgate)
    )
    grad_normed_in = lax.psum_scatter(input_part, "tp", scatter_dimension=1, tiled=True)
    hat_cols = lax.dynamic_slice_in_dim(hat_in, offset, channels, 1)
    scaled_in = grad_normed_in * lax.dynamic_slice_in_dim(gain_in_f, offset, channels, 0)
    input_inner = lax.psum(jnp.sum(scaled_in * hat_cols, axis=-1), "tp")
    grad_in = grad_resid_cols + inv_in * (scaled_in - hat_cols * (input_inner / width)[:, None])
    grad_gain_in = jnp.sum(grad_normed_in * hat_cols, axis=0)
    weight_sums = (
        lax.psum_scatter(grad_w_input, "seq", scatter_dimension=0, tiled=True),
        lax.psum_scatter(grad_w_forget, "seq", scatter_dimension=0, tiled=True),
        lax.psum_scatter(grad_w_outgate, "seq", scatter_dimension=0, tiled=True),
        lax.psum_scatter(grad_w_output, "seq", scatter_dimension=1, tiled=True),
        lax.psum_scatter(grad_w_gate, "seq", scatter_dimension=0, tiled=True),
        lax.psum_scatter(grad_w_up, "seq", scatter_dimension=0, tiled=True),
        lax.psum_scatter(grad_w_down, "seq", scatter_dimension=1, tiled=True),
    )
    square_sums = jnp.stack(
        [
            jnp.sum(valid * mixed_cols * mixed_cols),
            jnp.sum(valid * glu_cols * glu_cols),
            jnp.sum(valid * out_cols * out_cols),
        ]
    )
    vectors = jnp.stack(
        [
            place(grad_gain_in, offset, width),
            place(grad_forget_bias, offset, width),
            place(grad_gain_state, offset, width),
            place(grad_gain_mid, offset, width),
        ]
    )
    square_total, vector_total = lax.psum((square_sums, vectors), ("seq", "tp"))
    rms_stats = jnp.sqrt(square_total / (total.astype(jnp.float32) * width))
    return (
        out_cols.astype(jnp.bfloat16),
        grad_in,
        vector_total[0],
        weight_sums[0],
        weight_sums[1],
        vector_total[1],
        weight_sums[2],
        vector_total[2],
        weight_sums[3],
        vector_total[3],
        weight_sums[4],
        weight_sums[5],
        weight_sums[6],
        rms_stats,
    )


def solution(mesh):
    in_specs = (
        P("seq", None),
        P(),
        P("seq", "tp"),
        P("seq", "tp"),
        P(),
        P("seq", "tp"),
        P(),
        P("tp", "seq"),
        P(),
        P("seq", "tp"),
        P("seq", "tp"),
        P("tp", "seq"),
        P(),
        P(),
        P("seq", None),
    )
    out_specs = (
        P("seq", "tp"),
        P("seq", "tp"),
        P(),
        P("seq", "tp"),
        P("seq", "tp"),
        P(),
        P("seq", "tp"),
        P(),
        P("tp", "seq"),
        P(),
        P("seq", "tp"),
        P("seq", "tp"),
        P("tp", "seq"),
        P(),
    )
    return jax.shard_map(
        on_device, mesh=mesh, in_specs=in_specs, out_specs=out_specs, check_vma=False
    )
```

profile of v0, /device:TPU:0, one launch (start us, length us, event | category | flops | bytes accessed | tf_op | source)
XLA Modules:
  0.0 1792.5 jit_solution(1632482259559157769)
XLA Ops:
  18.0 22.5 %all-gather.11.cloned.1.call-done = bf16[2048,512]{1,0:T(8,128)(2,1)} async-done(((bf16[256,512]{1,0:T(8,128)(2,1)}), bf16[2048,512]{1,0:T(8,128)(2,1)}) %all-gather.11.cloned.1.call-update) | async-done | bytes 2097168 | tf_op jit(solution)/shard_map/all_gather | solution.py:87
  45.1 25.2 %all-gather.13.cloned.1.call-done = bf16[2048,512]{1,0:T(8,128)(2,1)} async-done(((bf16[256,512]{1,0:T(8,128)(2,1)}), bf16[2048,512]{1,0:T(8,128)(2,1)}) %all-gather.13.cloned.1.call-update) | async-done | bytes 2097168 | tf_op jit(solution)/shard_map/all_gather | solution.py:88
  70.4 6.2 fusion.17
  80.8 5.1 slice.871
  210.7 5.2 pad.619
  216.6 8.9 all-gather.1
  226.0 8.4 all-gather
  235.0 5.4 while.28
  316.4 11.7 psum.49
  328.1 6.4 multiply_convert_fusion.7
  334.5 6.3 fusion.82
  343.2 217.9 %all-reduce.95.cloned.1.call-done = f32[768,2048]{1,0:T(8,128)} async-done(((f32[768,2048]{1,0:T(8,128)}), f32[768,2048]{1,0:T(8,128)}) %all-reduce.95.cloned.1.call-update) | async-done | bytes 6291472 | tf_op jit(solution)/shard_map/psum | solution.py:124
  561.1 7.5 multiply_reduce_fusion.1
  575.7 29.5 %all-gather.19.cloned.1.call-done = bf16[2048,1408]{1,0:T(8,128)(2,1)} async-done(((bf16[256,1408]{1,0:T(8,128)(2,1)}), bf16[2048,1408]{1,0:T(8,128)(2,1)}) %all-gather.19.cloned.1.call-update) | async-done | bytes 5767184 | tf_op jit(solution)/shard_map/all_gather | solution.py:91
  605.1 9.7 fusion.83
  614.8 35.5 %all-gather.21.cloned.1.call-done = bf16[2048,1408]{1,0:T(8,128)(2,1)} async-done(((bf16[256,1408]{1,0:T(8,128)(2,1)}), bf16[2048,1408]{1,0:T(8,128)(2,1)}) %all-gather.21.cloned.1.call-update) | async-done | bytes 5767184 | tf_op jit(solution)/shard_map/all_gather | solution.py:92
  650.4 9.6 fusion.84
  660.0 36.6 %all-gather.23.cloned.1.call-done = bf16[1408,2048]{1,0:T(8,128)(2,1)} async-done(((bf16[1408,256]{1,0:T(8,128)(2,1)}), bf16[1408,2048]{1,0:T(8,128)(2,1)}) %all-gather.23.cloned.1.call-update) | async-done | bytes 5767184 | tf_op jit(solution)/shard_map/all_gather | solution.py:93
  696.6 12.5 multiply_convert_fusion.2
  709.1 8.7 fusion.86
  717.9 7.0 convolution_add_fusion
  744.1 6.8 slice.1005
  751.0 6.8 slice.1012
  757.8 7.0 slice.1003
  767.0 9.7 fusion.85
  776.7 171.2 %all-reduce.97.cloned.1.call-done = f32[768,2048]{1,0:T(8,128)} async-done(((f32[768,2048]{1,0:T(8,128)}), f32[768,2048]{1,0:T(8,128)}) %all-reduce.97.cloned.1.call-update) | async-done | bytes 6291472 | tf_op jit(solution)/shard_map/psum | solution.py:148
  947.9 5.4 multiply_reduce_fusion
  964.6 9.9 psum.52
  980.6 6.9 slice.1007
  1093.9 9.2 all-gather.2
  1103.2 5.3 while.29
  1112.7 6.8 slice.1079
  1156.7 10.4 rev.16
  1167.1 5.5 fusion.3
  1182.2 6.7 fusion.11
  1195.9 10.0 fusion.89
  1206.0 10.0 fusion.90
  1216.3 11.5 fusion.91
  1227.8 5.3 fusion.68
  1243.3 47.3 %reduce-scatter.12.cloned.1.call-done = f32[768,512]{1,0:T(8,128)} async-done(((f32[768,2048]{1,0:T(8,128)}), f32[768,512]{1,0:T(8,128)}) %reduce-scatter.12.cloned.1.call-update) | async-done | bytes 1572880 | tf_op jit(solution)/shard_map/reduce_scatter | solution.py:196
  1293.0 11.0 psum.53
  1304.0 39.0 %all-reduce.91 = (f32[4,2048]{1,0:T(4,128)S(1)}, f32[3]{0:T(128)S(1)}) all-reduce(f32[4,2048]{1,0:T(4,128)S(1)} %pad_maximum_fusion.32, f32[3]{0:T(128)S(1)} %pad_maximum_fusion.48), channel_id=1, replica_groups=mesh['seq'=8,'tp'=4] {'seq','tp'}, use_global_device_ids=true, to_apply=%region_21.22 | all-reduce | flops 8195 | bytes 65560 | tf_op jit(solution)/shard_map/psum | solution.py:226
  1347.6 54.8 %reduce-scatter.18.cloned.1.call-done = f32[256,512]{1,0:T(8,128)} async-done(((f32[2048,512]{1,0:T(8,128)}), f32[256,512]{1,0:T(8,128)}) %reduce-scatter.18.cloned.1.call-update) | async-done | bytes 524304 | tf_op jit(solution)/shard_map/reduce_scatter | solution.py:205
  1402.4 90.8 %reduce-scatter.22.cloned.1.call-done = f32[256,1408]{1,0:T(8,128)} async-done(((f32[2048,1408]{1,0:T(8,128)}), f32[256,1408]{1,0:T(8,128)}) %reduce-scatter.22.cloned.1.call-update) | async-done | bytes 1441808 | tf_op jit(solution)/shard_map/reduce_scatter | solution.py:207
  1493.1 90.7 %reduce-scatter.24.cloned.1.call-done = f32[256,1408]{1,0:T(8,128)} async-done(((f32[2048,1408]{1,0:T(8,128)}), f32[256,1408]{1,0:T(8,128)}) %reduce-scatter.24.cloned.1.call-update) | async-done | bytes 1441808 | tf_op jit(solution)/shard_map/reduce_scatter | solution.py:208
  1583.9 90.8 %reduce-scatter.26.cloned.1.call-done = f32[1408,256]{1,0:T(8,128)} async-done(((f32[1408,2048]{1,0:T(8,128)}), f32[1408,256]{1,0:T(8,128)}) %reduce-scatter.26.cloned.1.call-update) | async-done | bytes 1441808 | tf_op jit(solution)/shard_map/reduce_scatter | solution.py:209
  1674.6 55.1 %reduce-scatter.14.cloned.1.call-done = f32[256,512]{1,0:T(8,128)} async-done(((f32[2048,512]{1,0:T(8,128)}), f32[256,512]{1,0:T(8,128)}) %reduce-scatter.14.cloned.1.call-update) | async-done | bytes 524304 | tf_op jit(solution)/shard_map/reduce_scatter | solution.py:203
  1729.7 55.5 %reduce-scatter.16.cloned.1.call-done = f32[256,512]{1,0:T(8,128)} async-done(((f32[2048,512]{1,0:T(8,128)}), f32[256,512]{1,0:T(8,128)}) %reduce-scatter.16.cloned.1.call-update) | async-done | bytes 524304 | tf_op jit(solution)/shard_map/reduce_scatter | solution.py:204
  (806 shorter events, 458.7 us)
Async XLA Ops:
  7.2 33.4 %copy-start.3 = (bf16[768,2048]{1,0:T(8,128)(2,1)S(1)}, bf16[768,2048]{1,0:T(8,128)(2,1)}, u32[]{:S(2)}) copy-start(bf16[768,2048]{1,0:T(8,128)(2,1)} %param.19) | copy-start | bytes 9437188
  7.2 33.4 %all-gather.11.cloned.1.call-start = ((), (), s32[]{:S(2)}) async-start(), calls=%async_computation.9 | async-start | bytes 2359296 | tf_op jit(solution)/shard_map/all_gather | solution.py:87
  7.9 62.4 %all-gather.13.cloned.1.call-start = ((), (), s32[]{:S(2)}) async-start(), calls=%async_computation.10 | async-start | bytes 2359296 | tf_op jit(solution)/shard_map/all_gather | solution.py:88
  8.7 319.4 %all-gather.15.cloned.1.call-start = ((), (), s32[]{:S(2)}) async-start(), calls=%async_computation.11 | async-start | bytes 2359296 | tf_op jit(solution)/shard_map/all_gather | solution.py:89
  9.4 325.1 %all-gather.17.cloned.1.call-start = ((), (), s32[]{:S(2)}) async-start(), calls=%async_computation.12 | async-start | bytes 2359296 | tf_op jit(solution)/shard_map/all_gather | solution.py:90
  10.0 551.1 %all-reduce.95.cloned.1.call-start = ((), (), s32[]{:S(2)}) async-start(), calls=%async_computation.13 | async-start | bytes 12582912 | tf_op jit(solution)/shard_map/psum | solution.py:124
  12.7 57.7 %copy-start.83 = (f32[768]{0:T(1024)}, f32[768]{0:T(1024)S(1)}, u32[]{:S(2)}) copy-start(f32[768]{0:T(1024)S(1)} %add_rsqrt_fusion.2) | copy-start | bytes 9220
  12.7 57.7 %copy-start.117 = (f32[2048]{0:T(1024)}, f32[2048]{0:T(1024)S(1)}, u32[]{:S(2)}) copy-start(f32[2048]{0:T(1024)S(1)} %convert_element_type.73) | copy-start | bytes 24580
  15.2 55.1 %copy-start.100 = (f32[768]{0:T(1024)}, f32[768]{0:T(1024)S(1)}, u32[]{:S(2)}) copy-start(f32[768]{0:T(1024)S(1)} %convert_subtract_fusion) | copy-start | bytes 9220
  15.3 55.1 %copy-start.102 = (f32[768]{0:T(1024)}, f32[768]{0:T(1024)S(1)}, u32[]{:S(2)}) copy-start(f32[768]{0:T(1024)S(1)} %fusion.64) | copy-start | bytes 9220
  80.7 10.7 copy-start.6
  110.6 65.5 %copy-start.14 = (f32[384,512]{1,0:T(8,128)S(1)}, f32[384,512]{1,0:T(8,128)}, u32[]{:S(2)}) copy-start(f32[384,512]{1,0:T(8,128)} %get-tuple-element.303) | copy-start | bytes 2359300
  133.9 13.3 copy-start.65
  149.3 33.3 %copy-start.63 = (f32[5,512]{1,0:T(8,128)}, f32[5,512]{1,0:T(8,128)S(1)}, u32[]{:S(2)}) copy-start(f32[5,512]{1,0:T(8,128)S(1)} %slice.900) | copy-start | bytes 30724
  208.1 26.9 %copy-start.71 = (f32[512]{0:T(512)S(1)}, f32[512]{0:T(512)}, u32[]{:S(2)}) copy-start(f32[512]{0:T(512)} %custom-call) | copy-start | bytes 6148
  208.2 32.3 %copy-start.5 = (f32[768,512]{1,0:T(8,128)S(1)}, f32[768,512]{1,0:T(8,128)}, u32[]{:S(2)}) copy-start(f32[768,512]{1,0:T(8,128)} %get-tuple-element.298) | copy-start | bytes 4718596
  259.2 23.5 %copy-start.66 = (f32[6,512]{1,0:T(8,128)S(1)}, f32[6,512]{1,0:T(8,128)}, u32[]{:S(2)}) copy-start(f32[6,512]{1,0:T(8,128)} %copy-done.65) | copy-start | bytes 36868
  261.1 32.7 %copy-start.27 = (f32[192,512]{1,0:T(8,128)S(1)}, f32[192,512]{1,0:T(8,128)}, u32[]{:S(2)}) copy-start(f32[192,512]{1,0:T(8,128)} %multiply_add_fusion.9) | copy-start | bytes 1179652
  293.9 10.6 slice-start.14
  294.7 9.9 slice-start.10
  315.0 13.0 copy-start.84
  315.0 13.0 copy-start.107
  315.0 13.0 copy-start.118
  340.9 264.3 %all-gather.19.cloned.1.call-start = ((), (), s32[]{:S(2)}) async-start(), calls=%async_computation.14 | async-start | bytes 6488064 | tf_op jit(solution)/shard_map/all_gather | solution.py:91
  341.4 308.9 %all-gather.21.cloned.1.call-start = ((), (), s32[]{:S(2)}) async-start(), calls=%async_computation.15 | async-start | bytes 6488064 | tf_op jit(solution)/shard_map/all_gather | solution.py:92
  342.2 354.4 %all-gather.23.cloned.1.call-start = ((), (), s32[]{:S(2)}) async-start(), calls=%async_computation.16 | async-start | bytes 6488064 | tf_op jit(solution)/shard_map/all_gather | solution.py:93
  342.9 605.0 %all-reduce.97.cloned.1.call-start = ((), (), s32[]{:S(2)}) async-start(), calls=%async_computation.18 | async-start | bytes 12582912 | tf_op jit(solution)/shard_map/psum | solution.py:148
  724.9 442.2 %reduce-scatter.10.cloned.1.call-start = ((), (), s32[]{:S(2)}) async-start(), calls=%async_computation.17 | async-start | bytes 7864320 | tf_op jit(solution)/shard_map/reduce_scatter | solution.py:136
  776.7 176.7 %slice-start = ((s8[6291456]{0:T(1024)(128)(4,1)}), s8[2097152]{0:T(1024)(128)(4,1)S(1)}, s32[]{:S(2)}) async-start(s8[6291456]{0:T(1024)(128)(4,1)} %bitcast.78), calls=%async_computation.27 | async-start | bytes 4194304
  776.7 513.9 %reduce-scatter.12.cloned.1.call-start = ((), (), s32[]{:S(2)}) async-start(), calls=%async_computation.19 | async-start | bytes 7864320 | tf_op jit(solution)/shard_map/reduce_scatter | solution.py:196
  960.0 14.5 copy-start.12
  979.9 11.5 copy-start.7
  1037.9 10.7 copy-start.67
  1090.0 13.2 copy-start.78
  1112.0 11.5 copy-start.8
  1125.1 13.6 copy-start.15
  1156.7 10.4 copy-start.10
  1156.7 10.4 copy-start.73
  1156.7 10.4 copy-start.101
  1156.7 10.4 copy-start.103
  1181.1 166.5 %reduce-scatter.20.cloned.1.call-start = ((), (), s32[]{:S(2)}) async-start(), calls=%async_computation.23 | async-start | bytes 4718592 | tf_op jit(solution)/shard_map/reduce_scatter | solution.py:206
  1188.9 213.5 %reduce-scatter.18.cloned.1.call-start = ((), (), s32[]{:S(2)}) async-start(), calls=%async_computation.22 | async-start | bytes 4718592 | tf_op jit(solution)/shard_map/reduce_scatter | solution.py:205
  1195.9 297.2 %reduce-scatter.22.cloned.1.call-start = ((), (), s32[]{:S(2)}) async-start(), calls=%async_computation.24 | async-start | bytes 12976128 | tf_op jit(solution)/shard_map/reduce_scatter | solution.py:207
  1205.9 377.9 %reduce-scatter.24.cloned.1.call-start = ((), (), s32[]{:S(2)}) async-start(), calls=%async_computation.25 | async-start | bytes 12976128 | tf_op jit(solution)/shard_map/reduce_scatter | solution.py:208
  1216.0 458.6 %reduce-scatter.26.cloned.1.call-start = ((), (), s32[]{:S(2)}) async-start(), calls=%async_computation.26 | async-start | bytes 12976128 | tf_op jit(solution)/shard_map/reduce_scatter | solution.py:209
  1227.8 501.9 %reduce-scatter.14.cloned.1.call-start = ((), (), s32[]{:S(2)}) async-start(), calls=%async_computation.20 | async-start | bytes 4718592 | tf_op jit(solution)/shard_map/reduce_scatter | solution.py:203
  1233.1 552.1 %reduce-scatter.16.cloned.1.call-start = ((), (), s32[]{:S(2)}) async-start(), calls=%async_computation.21 | async-start | bytes 4718592 | tf_op jit(solution)/shard_map/reduce_scatter | solution.py:204
  1290.6 53.0 %copy-start.13 = (f32[768,512]{1,0:T(8,128)S(1)}, f32[768,512]{1,0:T(8,128)}, u32[]{:S(2)}) copy-start(f32[768,512]{1,0:T(8,128)} %reduce-scatter.12.cloned.1.call-done) | copy-start | bytes 4718596
  (113 other events, 538.5 us)
Sparse Core Ops, SparseCore 0:
  9.9 30.5 all-gather.10
  42.4 27.8 all-gather.12
  72.3 27.8 all-gather.14
  101.9 28.1 all-gather.16
  341.0 220.0 all-reduce.94
  562.8 42.2 all-gather.18
  607.0 43.3 all-gather.20
  652.2 44.3 all-gather.22
  725.0 222.8 all-reduce.96
  950.1 109.9 reduce-scatter.9
  1181.2 109.3 reduce-scatter.11
  1294.4 52.4 reduce-scatter.19
  1351.2 51.1 reduce-scatter.17
  1406.3 86.7 reduce-scatter.21
  1497.0 86.7 reduce-scatter.23
  1587.8 86.7 reduce-scatter.25
  1678.4 51.3 reduce-scatter.13
  1733.9 51.3 reduce-scatter.15
where the time goes:
time: 1810 us; the launch traced here: 1790 us
  waiting for transfers between devices  1030 us (57%)
  local copies, waits for them, and re-layouts  365 us (20%)
  matrix products  147 us (8%)
  other arithmetic  133 us (7%)
  blocking collectives  97.9 us (5%)
  between operations  19.5 us (1%)
    psum x1, waiting for transfers between devices, on_device(): mixed = lax.psum(mixed_part, 'tp')  218 us
    psum x1, waiting for transfers between devices, on_device(): grad_normed_mid = lax.psum(normed_part, 'tp')  171 us
    slice x59, local copies, waits for them, and re-layouts, on_device(): lax.associative_scan(chain, (forget_next[::-1], grad_states_out[::-1]), a...  119 us
    slice x61, local copies, waits for them, and re-layouts, on_device(): lax.associative_scan(chain, (forget_eff, drive), axis=0)  94.1 us
    reduce_scatter x1, waiting for transfers between devices, on_device(): lax.psum_scatter(grad_w_gate, 'seq', scatter_dimension=0, tiled=True)  90.8 us
    reduce_scatter x1, waiting for transfers between devices, on_device(): lax.psum_scatter(grad_w_down, 'seq', scatter_dimension=1, tiled=True)  90.8 us
    reduce_scatter x1, waiting for transfers between devices, on_device(): lax.psum_scatter(grad_w_up, 'seq', scatter_dimension=0, tiled=True)  90.7 us
    reduce_scatter x1, waiting for transfers between devices, on_device(): lax.psum_scatter(grad_w_forget, 'seq', scatter_dimension=0, tiled=True)  55.5 us
  transfers between devices with their start and end apart: 18, of which 14 were waited for; matrix products, arithmetic and copies ran while one was open for 33% of the time, Pallas kernels for 0%

commit v1 on v0

v1 whole, which is shorter than its diff:
```python
import functools

import jax
import jax.numpy as jnp
from jax import lax
from jax.experimental import pallas as pl
from jax.experimental.pallas import tpu as pltpu
from jax.sharding import PartitionSpec as P

LAYERS = 24
EPS = 1e-06
MESH = pl.DeviceIdType.MESH
BF = jnp.bfloat16
F32 = jnp.float32
VM = pl.BlockSpec(memory_space=pltpu.VMEM)
HB = pl.BlockSpec(memory_space=pl.ANY)
LANE = 128
SEG = 8
CHUNKS = 8
VMEM_LIMIT = 60 * 1024 * 1024


def nn(left, right):
    return jnp.dot(left, right, preferred_element_type=F32)


def nt(left, right):
    return lax.dot_general(left, right, (((1,), (1,)), ((), ())), preferred_element_type=F32)


def tn(left, right):
    return lax.dot_general(left, right, (((0,), (0,)), ((), ())), preferred_element_type=F32)


def shape(dims, dtype):
    return jax.ShapeDtypeStruct(dims, dtype)


def get(ref, at):
    return jnp.concatenate([ref[g, at, :] for g in range(ref.shape[0])], axis=1)


def put(ref, at, values):
    for g in range(ref.shape[0]):
        ref[g, at, :] = values[:, g * LANE : (g + 1) * LANE]


def row_tile(rows):
    return rows // 3 if rows % 48 == 0 else rows


def greet_all(n, t, seq, tp):
    barrier = pltpu.get_barrier_semaphore()

    def along_seq(o, c):
        pl.semaphore_signal(barrier, inc=1, device_id=(lax.rem(seq + o, n), tp), device_id_type=MESH)
        return c

    def along_tp(o, c):
        pl.semaphore_signal(barrier, inc=1, device_id=(seq, lax.rem(tp + o, t)), device_id_type=MESH)
        return c

    lax.fori_loop(1, n, along_seq, 0)
    lax.fori_loop(1, t, along_tp, 0)
    pl.semaphore_wait(barrier, n - 1 + t - 1)


def greet_line(t, seq, tp):
    barrier = pltpu.get_barrier_semaphore()

    def along_tp(o, c):
        pl.semaphore_signal(barrier, inc=1, device_id=(seq, lax.rem(tp + o, t)), device_id_type=MESH)
        return c

    lax.fori_loop(1, t, along_tp, 0)
    pl.semaphore_wait(barrier, t - 1)


def spread(size, me, slots, send, recv, target):
    def copy(o, slot):
        return pltpu.make_async_remote_copy(
            src_ref=slots.at[slot],
            dst_ref=slots.at[slot],
            send_sem=send.at[o],
            recv_sem=recv.at[slot],
            device_id=target(lax.rem(me + o, size)),
            device_id_type=MESH,
        )

    def go(o, c):
        copy(o, me).start()
        return c

    def done(o, c):
        copy(o, lax.rem(me + o, size)).wait_recv()
        return c

    def sent(o, c):
        copy(o, me).wait_send()
        return c

    lax.fori_loop(1, size, go, 0)
    lax.fori_loop(1, size, done, 0)
    lax.fori_loop(1, size, sent, 0)


def row_sums(values):
    ones = jnp.ones((8, values.shape[1]), BF)
    high = values.astype(BF)
    rest = values - high.astype(F32)
    low = rest.astype(BF)
    return nt(ones, high) + nt(ones, low)


def sum_over_tp(part, t, seq, tp, slots, send, recv):
    slots[tp] = part
    spread(t, tp, slots, send, recv, lambda k: (seq, k))
    total = slots[0]
    for k in range(1, t):
        total = total + slots[k]
    return jnp.transpose(total)[:, :1]


def carry_over_seq(prod, state, n, seq, tp, slots, send, recv, backward):
    slots[seq] = jnp.concatenate([prod, state] + [jnp.zeros_like(prod)] * 6, axis=0)
    spread(n, seq, slots, send, recv, lambda k: (k, tp))

    def hop(i, total):
        j = n - 1 - i if backward else i
        block = slots[j]
        longer = block[1:2] + block[0:1] * total
        inside = (j > seq) if backward else (j < seq)
        return jnp.where(inside, longer, total)

    return lax.fori_loop(0, n, hop, jnp.zeros_like(prod))


def line_all_reduce(t, seq, tp, rows, chunks, partial, send, buf, sems, finish):
    s_in, s_out, r_buf = sems
    step = rows // chunks
    half = t // 2
    depth = jnp.where(tp < half, tp, t - 1 - tp)
    inner = jnp.where(tp < half, tp + 1, tp - 1)
    outer = jnp.where(tp < half, tp - 1, tp + 1)
    outer = jnp.where(depth > 0, outer, inner)
    middle = (depth == half - 1).astype(jnp.int32)

    def part_of(k):
        return pl.ds(pl.multiple_of(k * step, step), step)

    def inward(k, slot):
        return pltpu.make_async_remote_copy(
            src_ref=send.at[part_of(k)],
            dst_ref=buf.at[slot, part_of(k)],
            send_sem=s_in.at[k],
            recv_sem=r_buf.at[slot, k],
            device_id=(seq, inner),
            device_id_type=MESH,
        )

    def outward(k):
        return pltpu.make_async_remote_copy(
            src_ref=buf.at[1, part_of(k)],
            dst_ref=buf.at[1, part_of(k)],
            send_sem=s_out.at[k],
            recv_sem=r_buf.at[1, k],
            device_id=(seq, outer),
            device_id_type=MESH,
        )

    def first(k):
        part = partial(k)

        @pl.when(depth > 0)
        def _():
            inward(k, 0).wait_recv()
            send[part_of(k), :] = (part + buf[0, part_of(k), :].astype(F32)).astype(BF)

        @pl.when(depth == 0)
        def _():
            send[part_of(k), :] = part.astype(BF)

        inward(k, middle).start()

    def second(k):
        inward(k, 1).wait_recv()

        @pl.when(middle == 1)
        def _():
            both = send[part_of(k), :].astype(F32) + buf[1, part_of(k), :].astype(F32)
            buf[1, part_of(k), :] = both.astype(BF)

        @pl.when(depth > 0)
        def _():
            outward(k).start()

        finish(k)

    def both(k, c):
        @pl.when(k < chunks)
        def _():
            first(k)

        @pl.when(k > 0)
        def _():
            second(k - 1)

        return c

    lax.fori_loop(0, chunks + 1, both, 0)

    def drain(k, c):
        inward(k, middle).wait_send()

        @pl.when(depth > 0)
        def _():
            outward(k).wait_send()

        return c

    lax.fori_loop(0, chunks, drain, 0)


def line_reduce_scatter(t, seq, tp, rows, chunks, own, right, left, sems, finish):
    s_r, r_r, s_l, r_l = sems
    step = rows // chunks

    def part_of(k):
        return pl.ds(pl.multiple_of(k * step, step), step)

    def rightward(q, k):
        return pltpu.make_async_remote_copy(
            src_ref=own.at[q, part_of(k)],
            dst_ref=right.at[q, part_of(k)],
            send_sem=s_r.at[q, k],
            recv_sem=r_r.at[q, k],
            device_id=(seq, lax.rem(tp + 1, t)),
            device_id_type=MESH,
        )

    def leftward(q, k):
        return pltpu.make_async_remote_copy(
            src_ref=own.at[q, part_of(k)],
            dst_ref=left.at[q, part_of(k)],
            send_sem=s_l.at[q, k],
            recv_sem=r_l.at[q, k],
            device_id=(seq, lax.rem(tp + t - 1, t)),
            device_id_type=MESH,
        )

    def add(q, k, other):
        own[q, part_of(k), :] = (
            own[q, part_of(k), :].astype(F32) + other[q, part_of(k), :].astype(F32)
        ).astype(BF)

    def step_of(i, c):
        k = i // (t - 1)
        j = lax.rem(i, t - 1)

        @pl.when(t - 1 - j > tp)
        def _():
            q = t - 1 - j

            @pl.when(tp > 0)
            def _():
                rightward(q, k).wait_recv()
                add(q, k, right)

            rightward(q, k).start()

        @pl.when(j < tp)
        def _():
            @pl.when(tp < t - 1)
            def _():
                leftward(j, k).wait_recv()
                add(j, k, left)

            leftward(j, k).start()

        return c

    lax.fori_loop(0, chunks * (t - 1), step_of, 0)

    def last(k, c):
        @pl.when(tp == 0)
        def _():
            leftward(tp, k).wait_recv()
            finish(k, own[tp, part_of(k), :].astype(F32) + left[tp, part_of(k), :].astype(F32))

        @pl.when(tp == t - 1)
        def _():
            rightward(tp, k).wait_recv()
            finish(k, own[tp, part_of(k), :].astype(F32) + right[tp, part_of(k), :].astype(F32))

        @pl.when((tp > 0) & (tp < t - 1))
        def _():
            leftward(tp, k).wait_recv()
            rightward(tp, k).wait_recv()
            finish(
                k,
                own[tp, part_of(k), :].astype(F32)
                + left[tp, part_of(k), :].astype(F32)
                + right[tp, part_of(k), :].astype(F32),
            )

        return c

    lax.fori_loop(0, chunks, last, 0)

    def drain(i, c):
        k = i // (t - 1)
        j = lax.rem(i, t - 1)

        @pl.when(t - 1 - j > tp)
        def _():
            rightward(t - 1 - j, k).wait_send()

        @pl.when(j < tp)
        def _():
            leftward(j, k).wait_send()

        return c

    lax.fori_loop(0, chunks * (t - 1), drain, 0)


def mixer_forward(
    n, t, width,
    normed, x, w1, crow, gmid, valid, starts,
    ipre, fpre, opre, feff, states, gated, nmid, mixed, invst, invmid,
    prod, ssq, cslots, zslots, send, buf,
    cs, cr, zs, zr, s_in, s_out, r_buf,
):
    seq, tp = lax.axis_index("seq"), lax.axis_index("tp")
    greet_all(n, t, seq, tp)
    rows, depth = normed.shape
    chan = ipre.shape[1]
    tile = row_tile(rows)
    bias, sgain, bound = crow[0:1, :], crow[1:2, :], crow[2:3, :]

    def project(i, c):
        at = pl.ds(pl.multiple_of(i * tile, tile), tile)
        pre = nn(normed[at, :], w1[:, : 3 * chan])
        a = pre[:, :chan]
        f = pre[:, chan : 2 * chan] + bias
        ipre[at, :] = a
        fpre[at, :] = f
        opre[at, :] = pre[:, 2 * chan :]
        gate = bound + (1.0 - bound) * jax.nn.sigmoid(f)
        put(feff, at, gate * (1.0 - starts[at, :]))
        shifted = pl.ds(pl.multiple_of(i * tile + 8, 8), tile)
        put(states, shifted, a * jax.nn.sigmoid(a) * (1.0 - gate) * valid[at, :])
        return c

    lax.fori_loop(0, rows // tile, project, 0)
    put(feff, slice(rows, rows + 8), jnp.ones((8, chan), F32))

    length = rows // SEG

    def scan(i, c):
        p, h = c
        at, shifted = pl.ds(i, SEG, stride=length), pl.ds(i + 8, SEG, stride=length)
        f = get(feff, at)
        h = f * h + get(states, shifted)
        p = f * p
        put(states, shifted, h)
        put(prod, at, p)
        return p, h

    p, h = lax.fori_loop(
        0, length, scan, (jnp.ones((SEG, chan), F32), jnp.zeros((SEG, chan), F32))
    )
    block_p, block_h = p[0:1], h[0:1]
    for s in range(1, SEG):
        block_h = h[s : s + 1] + p[s : s + 1] * block_h
        block_p = p[s : s + 1] * block_p
    arriving = carry_over_seq(block_p, block_h, n, seq, tp, cslots, cs, cr, False)
    put(states, slice(0, 8), jnp.broadcast_to(arriving, (8, chan)))
    for s in range(SEG):
        at = slice(s * length, (s + 1) * length)
        shifted = slice(s * length + 8, (s + 1) * length + 8)
        whole = get(states, shifted) + get(prod, at) * arriving
        put(states, shifted, whole)
        ssq[at, :] = whole * whole
        arriving = h[s : s + 1] + p[s : s + 1] * arriving
    total = sum_over_tp(row_sums(ssq[...]), t, seq, tp, zslots, zs, zr)
    invst[...] = lax.rsqrt(total / width + EPS)

    def gating(i, c):
        at = pl.ds(pl.multiple_of(i * tile, tile), tile)
        shifted = pl.ds(pl.multiple_of(i * tile + 8, 8), tile)
        o = opre[at, :]
        gated[at, :] = (
            get(states, shifted) * invst[at, :] * sgain * (o * jax.nn.sigmoid(o))
        ).astype(BF)
        return c

    lax.fori_loop(0, rows // tile, gating, 0)

    step = rows // CHUNKS

    def partial(k):
        at = pl.ds(pl.multiple_of(k * step, step), step)
        return nt(gated[at, :], w1[:, 3 * chan :])

    def finish(k):
        at = pl.ds(pl.multiple_of(k * step, step), step)
        total = buf[1, at, :]
        mixed[at, :] = total
        resid = x[at, :].astype(F32) + total.astype(F32)
        inv = lax.rsqrt(jnp.mean(resid * resid, axis=-1, keepdims=True) + EPS)
        invmid[at, :] = inv
        nmid[at, :] = (resid * inv * gmid[...]).astype(BF)

    line_all_reduce(t, seq, tp, rows, CHUNKS, partial, send, buf, (s_in, s_out, r_buf), finish)


def feed_forward(
    nmid_h, cot_h, w2_h, gnm_h, glu_h, dw2_h,
    nmid, cot, wg, wu, wd, hid, gg, gu, gnm, glu, stage,
    s_w, s_a, s_o, s_d,
):
    rows, width = nmid.shape
    ff = wg.shape[1]
    tile = row_tile(rows)
    act_copies = [
        pltpu.make_async_copy(nmid_h, nmid, s_a.at[0]),
        pltpu.make_async_copy(cot_h, cot, s_a.at[1]),
    ]
    w_copies = [
        pltpu.make_async_copy(w2_h.at[:, pl.ds(j * ff, ff)], w, s_w.at[j])
        for j, w in enumerate((wg, wu, wd))
    ]
    for copy in (act_copies[0], w_copies[0], w_copies[1], act_copies[1], w_copies[2]):
        copy.start()
    for copy in (act_copies[0], w_copies[0], w_copies[1], act_copies[1], w_copies[2]):
        copy.wait()

    def out_copy(i, which):
        at = pl.ds(pl.multiple_of(i * tile, tile), tile)
        src, dst = ((gnm, gnm_h), (glu, glu_h))[which]
        return pltpu.make_async_copy(src.at[at], dst.at[at], s_o.at[which, i])

    def block(i, c):
        at = pl.ds(pl.multiple_of(i * tile, tile), tile)
        g = nn(nmid[at, :], wg[...])
        u = nn(nmid[at, :], wu[...])
        gh = nn(cot[at, :], wd[...])
        sig = jax.nn.sigmoid(g)
        act = g * sig
        hid[at, :] = (act * u).astype(BF)
        gg[at, :] = (gh * u * (sig * (1.0 + g * (1.0 - sig)))).astype(BF)
        gu[at, :] = (gh * act).astype(BF)
        gnm[at, :] = (nt(gg[at, :], wg[...]) + nt(gu[at, :], wu[...])).astype(BF)
        out_copy(i, 0).start()
        glu[at, :] = nt(hid[at, :], wd[...]).astype(BF)
        out_copy(i, 1).start()
        return c

    lax.fori_loop(0, rows // tile, block, 0)

    span = min(512, width)
    pieces = width // span

    def d_copy(i, slot):
        j = i // pieces
        r = lax.rem(i, pieces)
        return pltpu.make_async_copy(
            stage.at[slot],
            dw2_h.at[pl.ds(pl.multiple_of(r * span, span), span), pl.ds(pl.multiple_of(j * ff, LANE), ff)],
            s_d.at[slot],
        )

    for j, (left, right) in enumerate(((nmid, gg), (nmid, gu), (cot, hid))):

        def slab(r, c, j=j, left=left, right=right):
            i = j * pieces + r
            slot = lax.rem(i, 2)

            @pl.when(i >= 2)
            def _():
                d_copy(i - 2, slot).wait()

            at = pl.ds(pl.multiple_of(r * span, span), span)
            stage[slot] = tn(left[:, at], right[...]).astype(BF)
            d_copy(i, slot).start()
            return c

        lax.fori_loop(0, pieces, slab, 0)
    d_copy(3 * pieces - 2, (3 * pieces) % 2).wait()
    d_copy(3 * pieces - 1, (3 * pieces + 1) % 2).wait()

    def drain(i, c):
        out_copy(i, 0).wait()
        out_copy(i, 1).wait()
        return c

    lax.fori_loop(0, rows // tile, drain, 0)


def mid_backward(
    t, width,
    gnm_part, x, mixed, invmid, cot, gmid,
    gmix, gres, ggain,
    send, buf, wide, s_in, s_out, r_buf,
):
    seq, tp = lax.axis_index("seq"), lax.axis_index("tp")
    greet_line(t, seq, tp)
    rows = x.shape[0]
    chan = gres.shape[1]
    step = rows // CHUNKS
    ggain[...] = jnp.zeros_like(ggain)

    def partial(k):
        at = pl.ds(pl.multiple_of(k * step, step), step)
        return gnm_part[at, :].astype(F32)

    def finish(k):
        at = pl.ds(pl.multiple_of(k * step, step), step)
        g = buf[1, at, :].astype(F32)
        inv = invmid[at, :]
        hat = (x[at, :].astype(F32) + mixed[at, :].astype(F32)) * inv
        ggain[0:1, :] += jnp.sum(g * hat, axis=0, keepdims=True)
        e = g * gmid[...]
        mean = jnp.mean(e * hat, axis=-1, keepdims=True)
        out = cot[at, :].astype(F32) + inv * (e - hat * mean)
        wide[...] = out
        gmix[at, :] = out.astype(BF)
        gres[at, :] = wide[:, pl.ds(pl.multiple_of(tp * chan, LANE), chan)]

    line_all_reduce(t, seq, tp, rows, CHUNKS, partial, send, buf, (s_in, s_out, r_buf), finish)


def mixer_backward(
    n, t, width,
    gmix, normed, w1, gated, states, feff, ipre, fpre, opre, invst, valid, starts, crow,
    gni, dw1, vecs,
    grad, weighted, prod, inner, out3, cslots, zslots,
    cs, cr, zs, zr,
):
    seq, tp = lax.axis_index("seq"), lax.axis_index("tp")
    greet_all(n, t, seq, tp)
    rows = gmix.shape[0]
    chan = ipre.shape[1]
    tile = row_tile(rows)
    sgain, bound = crow[1:2, :], crow[2:3, :]
    vecs[...] = jnp.zeros_like(vecs)

    def gates(i, c):
        at = pl.ds(pl.multiple_of(i * tile, tile), tile)
        shifted = pl.ds(pl.multiple_of(i * tile + 8, 8), tile)
        g = nn(gmix[at, :], grad[...])
        hat = get(states, shifted) * invst[at, :]
        o = opre[at, :]
        sig = jax.nn.sigmoid(o)
        q = o * sig
        vecs[2:3, :] += jnp.sum(g * hat * q, axis=0, keepdims=True)
        out3[at, 2 * chan :] = (g * hat * sgain * (sig * (1.0 + o * (1.0 - sig)))).astype(BF)
        w = g * q * sgain
        put(weighted, at, w)
        inner[at, :] = w * hat
        return c

    grad[...] = w1[:, 3 * chan :]
    lax.fori_loop(0, rows // tile, gates, 0)
    dot = sum_over_tp(row_sums(inner[...]), t, seq, tp, zslots, zs, zr) / width
    inner[:, 0:1] = dot

    def leaving(i, c):
        at = pl.ds(pl.multiple_of(i * tile, tile), tile)
        shifted = pl.ds(pl.multiple_of(i * tile + 8, 8), tile)
        inv = invst[at, :]
        put(weighted, at, inv * (get(weighted, at) - get(states, shifted) * inv * inner[at, 0:1]))
        return c

    lax.fori_loop(0, rows // tile, leaving, 0)

    length = rows // SEG

    def scan(i, c):
        p, h = c
        r = length - 1 - i
        at = pl.ds(r, SEG, stride=length)
        f = get(feff, pl.ds(r + 1, SEG, stride=length))
        h = f * h + get(weighted, at)
        p = f * p
        put(weighted, at, h)
        put(prod, at, p)
        return p, h

    p, h = lax.fori_loop(
        0, length, scan, (jnp.ones((SEG, chan), F32), jnp.zeros((SEG, chan), F32))
    )
    block_p, block_h = p[SEG - 1 : SEG], h[SEG - 1 : SEG]
    for s in range(SEG - 2, -1, -1):
        block_h = h[s : s + 1] + p[s : s + 1] * block_h
        block_p = p[s : s + 1] * block_p
    first = get(feff, slice(0, 1))
    arriving = carry_over_seq(first * block_p, first * block_h, n, seq, tp, cslots, cs, cr, True)
    bias_sum = jnp.zeros((1, chan), F32)
    for s in range(SEG - 1, -1, -1):
        at = slice(s * length, (s + 1) * length)
        gs = get(weighted, at) + get(prod, at) * arriving
        arriving = h[s : s + 1] + p[s : s + 1] * arriving
        a = ipre[at, :]
        sa = jax.nn.sigmoid(a)
        act = a * sa
        sf = jax.nn.sigmoid(fpre[at, :])
        gate = bound + (1.0 - bound) * sf
        ok = valid[at, :]
        out3[at, :chan] = (gs * (1.0 - gate) * ok * (sa * (1.0 + a * (1.0 - sa)))).astype(BF)
        before = get(states, slice(s * length + 7, (s + 1) * length + 7))
        gate_grad = gs * before * (1.0 - starts[at, :]) - gs * act * ok
        gf = (gate_grad * (1.0 - bound) * sf * (1.0 - sf)).astype(BF)
        out3[at, chan : 2 * chan] = gf
        bias_sum = bias_sum + jnp.sum(gf.astype(F32), axis=0, keepdims=True)
    vecs[1:2, :] = bias_sum

    def spread_in(i, c):
        at = pl.ds(pl.multiple_of(i * tile, tile), tile)
        gni[at, :] = nt(out3[at, :], w1[:, : 3 * chan]).astype(BF)
        return c

    lax.fori_loop(0, rows // tile, spread_in, 0)

    span = 512

    def slab(r, c):
        at = pl.ds(pl.multiple_of(r * span, span), span)
        dw1[at, : 3 * chan] = tn(normed[:, at], out3[...]).astype(BF)
        dw1[at, 3 * chan :] = tn(gmix[:, at], gated[...]).astype(BF)
        return c

    lax.fori_loop(0, width // span, slab, 0)


def closing(
    n, t, width,
    glu_h, gni_h, x_h, mixed_h, gres, invin, valid, gain_in, vecs, ggain,
    out, gin, allvec,
    xc, mc, own_a, right_a, left_a, own_b, right_b, left_b, scaled, inner, zslots, vslots,
    s_x, s_own, sr_a, rr_a, sl_a, rl_a, sr_b, rr_b, sl_b, rl_b, zs, zr, vs, vr, ts, tr,
):
    seq, tp = lax.axis_index("seq"), lax.axis_index("tp")
    rows, chan = gres.shape
    mine = pl.ds(pl.multiple_of(tp * chan, LANE), chan)
    locals_ = [
        pltpu.make_async_copy(x_h.at[:, mine], xc, s_x.at[0]),
        pltpu.make_async_copy(mixed_h.at[:, mine], mc, s_x.at[1]),
    ]
    for q in range(t):
        locals_.append(pltpu.make_async_copy(glu_h.at[:, pl.ds(q * chan, chan)], own_a.at[q], s_own.at[0, q]))
        locals_.append(pltpu.make_async_copy(gni_h.at[:, pl.ds(q * chan, chan)], own_b.at[q], s_own.at[1, q]))
    for copy in locals_:
        copy.start()
    greet_all(n, t, seq, tp)
    for copy in locals_:
        copy.wait()
    half = CHUNKS // 2
    step = rows // half
    vslots[seq] = vecs[...]

    def finish_b(k, values):
        at = pl.ds(pl.multiple_of(k * step, step), step)
        hat = xc[at, :].astype(F32) * invin[at, :]
        s = values * gain_in[...]
        scaled[at, :] = s
        inner[at, :] = s * hat
        vslots[seq, 0:1, :] += jnp.sum(values * hat, axis=0, keepdims=True)

    def finish_a(k, values):
        at = pl.ds(pl.multiple_of(k * step, step), step)
        ok = valid[at, :]
        m = mc[at, :].astype(F32)
        full = xc[at, :].astype(F32) + m + values
        out[at, :] = full.astype(BF)
        vslots[seq, 4:5, :] += jnp.sum(ok * m * m, axis=0, keepdims=True)
        vslots[seq, 5:6, :] += jnp.sum(ok * values * values, axis=0, keepdims=True)
        vslots[seq, 6:7, :] += jnp.sum(ok * full * full, axis=0, keepdims=True)

    line_reduce_scatter(t, seq, tp, rows, half, own_b, right_b, left_b, (sr_b, rr_b, sl_b, rl_b), finish_b)
    line_reduce_scatter(t, seq, tp, rows, half, own_a, right_a, left_a, (sr_a, rr_a, sl_a, rl_a), finish_a)
    vslots[seq, 3:4, :] = ggain[0:1, :]
    dot = sum_over_tp(row_sums(inner[...]), t, seq, tp, zslots, zs, zr) / width
    gin[...] = gres[...] + invin[...] * (scaled[...] - xc[...].astype(F32) * invin[...] * dot)
    spread(n, seq, vslots, vs, vr, lambda k: (k, tp))
    total = vslots[0]
    for k in range(1, n):
        total = total + vslots[k]
    allvec[tp] = total
    spread(t, tp, allvec, ts, tr, lambda k: (seq, k))


DMA = pltpu.SemaphoreType.DMA


def params(collective=None, limit=VMEM_LIMIT):
    if collective is None:
        return pltpu.CompilerParams(vmem_limit_bytes=limit)
    return pltpu.CompilerParams(
        vmem_limit_bytes=limit, collective_id=collective, has_side_effects=True
    )


def line_sems(chunks):
    return [DMA((chunks,)), DMA((chunks,)), DMA((2, chunks))]


def on_device(
    n, t,
    hidden_in, gain_in, w_input, w_forget, forget_bias, w_outgate, state_gain, w_output,
    gain_mid, w_gate, w_up, w_down, lengths, layer_index, cotangent,
):
    rows, width = hidden_in.shape
    chan = w_input.shape[1]
    ff = w_gate.shape[1]
    ffp = -(-ff // LANE) * LANE
    tp = lax.axis_index("tp")
    offset = tp * chan

    def padded(w):
        return w if ffp == ff else jnp.pad(w, ((0, 0), (0, ffp - ff)))

    w1 = lax.all_gather(
        jnp.concatenate([w_input, w_forget, w_outgate, w_output.T], axis=1), "seq", axis=0, tiled=True
    )
    w2 = lax.all_gather(
        jnp.concatenate([padded(w_gate), padded(w_up), padded(w_down.T)], axis=1),
        "seq", axis=0, tiled=True,
    )

    positions = lax.axis_index("seq") * rows + jnp.arange(rows, dtype=jnp.int32)
    total = lengths[0] + lengths[1]
    valid = (positions < total).astype(F32)[:, None]
    starts = ((positions == 0) | (positions == lengths[0])).astype(F32)[:, None]
    bound = layer_index[0].astype(F32) / LAYERS
    inputs_f = hidden_in.astype(F32)
    inv_in = lax.rsqrt(jnp.mean(inputs_f * inputs_f, axis=-1, keepdims=True) + EPS)
    normed_in = (inputs_f * inv_in * gain_in.astype(F32)).astype(BF)

    def cols(vector):
        return lax.dynamic_slice_in_dim(vector, offset, chan, 0).astype(F32)

    crow = jnp.concatenate(
        [
            cols(forget_bias)[None],
            cols(state_gain)[None],
            jnp.broadcast_to(bound, (1, chan)),
            jnp.zeros((5, chan), F32),
        ],
        axis=0,
    )
    gmid = gain_mid.astype(F32)[None]
    plane = shape((rows, chan), F32)
    column = shape((rows, 1), F32)

    def groups(more=0):
        return shape((chan // LANE, rows + more, LANE), F32)

    wide16 = shape((rows, width), BF)

    ipre, fpre, opre, feff, states, gated, nmid, mixed, invst, invmid = pl.pallas_call(
        functools.partial(mixer_forward, n, t, width),
        out_shape=[
            plane, plane, plane,
            groups(8), groups(8),
            shape((rows, chan), BF), wide16, wide16, column, column,
        ],
        in_specs=[VM] * 7,
        out_specs=[VM] * 10,
        scratch_shapes=[
            pltpu.VMEM(groups().shape, F32),
            pltpu.VMEM((rows, chan), F32),
            pltpu.VMEM((n, 8, chan), F32),
            pltpu.VMEM((t, 8, rows), F32),
            pltpu.VMEM((rows, width), BF),
            pltpu.VMEM((2, rows, width), BF),
            DMA((n,)), DMA((n,)), DMA((t,)), DMA((t,)),
            *line_sems(CHUNKS),
        ],
        compiler_params=params(1),
        name="mixer_forward",
    )(normed_in, hidden_in, w1, crow, gmid, valid, starts)

    gnm_part, glu_part, dw2 = pl.pallas_call(
        feed_forward,
        out_shape=[wide16, wide16, shape((width, 3 * ffp), BF)],
        in_specs=[HB] * 3,
        out_specs=[HB] * 3,
        scratch_shapes=[
            pltpu.VMEM((rows, width), BF),
            pltpu.VMEM((rows, width), BF),
            pltpu.VMEM((width, ffp), BF),
            pltpu.VMEM((width, ffp), BF),
            pltpu.VMEM((width, ffp), BF),
            pltpu.VMEM((rows, ffp), BF),
            pltpu.VMEM((rows, ffp), BF),
            pltpu.VMEM((rows, ffp), BF),
            pltpu.VMEM((rows, width), BF),
            pltpu.VMEM((rows, width), BF),
            pltpu.VMEM((2, min(512, width), ffp), BF),
            DMA((3,)), DMA((2,)), DMA((2, rows // row_tile(rows))), DMA((2,)),
        ],
        compiler_params=params(),
        cost_estimate=pl.CostEstimate(
            flops=18 * rows * width * ffp, bytes_accessed=50_000_000, transcendentals=0
        ),
        name="feed_forward",
    )(nmid, cotangent, w2)

    sums2 = lax.psum_scatter(dw2, "seq", scatter_dimension=0, tiled=True)

    gmix, gres, ggain = pl.pallas_call(
        functools.partial(mid_backward, t, width),
        out_shape=[wide16, plane, shape((8, width), F32)],
        in_specs=[VM] * 6,
        out_specs=[VM] * 3,
        scratch_shapes=[
            pltpu.VMEM((rows, width), BF),
            pltpu.VMEM((2, rows, width), BF),
            pltpu.VMEM((rows // CHUNKS, width), F32),
            *line_sems(CHUNKS),
        ],
        compiler_params=params(2),
        name="mid_backward",
    )(gnm_part, hidden_in, mixed, invmid, cotangent, gmid)

    gni_part, dw1, vecs = pl.pallas_call(
        functools.partial(mixer_backward, n, t, width),
        out_shape=[wide16, shape((width, 4 * chan), BF), shape((8, chan), F32)],
        in_specs=[VM] * 13,
        out_specs=[VM] * 3,
        scratch_shapes=[
            pltpu.VMEM((width, chan), BF),
            pltpu.VMEM(groups().shape, F32),
            pltpu.VMEM(groups().shape, F32),
            pltpu.VMEM((rows, chan), F32),
            pltpu.VMEM((rows, 3 * chan), BF),
            pltpu.VMEM((n, 8, chan), F32),
            pltpu.VMEM((t, 8, rows), F32),
            DMA((n,)), DMA((n,)), DMA((t,)), DMA((t,)),
        ],
        compiler_params=params(3),
        name="mixer_backward",
    )(gmix, normed_in, w1, gated, states, feff, ipre, fpre, opre, invst, valid, starts, crow)

    sums1 = lax.psum_scatter(dw1, "seq", scatter_dimension=0, tiled=True)

    half = CHUNKS // 2
    shard_sems = [DMA((t, half))] * 4
    shard_bufs = [pltpu.VMEM((t, rows, chan), BF)] * 3
    ggain_cols = lax.dynamic_slice_in_dim(ggain, offset, chan, 1)
    block_out, grad_in, allvec = pl.pallas_call(
        functools.partial(closing, n, t, width),
        out_shape=[shape((rows, chan), BF), plane, shape((t, 8, chan), F32)],
        in_specs=[HB] * 4 + [VM] * 6,
        out_specs=[VM] * 3,
        scratch_shapes=[
            pltpu.VMEM((rows, chan), BF),
            pltpu.VMEM((rows, chan), BF),
            *shard_bufs,
            *shard_bufs,
            pltpu.VMEM((rows, chan), F32),
            pltpu.VMEM((rows, chan), F32),
            pltpu.VMEM((t, 8, rows), F32),
            pltpu.VMEM((n, 8, chan), F32),
            DMA((2,)), DMA((2, t)),
            *shard_sems,
            *shard_sems,
            DMA((t,)), DMA((t,)), DMA((n,)), DMA((n,)), DMA((t,)), DMA((t,)),
        ],
        compiler_params=params(4),
        name="closing",
    )(
        glu_part, gni_part, hidden_in, mixed, gres, inv_in, valid,
        cols(gain_in)[None], vecs, ggain_cols,
    )

    def vector(r):
        return allvec[:, r, :].reshape(width)

    squares = jnp.stack([jnp.sum(allvec[:, r, :]) for r in (4, 5, 6)])
    rms_stats = jnp.sqrt(squares / (total.astype(F32) * width))

    def piece(sums, j, size):
        return sums[:, j : j + size].astype(F32)

    return (
        block_out,
        grad_in,
        vector(0),
        piece(sums1, 0, chan),
        piece(sums1, chan, chan),
        vector(1),
        piece(sums1, 2 * chan, chan),
        vector(2),
        piece(sums1, 3 * chan, chan).T,
        vector(3),
        piece(sums2, 0, ff),
        piece(sums2, ffp, ff),
        piece(sums2, 2 * ffp, ff).T,
        rms_stats,
    )


def solution(mesh):
    weight, turned = P("seq", "tp"), P("tp", "seq")
    in_specs = (
        P("seq", None), P(), weight, weight, P(), weight, P(), turned, P(), weight, weight, turned,
        P(), P(), P("seq", None),
    )
    out_specs = (
        weight, weight, P(), weight, weight, P(), weight, P(), turned, P(), weight, weight, turned, P(),
    )
    body = functools.partial(on_device, mesh.shape["seq"], mesh.shape["tp"])
    return jax.shard_map(
        body, mesh=mesh, in_specs=in_specs, out_specs=out_specs, check_vma=False
    )
```

time: 1810 us -> 702 us (0.39)
  waiting for transfers between devices: 1030 us -> 81.2 us
  Pallas kernels: 0 us -> 568 us
  local copies, waits for them, and re-layouts: 365 us -> 11.8 us
  matrix products: 147 us -> 0 us
  other arithmetic: 133 us -> 24.3 us
  blocking collectives: 97.9 us -> 0 us
    pallas_call x0 -> x5, Pallas kernels: none -> 568 us  [the longest x1 167 us: on_device(): pl.pallas_call(functools.partial(mixer_forward, n, t, width), out_shape=[...]
    reduce_scatter x9 -> x2, waiting for transfers between devices: 485 us -> 38.8 us  [the longest x1 38.8 us: on_device(): sums2 = lax.psum_scatter(dw2, 'seq', scatter_dimension=0, tiled=True)]
    psum x2 -> x0, waiting for transfers between devices: 389 us -> none  [the longest x1 218 us: on_device(): mixed = lax.psum(mixed_part, 'tp')]
    slice x202 -> x0, local copies, waits for them, and re-layouts: 290 us -> none  [the longest x59 119 us: on_device(): lax.associative_scan(chain, (forget_next[::-1], grad_states_out[::-1]), a...]
    dot_general x21 -> x0, matrix products: 147 us -> none  [the longest x7 53.6 us: outer_dot(): lax.dot_general(left, right, (((0,), (0,)), ((), ())), preferred_element_...]
    all_gather x7 -> x2, waiting for transfers between devices: 149 us -> 41.9 us  [the longest x1 41.8 us: on_device(): lax.all_gather(jnp.concatenate([w_input, w_forget, w_outgate, w_output.T]...]
    psum x4 -> x0, blocking collectives: 71.5 us -> none  [the longest x1 39 us: on_device(): square_total, vector_total = lax.psum((square_sums, vectors), ('seq', 'tp'))]
    add x103 -> x0, other arithmetic: 67.7 us -> none  [the longest x58 46.9 us: chain(): return (earlier[0] * later[0], later[0] * earlier[1] + later[1])]
  transfers between devices with their start and end apart: 18 -> 4, of which waited for: 14 -> 2; matrix products, arithmetic and copies ran while one was open for 33% -> 4% of each run, Pallas kernels for 0% -> 44%
where the time goes in v1:
time: 702 us
  Pallas kernels  568 us (81%)
  waiting for transfers between devices  81.2 us (12%)
  other arithmetic  24.3 us (3%)
  between operations  15.8 us (2%)
  local copies, waits for them, and re-layouts  11.8 us (2%)
    pallas_call x1, Pallas kernels, on_device(): pl.pallas_call(functools.partial(mixer_forward, n, t, width), out_shape=[...  167 us
    pallas_call x1, Pallas kernels, on_device(): pl.pallas_call(functools.partial(mid_backward, t, width), out_shape=[wide...  151 us
    pallas_call x1, Pallas kernels, on_device(): pl.pallas_call(functools.partial(closing, n, t, width), out_shape=[shape(...  144 us
    pallas_call x1, Pallas kernels, on_device(): pl.pallas_call(feed_forward, out_shape=[wide16, wide16, shape((width, 3 *...  56.8 us
    pallas_call x1, Pallas kernels, on_device(): pl.pallas_call(functools.partial(mixer_backward, n, t, width), out_shape=...  49.2 us
    all_gather x1, waiting for transfers between devices, on_device(): lax.all_gather(jnp.concatenate([w_input, w_forget, w_outgate, w_output.T]...  41.8 us
    reduce_scatter x1, waiting for transfers between devices, on_device(): sums2 = lax.psum_scatter(dw2, 'seq', scatter_dimension=0, tiled=True)  38.8 us
  transfers between devices with their start and end apart: 4, of which 2 were waited for; matrix products, arithmetic and copies ran while one was open for 4% of the time, Pallas kernels for 44%

profile of v1, /device:TPU:0, one launch (start us, length us, event | category | flops | bytes accessed | tf_op | source)
XLA Modules:
  0.0 701.8 jit_solution(4191893676475313052)
XLA Ops:
  7.2 0.0 copy-start.2
  7.2 0.0 all-gather.3.cloned.1.call-start
  7.2 1.1 copy.38
  8.4 2.2 pad_maximum_fusion.1
  10.6 0.0 all-gather.3.cloned.1.call-update
  10.6 0.0 all-gather.5.cloned.1.call-start
  10.7 0.0 copy-done.2
  10.7 1.1 copy.40
  11.8 3.2 pad_maximum_fusion
  15.0 0.0 all-gather.5.cloned.1.call-update
  15.1 0.0 reduce-scatter.3.cloned.1.call-start
  15.8 0.1 pad.8.clone
  15.9 0.1 pad.9.clone
  15.9 0.0 copy-done.3
  15.9 0.0 copy-done.4
  15.9 0.6 broadcast_in_dim.39
  16.5 0.8 dynamic_slice.12
  17.3 0.0 copy-done.5
  17.3 0.6 fusion.10
  19.2 0.8 dynamic-slice_convert_fusion.1
  19.9 1.5 fusion.8.starts
  21.4 0.8 fusion.6.valid
  22.2 0.0 copy-done
  22.2 0.7 fusion
  22.9 0.7 maximum_maximum_fusion.crow
  23.6 2.4 fusion.2.normed
  26.0 41.8 %all-gather.3.cloned.1.call-done.w1 = bf16[2048,2048]{1,0:T(8,128)(2,1)} async-done(((bf16[256,2048]{1,0:T(8,128)(2,1)}), bf16[2048,2048]{1,0:T(8,128)(2,1)}) %all-gather.3.cloned.1.call-update) | async-done | bytes 8388624 | tf_op jit(solution)/shard_map/all_gather | solution.py:724
  67.9 167.5 %mixer_forward.1 = (f32[768,512]{1,0:T(8,128)}, f32[768,512]{1,0:T(8,128)}, f32[768,512]{1,0:T(8,128)}, f32[4,776,128]{2,1,0:T(8,128)}, f32[4,776,128]{2,1,0:T(8...) custom-call(bf16[768,2048]{1,0:T(8,128)(2,1)} %fusion.2.normed, ...), custom_call_target="tpu_custom_call" | custom-call | tf_op jit(solution)/shard_map/mixer_forward/pallas_call | solution.py:762
  235.3 0.0 all-gather.5.cloned.1.call-done.w2_h
  235.4 56.8 %feed_forward.1 = (bf16[768,2048]{1,0:T(8,128)(2,1)}, bf16[768,2048]{1,0:T(8,128)(2,1)}, bf16[2048,4224]{1,0:T(8,128)(2,1)}) custom-call(bf16[768,2048]{1,0:T(8,128)(2,1)} %get-tuple-element.36.nmid_h, bf16[768,2048]{1,0:T(8,128)(2,1)} %cot.1, bf16[2048,4224]{1,0:T(8,128)(2,1)} %all-gather.5.cloned.1.call-done.w2_h), custom_call_target="tpu_custom_call" | custom-call | flops 39862665216 | bytes 50000000 | tf_op jit(solution)/shard_map/feed_forward/pallas_call | solution.py:785
  292.2 151.0 %mid_backward.1 = (bf16[768,2048]{1,0:T(8,128)(2,1)}, f32[768,512]{1,0:T(8,128)}, f32[8,2048]{1,0:T(8,128)}) custom-call(bf16[768,2048]{1,0:T(8,128)(2,1)} %get-tuple-element.38.gnm_part, bf16[768,2048]{1,0:T(8,128)(2,1)} %x_h.1, bf16[768,2048]{1,0:T(8,128)(2,1)} %get-tuple-element.39.mixed.mixed_h, f32[768,1]{1,0:T(8,128)} %get-tuple-element.40.invmid, ...), custom_call_target="tpu_custom_call" | custom-call | tf_op jit(solution)/shard_map/mid_backward/pallas_call | solution.py:813
  443.2 49.2 %mixer_backward.1 = (bf16[768,2048]{1,0:T(8,128)(2,1)}, bf16[2048,2048]{1,0:T(8,128)(2,1)}, f32[8,512]{1,0:T(8,128)}) custom-call(bf16[768,2048]{1,0:T(8,128)(2,1)} %get-tuple-element.41.gmix, bf16[768,2048]{1,0:T(8,128)(2,1)} %fusion.2.normed, bf16[2048,2048]{1,0:T(8,128)(2,1)} %all-gather.3.cloned.1.call-done.w1, ...), custom_call_target="tpu_custom_call" | custom-call | tf_op jit(solution)/shard_map/mixer_backward/pallas_call | solution.py:828
  492.3 0.0 reduce-scatter.3.cloned.1.call-update
  492.3 0.0 reduce-scatter.5.cloned.1.call-start
  492.4 0.5 reduce-scatter.5.cloned.1.call-update
  492.9 0.9 rsqrt.7.invin
  493.8 0.7 dynamic-slice_convert_fusion
  494.5 1.3 constant_dynamic-slice_fusion.ggain
  495.8 144.1 %closing.1 = (bf16[768,512]{1,0:T(8,128)(2,1)}, f32[768,512]{1,0:T(8,128)}, f32[4,8,512]{2,1,0:T(8,128)}) custom-call(bf16[768,2048]{1,0:T(8,128)(2,1)} %get-tuple-element.37.glu_h, bf16[768,2048]{1,0:T(8,128)(2,1)} %get-tuple-element.49.gni_h, bf16[768,2048]{1,0:T(8,128)(2,1)} %x_h.1, bf16[768,2048]{1,0:T(8,128)(2,1)} %get-tuple-element.39.mixed.mixed_h, ...), custom_call_target="tpu_custom_call" | custom-call | tf_op jit(solution)/shard_map/closing/pallas_call | solution.py:853
  639.9 2.4 slice_reduce_fusion.2
  642.3 2.5 fusion.9
  644.9 2.4 convert_bitcast_fusion.1
  647.3 1.0 copy.42
  648.3 38.8 %reduce-scatter.5.cloned.1.call-done = bf16[256,4224]{1,0:T(8,128)(2,1)} async-done(((bf16[2048,4224]{1,0:T(8,128)(2,1)}), bf16[256,4224]{1,0:T(8,128)(2,1)}) %reduce-scatter.5.cloned.1.call-update) | async-done | bytes 2162704 | tf_op jit(solution)/shard_map/reduce_scatter | solution.py:811
  687.1 3.4 convert_bitcast_fusion
  690.5 1.5 copy.43
  692.0 2.1 copy.47
  694.1 1.1 copy.48
  (10 shorter events, 0.0 us)
Async XLA Ops:
  7.2 3.5 copy-start.2
  7.2 60.7 %all-gather.3.cloned.1.call-start = ((), (), s32[]{:S(2)}) async-start(), calls=%async_computation.2 | async-start | bytes 9437184 | tf_op jit(solution)/shard_map/all_gather | solution.py:724
  10.6 224.7 %all-gather.5.cloned.1.call-start = ((), (), s32[]{:S(2)}) async-start(), calls=%async_computation.3 | async-start | bytes 19464192 | tf_op jit(solution)/shard_map/all_gather | solution.py:727
  11.8 10.4 %copy-start = (bf16[768,2048]{1,0:T(8,128)(2,1)S(1)}, bf16[768,2048]{1,0:T(8,128)(2,1)}, u32[]{:S(2)}) copy-start(bf16[768,2048]{1,0:T(8,128)(2,1)} %x_h.1) | copy-start | bytes 9437188
  15.0 0.9 copy-start.3
  15.0 0.9 copy-start.4
  15.0 2.3 copy-start.5
  15.1 629.8 %reduce-scatter.3.cloned.1.call-start = ((), (), s32[]{:S(2)}) async-start(), calls=%async_computation.4 | async-start | bytes 9437184 | tf_op jit(solution)/shard_map/reduce_scatter | solution.py:847
  492.3 194.7 %reduce-scatter.5.cloned.1.call-start = ((), (), s32[]{:S(2)}) async-start(), calls=%async_computation.5 | async-start | bytes 19464192 | tf_op jit(solution)/shard_map/reduce_scatter | solution.py:811
  690.5 3.6 copy-start.1
Sparse Core Ops, SparseCore 0:
  10.7 57.0 all-gather.2
  69.7 93.4 all-gather.4
  492.5 70.6 reduce-scatter.2
  567.1 119.9 reduce-scatter.4

commit v2 on v1

--- a/solution.py
+++ b/solution.py
@@ -10,13 +10,16 @@
 LAYERS = 24
 EPS = 1e-06
 MESH = pl.DeviceIdType.MESH
+DMA = pltpu.SemaphoreType.DMA
 BF = jnp.bfloat16
 F32 = jnp.float32
 VM = pl.BlockSpec(memory_space=pltpu.VMEM)
 HB = pl.BlockSpec(memory_space=pl.ANY)
 LANE = 128
 SEG = 8
-CHUNKS = 8
+CHUNKS = 16
+SHARD_CHUNKS = 4
+ROUND_TRIP = 3
 VMEM_LIMIT = 60 * 1024 * 1024
 
 
@@ -43,6 +46,19 @@
 def put(ref, at, values):
     for g in range(ref.shape[0]):
         ref[g, at, :] = values[:, g * LANE : (g + 1) * LANE]
+
+
+def put_shards(ref, at, values):
+    k = ref.shape[2]
+    for q in range(ref.shape[0]):
+        ref[q, at, :] = values[:, q * k : (q + 1) * k]
+
+
+def put_blocks(ref, h, values):
+    for core in range(2):
+        for half in range(2):
+            first = (core * 2 + half) * h
+            ref[core, half] = values[first : first + h].astype(ref.dtype)
 
 
 def row_tile(rows):
@@ -135,7 +151,7 @@
     return lax.fori_loop(0, n, hop, jnp.zeros_like(prod))
 
 
-def line_all_reduce(t, seq, tp, rows, chunks, partial, send, buf, sems, finish):
+def line_all_reduce(t, seq, tp, rows, chunks, partial, send, buf, sems, finish, beside=None):
     s_in, s_out, r_buf = sems
     step = rows // chunks
     half = t // 2
@@ -196,18 +212,22 @@
 
         finish(k)
 
+    lag = 1 + ROUND_TRIP * (half - 1 - depth)
+
     def both(k, c):
         @pl.when(k < chunks)
         def _():
             first(k)
 
-        @pl.when(k > 0)
-        def _():
-            second(k - 1)
-
-        return c
-
-    lax.fori_loop(0, chunks + 1, both, 0)
+        @pl.when((k >= lag) & (k - lag < chunks))
+        def _():
+            second(k - lag)
+
+        if beside is not None:
+            beside(k)
+        return c
+
+    lax.fori_loop(0, chunks + 1 + ROUND_TRIP * (half - 1), both, 0)
 
     def drain(k, c):
         inward(k, middle).wait_send()
@@ -221,8 +241,10 @@
     lax.fori_loop(0, chunks, drain, 0)
 
 
-def line_reduce_scatter(t, seq, tp, rows, chunks, own, right, left, sems, finish):
+def line_reduce_scatter(t, seq, tp, own, inbox, sems, finish):
     s_r, r_r, s_l, r_l = sems
+    rows = own.shape[1]
+    chunks = SHARD_CHUNKS
     step = rows // chunks
 
     def part_of(k):
@@ -231,7 +253,7 @@
     def rightward(q, k):
         return pltpu.make_async_remote_copy(
             src_ref=own.at[q, part_of(k)],
-            dst_ref=right.at[q, part_of(k)],
+            dst_ref=inbox.at[q + 1, part_of(k)],
             send_sem=s_r.at[q, k],
             recv_sem=r_r.at[q, k],
             device_id=(seq, lax.rem(tp + 1, t)),
@@ -241,19 +263,19 @@
     def leftward(q, k):
         return pltpu.make_async_remote_copy(
             src_ref=own.at[q, part_of(k)],
-            dst_ref=left.at[q, part_of(k)],
+            dst_ref=inbox.at[q, part_of(k)],
             send_sem=s_l.at[q, k],
             recv_sem=r_l.at[q, k],
             device_id=(seq, lax.rem(tp + t - 1, t)),
             device_id_type=MESH,
         )
 
-    def add(q, k, other):
+    def add(q, k, slot):
         own[q, part_of(k), :] = (
-            own[q, part_of(k), :].astype(F32) + other[q, part_of(k), :].astype(F32)
+            own[q, part_of(k), :].astype(F32) + inbox[slot, part_of(k), :].astype(F32)
         ).astype(BF)
 
-    def step_of(i, c):
+    def step_of(i):
         k = i // (t - 1)
         j = lax.rem(i, t - 1)
 
@@ -264,7 +286,7 @@
             @pl.when(tp > 0)
             def _():
                 rightward(q, k).wait_recv()
-                add(q, k, right)
+                add(q, k, q + 1)
 
             rightward(q, k).start()
 
@@ -273,24 +295,20 @@
             @pl.when(tp < t - 1)
             def _():
                 leftward(j, k).wait_recv()
-                add(j, k, left)
+                add(j, k, j)
 
             leftward(j, k).start()
 
-        return c
-
-    lax.fori_loop(0, chunks * (t - 1), step_of, 0)
-
-    def last(k, c):
+    def last(k):
         @pl.when(tp == 0)
         def _():
             leftward(tp, k).wait_recv()
-            finish(k, own[tp, part_of(k), :].astype(F32) + left[tp, part_of(k), :].astype(F32))
+            finish(k, own[tp, part_of(k), :].astype(F32) + inbox[tp, part_of(k), :].astype(F32))
 
         @pl.when(tp == t - 1)
         def _():
             rightward(tp, k).wait_recv()
-            finish(k, own[tp, part_of(k), :].astype(F32) + right[tp, part_of(k), :].astype(F32))
+            finish(k, own[tp, part_of(k), :].astype(F32) + inbox[tp + 1, part_of(k), :].astype(F32))
 
         @pl.when((tp > 0) & (tp < t - 1))
         def _():
@@ -299,36 +317,186 @@
             finish(
                 k,
                 own[tp, part_of(k), :].astype(F32)
-                + left[tp, part_of(k), :].astype(F32)
-                + right[tp, part_of(k), :].astype(F32),
+                + inbox[tp, part_of(k), :].astype(F32)
+                + inbox[tp + 1, part_of(k), :].astype(F32),
             )
 
-        return c
-
-    lax.fori_loop(0, chunks, last, 0)
-
-    def drain(i, c):
-        k = i // (t - 1)
-        j = lax.rem(i, t - 1)
-
-        @pl.when(t - 1 - j > tp)
-        def _():
-            rightward(t - 1 - j, k).wait_send()
-
-        @pl.when(j < tp)
-        def _():
-            leftward(j, k).wait_send()
-
-        return c
-
-    lax.fori_loop(0, chunks * (t - 1), drain, 0)
+    def drain():
+        def sent(i, c):
+            k = i // (t - 1)
+            j = lax.rem(i, t - 1)
+
+            @pl.when(t - 1 - j > tp)
+            def _():
+                rightward(t - 1 - j, k).wait_send()
+
+            @pl.when(j < tp)
+            def _():
+                leftward(j, k).wait_send()
+
+            return c
+
+        lax.fori_loop(0, chunks * (t - 1), sent, 0)
+
+    return chunks * (t - 1), step_of, last, drain
+
+
+def chip_grid(n):
+    chips = n // 2
+    b = max(k for k in range(1, chips + 1) if chips % k == 0 and k * k <= chips)
+    return chips // b, b
+
+
+def grid_buffers(n, width, pieces, cols):
+    ga, gb = chip_grid(n)
+    h = width // n // 2
+    pa, pb = max(ga - 1, 1), max(gb - 1, 1)
+    return [
+        pltpu.VMEM((pieces, 2, ga, gb, h, cols), BF),
+        pltpu.VMEM((pieces, 2, ga, gb, h, cols), BF),
+        pltpu.VMEM((pieces, pb, ga, h, cols), BF),
+        pltpu.VMEM((pieces, pa, gb, h, cols), BF),
+        pltpu.VMEM((pieces, pa, h, cols), BF),
+        pltpu.VMEM((pieces, pb, h, cols), BF),
+        DMA((pieces,)), DMA((pieces,)), DMA((pieces,)),
+        DMA((2, pieces, pb)), DMA((2, pieces, pa)), DMA((2, pieces, pa)), DMA((2, pieces, pb)),
+    ]
+
+
+def grid_reduce(n, seq, tp, terms, pieces, cols, bufs, out):
+    acc, first, far_b, far_a, near_a, near_b, s_own, s_f, r_f, m_fb, m_fa, m_na, m_nb = bufs
+    ga, gb = chip_grid(n)
+    core = lax.rem(seq, 2)
+    a, b = seq // 2 // gb, lax.rem(seq // 2, gb)
+
+    def device(a_, b_, core_):
+        return ((a_ * gb + b_) * 2 + core_, tp)
+
+    def columns(j):
+        return pl.ds(j * cols, cols)
+
+    def load(j):
+        return pltpu.make_async_copy(
+            terms.at[core, :, :, :, :, columns(j)], acc.at[j], s_own.at[j]
+        )
+
+    def swap(j):
+        return pltpu.make_async_remote_copy(
+            src_ref=terms.at[1 - core, :, :, :, :, columns(j)],
+            dst_ref=first.at[j],
+            send_sem=s_f.at[j],
+            recv_sem=r_f.at[j],
+            device_id=device(a, b, 1 - core),
+            device_id_type=MESH,
+        )
+
+    def remote(src, dst, sems, j, o, target):
+        return pltpu.make_async_remote_copy(
+            src_ref=src,
+            dst_ref=dst,
+            send_sem=sems.at[0, j, o],
+            recv_sem=sems.at[1, j, o],
+            device_id=target,
+            device_id_type=MESH,
+        )
+
+    def far(j):
+        copies = []
+        for o in range(1, gb):
+            to = lax.rem(b + o, gb)
+            copies.append(
+                remote(acc.at[j, 0, :, to], far_b.at[j, o - 1], m_fb, j, o - 1, device(a, to, core))
+            )
+        for o in range(1, ga):
+            to = lax.rem(a + o, ga)
+            copies.append(
+                remote(acc.at[j, 1, to], far_a.at[j, o - 1], m_fa, j, o - 1, device(to, b, core))
+            )
+        return copies
+
+    def near(j):
+        copies = []
+        for o in range(1, ga):
+            to = lax.rem(a + o, ga)
+            copies.append(
+                remote(acc.at[j, 0, to, b], near_a.at[j, o - 1], m_na, j, o - 1, device(to, b, core))
+            )
+        for o in range(1, gb):
+            to = lax.rem(b + o, gb)
+            copies.append(
+                remote(acc.at[j, 1, a, to], near_b.at[j, o - 1], m_nb, j, o - 1, device(a, to, core))
+            )
+        return copies
+
+    def start(j):
+        load(j).start()
+        swap(j).start()
+
+    def stage1(j):
+        load(j).wait()
+        swap(j).wait_recv()
+
+        def chip(i, c):
+            x, y = i // gb, lax.rem(i, gb)
+            for half in range(2):
+                acc[j, half, x, y] = (
+                    acc[j, half, x, y].astype(F32) + first[j, half, x, y].astype(F32)
+                ).astype(BF)
+            return c
+
+        lax.fori_loop(0, ga * gb, chip, 0)
+        for copy in far(j):
+            copy.start()
+
+    def stage2(j):
+        for copy in far(j):
+            copy.wait_recv()
+
+        def along_a(x, c):
+            total = acc[j, 0, x, b].astype(F32)
+            for o in range(1, gb):
+                total = total + far_b[j, o - 1, x].astype(F32)
+            acc[j, 0, x, b] = total.astype(BF)
+            return c
+
+        def along_b(y, c):
+            total = acc[j, 1, a, y].astype(F32)
+            for o in range(1, ga):
+                total = total + far_a[j, o - 1, y].astype(F32)
+            acc[j, 1, a, y] = total.astype(BF)
+            return c
+
+        lax.fori_loop(0, ga, along_a, 0)
+        lax.fori_loop(0, gb, along_b, 0)
+        for copy in near(j):
+            copy.start()
+
+    def stage3(j):
+        for copy in near(j):
+            copy.wait_recv()
+        total = acc[j, 0, a, b].astype(F32)
+        for o in range(1, ga):
+            total = total + near_a[j, o - 1].astype(F32)
+        out(j, 0, total)
+        total = acc[j, 1, a, b].astype(F32)
+        for o in range(1, gb):
+            total = total + near_b[j, o - 1].astype(F32)
+        out(j, 1, total)
+
+    def drain():
+        for j in range(pieces):
+            swap(j).wait_send()
+            for copy in far(j) + near(j):
+                copy.wait_send()
+
+    return start, stage1, stage2, stage3, drain
 
 
 def mixer_forward(
     n, t, width,
     normed, x, w1, crow, gmid, valid, starts,
     ipre, fpre, opre, feff, states, gated, nmid, mixed, invst, invmid,
-    prod, ssq, cslots, zslots, send, buf,
+    prod, ssq, part, cslots, zslots, send, buf,
     cs, cr, zs, zr, s_in, s_out, r_buf,
 ):
     seq, tp = lax.axis_index("seq"), lax.axis_index("tp")
@@ -399,9 +567,15 @@
 
     step = rows // CHUNKS
 
+    group = part.shape[0] // step
+
     def partial(k):
-        at = pl.ds(pl.multiple_of(k * step, step), step)
-        return nt(gated[at, :], w1[:, 3 * chan :])
+        @pl.when(lax.rem(k, group) == 0)
+        def _():
+            big = pl.ds(pl.multiple_of(k * step, step), step * group)
+            part[...] = nt(gated[big, :], w1[:, 3 * chan :])
+
+        return part[pl.ds(pl.multiple_of(lax.rem(k, group) * step, step), step), :]
 
     def finish(k):
         at = pl.ds(pl.multiple_of(k * step, step), step)
@@ -438,8 +612,9 @@
 
     def out_copy(i, which):
         at = pl.ds(pl.multiple_of(i * tile, tile), tile)
-        src, dst = ((gnm, gnm_h), (glu, glu_h))[which]
-        return pltpu.make_async_copy(src.at[at], dst.at[at], s_o.at[which, i])
+        if which == 0:
+            return pltpu.make_async_copy(gnm.at[at], gnm_h.at[at], s_o.at[0, i])
+        return pltpu.make_async_copy(glu.at[:, at], glu_h.at[:, at], s_o.at[1, i])
 
     def block(i, c):
         at = pl.ds(pl.multiple_of(i * tile, tile), tile)
@@ -453,21 +628,22 @@
         gu[at, :] = (gh * act).astype(BF)
         gnm[at, :] = (nt(gg[at, :], wg[...]) + nt(gu[at, :], wu[...])).astype(BF)
         out_copy(i, 0).start()
-        glu[at, :] = nt(hid[at, :], wd[...]).astype(BF)
+        put_shards(glu, at, nt(hid[at, :], wd[...]).astype(BF))
         out_copy(i, 1).start()
         return c
 
     lax.fori_loop(0, rows // tile, block, 0)
 
-    span = min(512, width)
-    pieces = width // span
+    ga, gb, h = dw2_h.shape[2:5]
+    span = 4 * h
+    pieces = ga * gb
 
     def d_copy(i, slot):
         j = i // pieces
         r = lax.rem(i, pieces)
         return pltpu.make_async_copy(
             stage.at[slot],
-            dw2_h.at[pl.ds(pl.multiple_of(r * span, span), span), pl.ds(pl.multiple_of(j * ff, LANE), ff)],
+            dw2_h.at[:, :, r // gb, lax.rem(r, gb), :, pl.ds(pl.multiple_of(j * ff, LANE), ff)],
             s_d.at[slot],
         )
 
@@ -482,7 +658,7 @@
                 d_copy(i - 2, slot).wait()
 
             at = pl.ds(pl.multiple_of(r * span, span), span)
-            stage[slot] = tn(left[:, at], right[...]).astype(BF)
+            put_blocks(stage.at[slot], h, tn(left[:, at], right[...]))
             d_copy(i, slot).start()
             return c
 
@@ -499,21 +675,31 @@
 
 
 def mid_backward(
-    t, width,
-    gnm_part, x, mixed, invmid, cot, gmid,
-    gmix, gres, ggain,
-    send, buf, wide, s_in, s_out, r_buf,
+    n, t, width,
+    gnm_h, dw2_h, x, mixed, invmid, cot, gmid,
+    gmix, gres, ggain, sums,
+    send, buf, wide, s_g, s_in, s_out, r_buf, *bufs,
 ):
     seq, tp = lax.axis_index("seq"), lax.axis_index("tp")
-    greet_line(t, seq, tp)
+    load = pltpu.make_async_copy(gnm_h, send, s_g)
+    load.start()
+    greet_all(n, t, seq, tp)
     rows = x.shape[0]
     chan = gres.shape[1]
     step = rows // CHUNKS
+    pieces, shard, cols = sums.shape
     ggain[...] = jnp.zeros_like(ggain)
+
+    def out(j, half, values):
+        sums[j, half * (shard // 2) : (half + 1) * (shard // 2), :] = values
+
+    start, stage1, stage2, stage3, drain = grid_reduce(n, seq, tp, dw2_h, pieces, cols, bufs, out)
+    start(0)
+    load.wait()
 
     def partial(k):
         at = pl.ds(pl.multiple_of(k * step, step), step)
-        return gnm_part[at, :].astype(F32)
+        return send[at, :].astype(F32)
 
     def finish(k):
         at = pl.ds(pl.multiple_of(k * step, step), step)
@@ -528,28 +714,82 @@
         gmix[at, :] = out.astype(BF)
         gres[at, :] = wide[:, pl.ds(pl.multiple_of(tp * chan, LANE), chan)]
 
-    line_all_reduce(t, seq, tp, rows, CHUNKS, partial, send, buf, (s_in, s_out, r_buf), finish)
+    turns = [
+        (1, lambda: (stage1(0), start(1))),
+        (4, lambda: (stage1(1), start(2))),
+        (5, lambda: stage2(0)),
+        (8, lambda: stage1(2)),
+        (9, lambda: stage3(0)),
+        (10, lambda: stage2(1)),
+        (13, lambda: stage3(1)),
+        (14, lambda: stage2(2)),
+        (16, lambda: stage3(2)),
+    ]
+
+    def beside(k):
+        for turn, work in turns:
+
+            @pl.when(k == turn)
+            def _(work=work):
+                work()
+
+    line_all_reduce(
+        t, seq, tp, rows, CHUNKS, partial, send, buf, (s_in, s_out, r_buf), finish, beside
+    )
+    drain()
 
 
 def mixer_backward(
     n, t, width,
+    glu_h, x_h, mixed_h,
     gmix, normed, w1, gated, states, feff, ipre, fpre, opre, invst, valid, starts, crow,
-    gni, dw1, vecs,
-    grad, weighted, prod, inner, out3, cslots, zslots,
-    cs, cr, zs, zr,
+    gni_h, dw1_h, vecs, out,
+    weighted, prod, inner, out3, cslots, zslots, xc, mc, own, inbox, gni, stage,
+    cs, cr, zs, zr, s_x, sr, rr, sl, rl, s_o, s_d,
 ):
     seq, tp = lax.axis_index("seq"), lax.axis_index("tp")
-    greet_all(n, t, seq, tp)
     rows = gmix.shape[0]
     chan = ipre.shape[1]
+    mine = pl.ds(pl.multiple_of(tp * chan, LANE), chan)
+    fetches = [
+        pltpu.make_async_copy(glu_h, own, s_x.at[0]),
+        pltpu.make_async_copy(x_h.at[:, mine], xc, s_x.at[1]),
+        pltpu.make_async_copy(mixed_h.at[:, mine], mc, s_x.at[2]),
+    ]
+    for copy in fetches:
+        copy.start()
+    greet_all(n, t, seq, tp)
     tile = row_tile(rows)
     sgain, bound = crow[1:2, :], crow[2:3, :]
     vecs[...] = jnp.zeros_like(vecs)
+    for copy in fetches:
+        copy.wait()
+    step = rows // SHARD_CHUNKS
+
+    def finish(k, values):
+        at = pl.ds(pl.multiple_of(k * step, step), step)
+        ok = valid[at, :]
+        m = mc[at, :].astype(F32)
+        full = xc[at, :].astype(F32) + m + values
+        out[at, :] = full.astype(BF)
+        vecs[4:5, :] += jnp.sum(ok * m * m, axis=0, keepdims=True)
+        vecs[5:6, :] += jnp.sum(ok * values * values, axis=0, keepdims=True)
+        vecs[6:7, :] += jnp.sum(ok * full * full, axis=0, keepdims=True)
+
+    steps, step_of, last, drain = line_reduce_scatter(t, seq, tp, own, inbox, (sr, rr, sl, rl), finish)
+
+    def pump(slot):
+        def one(i, c):
+            step_of(i)
+            return c
+
+        lax.fori_loop(slot * steps // 12, (slot + 1) * steps // 12, one, 0)
 
     def gates(i, c):
         at = pl.ds(pl.multiple_of(i * tile, tile), tile)
         shifted = pl.ds(pl.multiple_of(i * tile + 8, 8), tile)
-        g = nn(gmix[at, :], grad[...])
+        pump(i)
+        g = nn(gmix[at, :], w1[:, 3 * chan :])
         hat = get(states, shifted) * invst[at, :]
         o = opre[at, :]
         sig = jax.nn.sigmoid(o)
@@ -561,10 +801,10 @@
         inner[at, :] = w * hat
         return c
 
-    grad[...] = w1[:, 3 * chan :]
     lax.fori_loop(0, rows // tile, gates, 0)
     dot = sum_over_tp(row_sums(inner[...]), t, seq, tp, zslots, zs, zr) / width
     inner[:, 0:1] = dot
+    pump(rows // tile)
 
     def leaving(i, c):
         at = pl.ds(pl.multiple_of(i * tile, tile), tile)
@@ -595,6 +835,7 @@
     for s in range(SEG - 2, -1, -1):
         block_h = h[s : s + 1] + p[s : s + 1] * block_h
         block_p = p[s : s + 1] * block_p
+    pump(rows // tile + 1)
     first = get(feff, slice(0, 1))
     arriving = carry_over_seq(first * block_p, first * block_h, n, seq, tp, cslots, cs, cr, True)
     bias_sum = jnp.zeros((1, chan), F32)
@@ -614,53 +855,90 @@
         gf = (gate_grad * (1.0 - bound) * sf * (1.0 - sf)).astype(BF)
         out3[at, chan : 2 * chan] = gf
         bias_sum = bias_sum + jnp.sum(gf.astype(F32), axis=0, keepdims=True)
+        if s % 2 == 0:
+            pump(rows // tile + 5 - s // 2)
     vecs[1:2, :] = bias_sum
+
+    def gni_copy(i):
+        at = pl.ds(pl.multiple_of(i * tile, tile), tile)
+        return pltpu.make_async_copy(gni.at[:, at], gni_h.at[:, at], s_o.at[i])
 
     def spread_in(i, c):
         at = pl.ds(pl.multiple_of(i * tile, tile), tile)
-        gni[at, :] = nt(out3[at, :], w1[:, : 3 * chan]).astype(BF)
+        put_shards(gni, at, nt(out3[at, :], w1[:, : 3 * chan]).astype(BF))
+        gni_copy(i).start()
+        pump(12 - rows // tile + i)
         return c
 
     lax.fori_loop(0, rows // tile, spread_in, 0)
 
-    span = 512
+    ga, gb, h = dw1_h.shape[2:5]
+    span = 4 * h
+
+    def d_copy(r, slot):
+        return pltpu.make_async_copy(
+            stage.at[slot], dw1_h.at[:, :, r // gb, lax.rem(r, gb)], s_d.at[slot]
+        )
 
     def slab(r, c):
+        slot = lax.rem(r, 2)
+
+        @pl.when(r >= 2)
+        def _():
+            d_copy(r - 2, slot).wait()
+
         at = pl.ds(pl.multiple_of(r * span, span), span)
-        dw1[at, : 3 * chan] = tn(normed[:, at], out3[...]).astype(BF)
-        dw1[at, 3 * chan :] = tn(gmix[:, at], gated[...]).astype(BF)
-        return c
-
-    lax.fori_loop(0, width // span, slab, 0)
+        put_blocks(stage.at[slot, :, :, :, pl.ds(0, 3 * chan)], h, tn(normed[:, at], out3[...]))
+        put_blocks(stage.at[slot, :, :, :, pl.ds(3 * chan, chan)], h, tn(gmix[:, at], gated[...]))
+        d_copy(r, slot).start()
+        return c
+
+    lax.fori_loop(0, ga * gb, slab, 0)
+
+    def ending(k, c):
+        last(k)
+        return c
+
+    lax.fori_loop(0, SHARD_CHUNKS, ending, 0)
+    for r in range(max(ga * gb - 2, 0), ga * gb):
+        d_copy(r, r % 2).wait()
+
+    def stored(i, c):
+        gni_copy(i).wait()
+        return c
+
+    lax.fori_loop(0, rows // tile, stored, 0)
+    drain()
 
 
 def closing(
     n, t, width,
-    glu_h, gni_h, x_h, mixed_h, gres, invin, valid, gain_in, vecs, ggain,
-    out, gin, allvec,
-    xc, mc, own_a, right_a, left_a, own_b, right_b, left_b, scaled, inner, zslots, vslots,
-    s_x, s_own, sr_a, rr_a, sl_a, rl_a, sr_b, rr_b, sl_b, rl_b, zs, zr, vs, vr, ts, tr,
+    gni_h, dw1_h, xc, gres, invin, gain_in, vecs, ggain,
+    gin, allvec, sums,
+    own, inbox, scaled, inner, zslots, vslots,
+    s_own, sr, rr, sl, rl, zs, zr, vs, vr, ts, tr, *bufs,
 ):
     seq, tp = lax.axis_index("seq"), lax.axis_index("tp")
     rows, chan = gres.shape
-    mine = pl.ds(pl.multiple_of(tp * chan, LANE), chan)
-    locals_ = [
-        pltpu.make_async_copy(x_h.at[:, mine], xc, s_x.at[0]),
-        pltpu.make_async_copy(mixed_h.at[:, mine], mc, s_x.at[1]),
-    ]
-    for q in range(t):
-        locals_.append(pltpu.make_async_copy(glu_h.at[:, pl.ds(q * chan, chan)], own_a.at[q], s_own.at[0, q]))
-        locals_.append(pltpu.make_async_copy(gni_h.at[:, pl.ds(q * chan, chan)], own_b.at[q], s_own.at[1, q]))
-    for copy in locals_:
-        copy.start()
+    fetch = pltpu.make_async_copy(gni_h, own, s_own)
+    fetch.start()
     greet_all(n, t, seq, tp)
-    for copy in locals_:
-        copy.wait()
-    half = CHUNKS // 2
-    step = rows // half
+    pieces, shard, cols = sums.shape
+
+    def out(j, half, values):
+        sums[j, half * (shard // 2) : (half + 1) * (shard // 2), :] = values
+
+    start, stage1, stage2, stage3, drain_grid = grid_reduce(
+        n, seq, tp, dw1_h, pieces, cols, bufs, out
+    )
+    start(0)
+    start(1)
+    fetch.wait()
+    step = rows // SHARD_CHUNKS
     vslots[seq] = vecs[...]
-
-    def finish_b(k, values):
+    vslots[seq, 3:4, :] = ggain[0:1, :]
+
+    def finish(k, values):
         at = pl.ds(pl.multiple_of(k * step, step), step)
         hat = xc[at, :].astype(F32) * invin[at, :]
         s = values * gain_in[...]
@@ -668,19 +946,37 @@
         inner[at, :] = s * hat
         vslots[seq, 0:1, :] += jnp.sum(values * hat, axis=0, keepdims=True)
 
-    def finish_a(k, values):
-        at = pl.ds(pl.multiple_of(k * step, step), step)
-        ok = valid[at, :]
-        m = mc[at, :].astype(F32)
-        full = xc[at, :].astype(F32) + m + values
-        out[at, :] = full.astype(BF)
-        vslots[seq, 4:5, :] += jnp.sum(ok * m * m, axis=0, keepdims=True)
-        vslots[seq, 5:6, :] += jnp.sum(ok * values * values, axis=0, keepdims=True)
-        vslots[seq, 6:7, :] += jnp.sum(ok * full * full, axis=0, keepdims=True)
-
-    line_reduce_scatter(t, seq, tp, rows, half, own_b, right_b, left_b, (sr_b, rr_b, sl_b, rl_b), finish_b)
-    line_reduce_scatter(t, seq, tp, rows, half, own_a, right_a, left_a, (sr_a, rr_a, sl_a, rl_a), finish_a)
-    vslots[seq, 3:4, :] = ggain[0:1, :]
+    steps, step_of, last, drain = line_reduce_scatter(t, seq, tp, own, inbox, (sr, rr, sl, rl), finish)
+    turns = [
+        (2, lambda: stage1(0)),
+        (4, lambda: stage1(1)),
+        (6, lambda: stage2(0)),
+        (9, lambda: stage3(0)),
+        (10, lambda: stage2(1)),
+        (11, lambda: stage3(1)),
+    ]
+
+    def turn_of(slot, c):
+        def one(i, c):
+            step_of(i)
+            return c
+
+        lax.fori_loop(slot * steps // 12, (slot + 1) * steps // 12, one, 0)
+        for turn, work in turns:
+
+            @pl.when(slot == turn)
+            def _(work=work):
+                work()
+
+        return c
+
+    lax.fori_loop(0, 12, turn_of, 0)
+
+    def ending(k, c):
+        last(k)
+        return c
+
+    lax.fori_loop(0, SHARD_CHUNKS, ending, 0)
     dot = sum_over_tp(row_sums(inner[...]), t, seq, tp, zslots, zs, zr) / width
     gin[...] = gres[...] + invin[...] * (scaled[...] - xc[...].astype(F32) * invin[...] * dot)
     spread(n, seq, vslots, vs, vr, lambda k: (k, tp))
@@ -689,9 +985,8 @@
         total = total + vslots[k]
     allvec[tp] = total
     spread(t, tp, allvec, ts, tr, lambda k: (seq, k))
-
-
-DMA = pltpu.SemaphoreType.DMA
+    drain()
+    drain_grid()
 
 
 def params(collective=None, limit=VMEM_LIMIT):
@@ -753,6 +1048,9 @@
     gmid = gain_mid.astype(F32)[None]
     plane = shape((rows, chan), F32)
     column = shape((rows, 1), F32)
+    ga, gb = chip_grid(n)
+    h = width // n // 2
+    shards16 = shape((t, rows, chan), BF)
 
     def groups(more=0):
         return shape((chan // LANE, rows + more, LANE), F32)
@@ -771,6 +1069,7 @@
         scratch_shapes=[
             pltpu.VMEM(groups().shape, F32),
             pltpu.VMEM((rows, chan), F32),
+            pltpu.VMEM((rows // CHUNKS * 4, width), F32),
             pltpu.VMEM((n, 8, chan), F32),
             pltpu.VMEM((t, 8, rows), F32),
             pltpu.VMEM((rows, width), BF),
@@ -784,7 +1083,7 @@
 
     gnm_part, glu_part, dw2 = pl.pallas_call(
         feed_forward,
-        out_shape=[wide16, wide16, shape((width, 3 * ffp), BF)],
+        out_shape=[wide16, shards16, shape((2, 2, ga, gb, h, 3 * ffp), BF)],
         in_specs=[HB] * 3,
         out_specs=[HB] * 3,
         scratch_shapes=[
@@ -797,8 +1096,8 @@
             pltpu.VMEM((rows, ffp), BF),
             pltpu.VMEM((rows, ffp), BF),
             pltpu.VMEM((rows, width), BF),
-            pltpu.VMEM((rows, width), BF),
-            pltpu.VMEM((2, min(512, width), ffp), BF),
+            pltpu.VMEM((t, rows, chan), BF),
+            pltpu.VMEM((2, 2, 2, h, ffp), BF),
             DMA((3,)), DMA((2,)), DMA((2, rows // row_tile(rows))), DMA((2,)),
         ],
         compiler_params=params(),
@@ -808,72 +1107,78 @@
         name="feed_forward",
     )(nmid, cotangent, w2)
 
-    sums2 = lax.psum_scatter(dw2, "seq", scatter_dimension=0, tiled=True)
-
-    gmix, gres, ggain = pl.pallas_call(
-        functools.partial(mid_backward, t, width),
-        out_shape=[wide16, plane, shape((8, width), F32)],
-        in_specs=[VM] * 6,
-        out_specs=[VM] * 3,
+    gmix, gres, ggain, sums2 = pl.pallas_call(
+        functools.partial(mid_backward, n, t, width),
+        out_shape=[wide16, plane, shape((8, width), F32), shape((3, 2 * h, ffp), F32)],
+        in_specs=[HB] * 2 + [VM] * 5,
+        out_specs=[VM] * 4,
         scratch_shapes=[
             pltpu.VMEM((rows, width), BF),
             pltpu.VMEM((2, rows, width), BF),
             pltpu.VMEM((rows // CHUNKS, width), F32),
+            DMA,
             *line_sems(CHUNKS),
+            *grid_buffers(n, width, 3, ffp),
         ],
         compiler_params=params(2),
         name="mid_backward",
-    )(gnm_part, hidden_in, mixed, invmid, cotangent, gmid)
-
-    gni_part, dw1, vecs = pl.pallas_call(
+    )(gnm_part, dw2, hidden_in, mixed, invmid, cotangent, gmid)
+
+    shard_sems = [DMA((t, SHARD_CHUNKS))] * 4
+    shard_bufs = [pltpu.VMEM((t, rows, chan), BF), pltpu.VMEM((t + 1, rows, chan), BF)]
+    gni_part, dw1, vecs, block_out = pl.pallas_call(
         functools.partial(mixer_backward, n, t, width),
-        out_shape=[wide16, shape((width, 4 * chan), BF), shape((8, chan), F32)],
-        in_specs=[VM] * 13,
-        out_specs=[VM] * 3,
+        out_shape=[
+            shards16, shape((2, 2, ga, gb, h, 4 * chan), BF), shape((8, chan), F32),
+            shape((rows, chan), BF),
+        ],
+        in_specs=[HB] * 3 + [VM] * 13,
+        out_specs=[HB] * 2 + [VM] * 2,
         scratch_shapes=[
-            pltpu.VMEM((width, chan), BF),
             pltpu.VMEM(groups().shape, F32),
             pltpu.VMEM(groups().shape, F32),
             pltpu.VMEM((rows, chan), F32),
             pltpu.VMEM((rows, 3 * chan), BF),
             pltpu.VMEM((n, 8, chan), F32),
             pltpu.VMEM((t, 8, rows), F32),
-            DMA((n,)), DMA((n,)), DMA((t,)), DMA((t,)),
+            pltpu.VMEM((rows, chan), BF),
+            pltpu.VMEM((rows, chan), BF),
+            *shard_bufs,
+            pltpu.VMEM((t, rows, chan), BF),
+            pltpu.VMEM((2, 2, 2, h, 4 * chan), BF),
+            DMA((n,)), DMA((n,)), DMA((t,)), DMA((t,)), DMA((3,)),
+            *shard_sems,
+            DMA((rows // row_tile(rows),)), DMA((2,)),
         ],
         compiler_params=params(3),
         name="mixer_backward",
-    )(gmix, normed_in, w1, gated, states, feff, ipre, fpre, opre, invst, valid, starts, crow)
-
-    sums1 = lax.psum_scatter(dw1, "seq", scatter_dimension=0, tiled=True)
-
-    half = CHUNKS // 2
-    shard_sems = [DMA((t, half))] * 4
-    shard_bufs = [pltpu.VMEM((t, rows, chan), BF)] * 3
+    )(
+        glu_part, hidden_in, mixed,
+        gmix, normed_in, w1, gated, states, feff, ipre, fpre, opre, invst, valid, starts, crow,
+    )
+
     ggain_cols = lax.dynamic_slice_in_dim(ggain, offset, chan, 1)
-    block_out, grad_in, allvec = pl.pallas_call(
+    x_cols = lax.dynamic_slice_in_dim(hidden_in, offset, chan, 1)
+    grad_in, allvec, sums1 = pl.pallas_call(
         functools.partial(closing, n, t, width),
-        out_shape=[shape((rows, chan), BF), plane, shape((t, 8, chan), F32)],
-        in_specs=[HB] * 4 + [VM] * 6,
+        out_shape=[plane, shape((t, 8, chan), F32), shape((2, 2 * h, 2 * chan), F32)],
+        in_specs=[HB] * 2 + [VM] * 6,
         out_specs=[VM] * 3,
         scratch_shapes=[
-            pltpu.VMEM((rows, chan), BF),
-            pltpu.VMEM((rows, chan), BF),
-            *shard_bufs,
             *shard_bufs,
             pltpu.VMEM((rows, chan), F32),
             pltpu.VMEM((rows, chan), F32),
             pltpu.VMEM((t, 8, rows), F32),
             pltpu.VMEM((n, 8, chan), F32),
-            DMA((2,)), DMA((2, t)),
-            *shard_sems,
+            DMA,
             *shard_sems,
             DMA((t,)), DMA((t,)), DMA((n,)), DMA((n,)), DMA((t,)), DMA((t,)),
+            *grid_buffers(n, width, 2, 2 * chan),
         ],
         compiler_params=params(4),
         name="closing",
     )(
-        glu_part, gni_part, hidden_in, mixed, gres, inv_in, valid,
-        cols(gain_in)[None], vecs, ggain_cols,
+        gni_part, dw1, x_cols, gres, inv_in, cols(gain_in)[None], vecs, ggain_cols,
     )
 
     def vector(r):
@@ -881,24 +1186,21 @@
 
     squares = jnp.stack([jnp.sum(allvec[:, r, :]) for r in (4, 5, 6)])
     rms_stats = jnp.sqrt(squares / (total.astype(F32) * width))
-
-    def piece(sums, j, size):
-        return sums[:, j : j + size].astype(F32)
 
     return (
         block_out,
         grad_in,
         vector(0),
-        piece(sums1, 0, chan),
-        piece(sums1, chan, chan),
+        sums1[0, :, :chan],
+        sums1[0, :, chan:],
         vector(1),
-        piece(sums1, 2 * chan, chan),
+        sums1[1, :, :chan],
         vector(2),
-        piece(sums1, 3 * chan, chan).T,
+        sums1[1, :, chan:].T,
         vector(3),
-        piece(sums2, 0, ff),
-        piece(sums2, ffp, ff),
-        piece(sums2, 2 * ffp, ff).T,
+        sums2[0, :, :ff],
+        sums2[1, :, :ff],
+        sums2[2, :, :ff].T,
         rms_stats,
     )
 

time: 702 us -> 549 us (0.78)
  Pallas kernels: 568 us -> 455 us
  waiting for transfers between devices: 81.2 us -> 40.1 us
  local copies, waits for them, and re-layouts: 11.8 us -> 19.5 us
    pallas_call x3, Pallas kernels: 352 us -> 242 us  [the longest x1 101 us: on_device(): pl.pallas_call(functools.partial(mid_backward, n, t, width), out_shape=[w...]
    pallas_call x1, Pallas kernels: 167 us -> 118 us  [on_device(): pl.pallas_call(functools.partial(mixer_forward, n, t, width), out_shape=[...]
    pallas_call x1, Pallas kernels: 49.2 us -> 94.9 us  [on_device(): pl.pallas_call(functools.partial(mixer_backward, n, t, width), out_shape=...]
    reduce_scatter x2 -> x0, waiting for transfers between devices: 38.8 us -> none  [the longest x1 38.8 us: on_device(): sums2 = lax.psum_scatter(dw2, 'seq', scatter_dimension=0, tiled=True)]
  transfers between devices with their start and end apart: 4 -> 2, of which waited for: 2 -> 1; matrix products, arithmetic and copies ran while one was open for 4% -> 3% of each run, Pallas kernels for 44% -> 22%
where the time goes in v2:
time: 549 us
  Pallas kernels  455 us (83%)
  waiting for transfers between devices  40.1 us (7%)
  local copies, waits for them, and re-layouts  19.5 us (4%)
  other arithmetic  17.9 us (3%)
  between operations  16.1 us (3%)
    pallas_call x1, Pallas kernels, on_device(): pl.pallas_call(functools.partial(mixer_forward, n, t, width), out_shape=[...  118 us
    pallas_call x1, Pallas kernels, on_device(): pl.pallas_call(functools.partial(mid_backward, n, t, width), out_shape=[w...  101 us
    pallas_call x1, Pallas kernels, on_device(): pl.pallas_call(functools.partial(mixer_backward, n, t, width), out_shape=...  94.9 us
    pallas_call x1, Pallas kernels, on_device(): pl.pallas_call(functools.partial(closing, n, t, width), out_shape=[plane,...  84 us
    pallas_call x1, Pallas kernels, on_device(): pl.pallas_call(feed_forward, out_shape=[wide16, shards16, shape((2, 2, ga...  56.8 us
    all_gather x1, waiting for transfers between devices, on_device(): lax.all_gather(jnp.concatenate([w_input, w_forget, w_outgate, w_output.T]...  40.1 us
  transfers between devices with their start and end apart: 2, of which 1 were waited for; matrix products, arithmetic and copies ran while one was open for 3% of the time, Pallas kernels for 22%

profile of v2, /device:TPU:0, one launch (start us, length us, event | category | flops | bytes accessed | tf_op | source)
XLA Modules:
  0.0 548.6 jit_solution(17543777679560852213)
XLA Ops:
  7.2 0.0 copy-start.2
  7.2 0.0 all-gather.3.cloned.1.call-start
  7.2 1.1 copy.38
  8.4 2.2 pad_maximum_fusion.1
  10.6 0.0 all-gather.3.cloned.1.call-update
  10.6 0.0 all-gather.5.cloned.1.call-start
  10.7 0.0 copy-done.2
  10.7 1.1 copy.40
  11.8 0.0 copy-start.3
  11.8 0.0 copy-start.4
  11.8 0.0 copy-start
  11.8 3.2 pad_maximum_fusion
  15.0 0.0 copy-start.5
  15.0 0.0 all-gather.5.cloned.1.call-update
  15.7 0.1 pad.8.clone
  15.7 0.1 pad.9.clone
  15.8 0.0 copy-done.3
  15.8 0.0 copy-done.4
  15.8 0.6 broadcast_in_dim.39
  16.4 0.0 copy-done
  16.4 0.7 fusion
  17.1 0.9 rsqrt.7.invin
  18.1 0.0 copy-done.5
  18.1 0.6 fusion.10
  19.9 0.8 dynamic_slice.15
  20.7 0.7 dynamic-slice_convert_fusion
  21.4 0.8 dynamic-slice_convert_fusion.1
  22.1 1.0 constant_dynamic-slice_fusion.1.xc
  23.1 1.6 fusion.6
  24.7 0.7 maximum_maximum_fusion.crow
  25.4 2.4 fusion.2.normed
  27.8 40.1 %all-gather.3.cloned.1.call-done.w1 = bf16[2048,2048]{1,0:T(8,128)(2,1)} async-done(((bf16[256,2048]{1,0:T(8,128)(2,1)}), bf16[2048,2048]{1,0:T(8,128)(2,1)}) %all-gather.3.cloned.1.call-update) | async-done | bytes 8388624 | tf_op jit(solution)/shard_map/all_gather | solution.py:1019
  67.9 118.0 %mixer_forward.1 = (f32[768,512]{1,0:T(8,128)}, f32[768,512]{1,0:T(8,128)}, f32[768,512]{1,0:T(8,128)}, f32[4,776,128]{2,1,0:T(8,128)}, f32[4,776,128]{2,1,0:T(8...) custom-call(bf16[768,2048]{1,0:T(8,128)(2,1)} %fusion.2.normed, ...), custom_call_target="tpu_custom_call" | custom-call | tf_op jit(solution)/shard_map/mixer_forward/pallas_call | solution.py:1060
  185.9 0.0 all-gather.5.cloned.1.call-done.w2_h
  186.0 56.8 %feed_forward.1 = (bf16[768,2048]{1,0:T(8,128)(2,1)}, bf16[4,768,512]{2,1,0:T(8,128)(2,1)}, bf16[2,2,2,2,128,4224]{5,4,3,2,1,0:T(8,128)(2,1)}) custom-call(bf16[768,2048]{1,0:T(8,128)(2,1)} %get-tuple-element.38.nmid_h, bf16[768,2048]{1,0:T(8,128)(2,1)} %cot.1, bf16[2048,4224]{1,0:T(8,128)(2,1)} %all-gather.5.cloned.1.call-done.w2_h), custom_call_target="tpu_custom_call" | custom-call | flops 39862665216 | bytes 50000000 | tf_op jit(solution)/shard_map/feed_forward/pallas_call | solution.py:1084
  242.8 101.1 %mid_backward.1 = (bf16[768,2048]{1,0:T(8,128)(2,1)}, f32[768,512]{1,0:T(8,128)}, f32[8,2048]{1,0:T(8,128)}, f32[3,256,1408]{2,1,0:T(8,128)}) custom-call(bf16[768,2048]{1,0:T(8,128)(2,1)} %get-tuple-element.41.gnm_h, bf16[2,2,2,2,128,4224]{5,4,3,2,1,0:T(8,128)(2,1)} %get-tuple-element.42.dw2_h, bf16[768,2048]{1,0:T(8,128)(2,1)} %x_h.1, ...), custom_call_target="tpu_custom_call" | custom-call | tf_op jit(solution)/shard_map/mid_backward/pallas_call | solution.py:1110
  343.9 1.3 constant_dynamic-slice_fusion.ggain
  345.3 94.9 %mixer_backward.1 = (bf16[4,768,512]{2,1,0:T(8,128)(2,1)}, bf16[2,2,2,2,128,2048]{5,4,3,2,1,0:T(8,128)(2,1)}, f32[8,512]{1,0:T(8,128)}, bf16[768,512]{1,0:T(8,128)(2,1)}) custom-call(bf16[4,768,512]{2,1,0:T(8,128)(2,1)} %get-tuple-element.39.glu_h, bf16[768,2048]{1,0:T(8,128)(2,1)} %x_h.1, bf16[768,2048]{1,0:T(8,128)(2,1)} %get-tuple-element.40.mixed.mixed_h, ...), custom_call_target="tpu_custom_call" | custom-call | tf_op jit(solution)/shard_map/mixer_backward/pallas_call | solution.py:1129
  440.1 84.0 %closing.1 = (f32[768,512]{1,0:T(8,128)}, f32[4,8,512]{2,1,0:T(8,128)}, f32[2,256,1024]{2,1,0:T(8,128)}) custom-call(bf16[4,768,512]{2,1,0:T(8,128)(2,1)} %get-tuple-element.53.gni_h, bf16[2,2,2,2,128,2048]{5,4,3,2,1,0:T(8,128)(2,1)} %get-tuple-element.54.dw1_h, bf16[768,512]{1,0:T(8,128)(2,1)} %constant_dynamic-slice_fusion.1.xc, ...), custom_call_target="tpu_custom_call" | custom-call | tf_op jit(solution)/shard_map/closing/pallas_call | solution.py:1162
  524.1 2.7 slice_reduce_fusion.2
  526.8 2.7 slice_bitcast_fusion.3
  529.5 1.0 copy.42
  530.5 4.1 slice_bitcast_fusion
  534.5 1.5 copy.43
  536.1 2.4 fusion.9
  538.5 2.1 copy.47
  540.6 0.0 copy-done.1
  540.6 1.1 copy.48
  (4 shorter events, 0.0 us)
Async XLA Ops:
  7.2 3.5 copy-start.2
  7.2 60.7 %all-gather.3.cloned.1.call-start = ((), (), s32[]{:S(2)}) async-start(), calls=%async_computation | async-start | bytes 9437184 | tf_op jit(solution)/shard_map/all_gather | solution.py:1019
  10.6 175.3 %all-gather.5.cloned.1.call-start = ((), (), s32[]{:S(2)}) async-start(), calls=%async_computation.1 | async-start | bytes 19464192 | tf_op jit(solution)/shard_map/all_gather | solution.py:1022
  11.8 4.0 copy-start.3
  11.8 4.0 copy-start.4
  11.8 4.6 copy-start
  15.0 3.1 copy-start.5
  534.5 6.0 %copy-start.1 = (f32[768,512]{1,0:T(8,128)S(1)}, f32[768,512]{1,0:T(8,128)}, u32[]{:S(2)}) copy-start(f32[768,512]{1,0:T(8,128)} %get-tuple-element.137) | copy-start | bytes 4718596
Sparse Core Ops, SparseCore 0:
  10.7 57.0 all-gather.2
  69.7 93.4 all-gather.4

commit v3 on v2

--- a/solution.py
+++ b/solution.py
@@ -19,6 +19,7 @@
 SEG = 8
 CHUNKS = 16
 SHARD_CHUNKS = 4
+HOP_LAG = 2
 ROUND_TRIP = 3
 VMEM_LIMIT = 60 * 1024 * 1024
 
@@ -103,11 +104,11 @@
             device_id_type=MESH,
         )
 
-    def go(o, c):
+    def one(o, c):
         copy(o, me).start()
         return c
 
-    def done(o, c):
+    def arrived(o, c):
         copy(o, lax.rem(me + o, size)).wait_recv()
         return c
 
@@ -115,9 +116,14 @@
         copy(o, me).wait_send()
         return c
 
-    lax.fori_loop(1, size, go, 0)
-    lax.fori_loop(1, size, done, 0)
-    lax.fori_loop(1, size, sent, 0)
+    def go():
+        lax.fori_loop(1, size, one, 0)
+
+    def done():
+        lax.fori_loop(1, size, arrived, 0)
+        lax.fori_loop(1, size, sent, 0)
+
+    return go, done
 
 
 def row_sums(values):
@@ -128,18 +134,26 @@
     return nt(ones, high) + nt(ones, low)
 
 
-def sum_over_tp(part, t, seq, tp, slots, send, recv):
+def sum_over_tp(part, t, seq, tp, slots, send, recv, between=None):
     slots[tp] = part
-    spread(t, tp, slots, send, recv, lambda k: (seq, k))
+    go, done = spread(t, tp, slots, send, recv, lambda k: (seq, k))
+    go()
+    if between is not None:
+        between()
+    done()
     total = slots[0]
     for k in range(1, t):
         total = total + slots[k]
     return jnp.transpose(total)[:, :1]
 
 
-def carry_over_seq(prod, state, n, seq, tp, slots, send, recv, backward):
+def carry_over_seq(prod, state, n, seq, tp, slots, send, recv, backward, between=None):
     slots[seq] = jnp.concatenate([prod, state] + [jnp.zeros_like(prod)] * 6, axis=0)
-    spread(n, seq, slots, send, recv, lambda k: (k, tp))
+    go, done = spread(n, seq, slots, send, recv, lambda k: (k, tp))
+    go()
+    if between is not None:
+        between()
+    done()
 
     def hop(i, total):
         j = n - 1 - i if backward else i
@@ -246,6 +260,7 @@
     rows = own.shape[1]
     chunks = SHARD_CHUNKS
     step = rows // chunks
+    count = chunks * (t - 1)
 
     def part_of(k):
         return pl.ds(pl.multiple_of(k * step, step), step)
@@ -275,14 +290,12 @@
             own[q, part_of(k), :].astype(F32) + inbox[slot, part_of(k), :].astype(F32)
         ).astype(BF)
 
-    def step_of(i):
-        k = i // (t - 1)
-        j = lax.rem(i, t - 1)
-
-        @pl.when(t - 1 - j > tp)
-        def _():
-            q = t - 1 - j
-
+    def right_turn(i):
+        k, j = i // (t - 1), lax.rem(i, t - 1)
+        q = t - 1 - j
+
+        @pl.when((i >= 0) & (i < count) & (q > tp))
+        def _():
             @pl.when(tp > 0)
             def _():
                 rightward(q, k).wait_recv()
@@ -290,14 +303,21 @@
 
             rightward(q, k).start()
 
-        @pl.when(j < tp)
+    def left_turn(i):
+        k, q = i // (t - 1), lax.rem(i, t - 1)
+
+        @pl.when((i >= 0) & (i < count) & (q < tp))
         def _():
             @pl.when(tp < t - 1)
             def _():
-                leftward(j, k).wait_recv()
-                add(j, k, j)
-
-            leftward(j, k).start()
+                leftward(q, k).wait_recv()
+                add(q, k, q)
+
+            leftward(q, k).start()
+
+    def turn(i):
+        right_turn(i - HOP_LAG * tp)
+        left_turn(i - HOP_LAG * (t - 1 - tp))
 
     def last(k):
         @pl.when(tp == 0)
@@ -336,9 +356,9 @@
 
             return c
 
-        lax.fori_loop(0, chunks * (t - 1), sent, 0)
-
-    return chunks * (t - 1), step_of, last, drain
+        lax.fori_loop(0, count, sent, 0)
+
+    return count + HOP_LAG * (t - 2), turn, last, drain
 
 
 def chip_grid(n):
@@ -492,35 +512,207 @@
     return start, stage1, stage2, stage3, drain
 
 
+def gather_sems(n, pieces):
+    ga, gb = chip_grid(n)
+    pa, pb = max(ga - 1, 1), max(gb - 1, 1)
+    return [
+        DMA((pieces,)), DMA((2, pieces, ga * gb)),
+        DMA((2, pieces, pb)), DMA((2, pieces, pa)), DMA((2, pieces, gb, pa)), DMA((2, pieces, ga, pb)),
+    ]
+
+
+def grid_gather(n, seq, tp, j, src, dst, sems):
+    s_local, m_core, m_fb, m_fa, m_na, m_nb = sems
+    ga, gb = chip_grid(n)
+    shard = src.shape[0]
+    h = shard // 2
+    core = lax.rem(seq, 2)
+    a, b = seq // 2 // gb, lax.rem(seq // 2, gb)
+
+    def device(a_, b_, core_):
+        return ((a_ * gb + b_) * 2 + core_, tp)
+
+    def block(x, y, core_, half, count):
+        return pl.ds(pl.multiple_of(((x * gb + y) * 2 + core_) * shard + half * h, h), count)
+
+    def remote(from_, rows, sem, index, target):
+        return pltpu.make_async_remote_copy(
+            src_ref=from_,
+            dst_ref=dst.at[rows],
+            send_sem=sem.at[(0, j) + index],
+            recv_sem=sem.at[(1, j) + index],
+            device_id=target,
+            device_id_type=MESH,
+        )
+
+    def own(half):
+        return src.at[pl.ds(half * h, h)]
+
+    def far(incoming):
+        copies = []
+        for o in range(1, gb):
+            to, of = lax.rem(b + o, gb), lax.rem(b + gb - o, gb)
+            rows = block(a, of if incoming else b, core, 0, h)
+            copies.append(remote(own(0), rows, m_fb, (o - 1,), device(a, to, core)))
+        for o in range(1, ga):
+            to, of = lax.rem(a + o, ga), lax.rem(a + ga - o, ga)
+            rows = block(of if incoming else a, b, core, 1, h)
+            copies.append(remote(own(1), rows, m_fa, (o - 1,), device(to, b, core)))
+        return copies
+
+    def near(incoming, first, least):
+        copies = []
+        for i in range(0 if first else 1, gb if least else 1):
+            y = lax.rem(b + gb - i, gb)
+            for o in range(1, ga):
+                to, of = lax.rem(a + o, ga), lax.rem(a + ga - o, ga)
+                rows = block(of if incoming else a, y, core, 0, h)
+                from_ = own(0) if i == 0 or incoming else dst.at[rows]
+                copies.append(remote(from_, rows, m_na, (i, o - 1), device(to, b, core)))
+        for i in range(0 if first else 1, ga if least else 1):
+            x = lax.rem(a + ga - i, ga)
+            for o in range(1, gb):
+                to, of = lax.rem(b + o, gb), lax.rem(b + gb - o, gb)
+                rows = block(x, of if incoming else b, core, 1, h)
+                from_ = own(1) if i == 0 or incoming else dst.at[rows]
+                copies.append(remote(from_, rows, m_nb, (i, o - 1), device(a, to, core)))
+        return copies
+
+    def across(incoming, first, others):
+        copies = []
+        for i in range(ga):
+            for k in range(gb):
+                mine = i == 0 and k == 0
+                if (mine and not first) or (not mine and not others):
+                    continue
+                x, y = lax.rem(a + i, ga), lax.rem(b + k, gb)
+                rows = block(x, y, 1 - core if incoming else core, 0, shard)
+                from_ = src if mine or incoming else dst.at[rows]
+                copies.append(remote(from_, rows, m_core, (i * gb + k,), device(a, b, 1 - core)))
+        return copies
+
+    def local():
+        return pltpu.make_async_copy(src, dst.at[block(a, b, core, 0, shard)], s_local.at[j])
+
+    def start():
+        for copy in far(False) + near(False, True, False) + across(False, True, False):
+            copy.start()
+        local().start()
+
+    def relay():
+        for copy in far(True):
+            copy.wait_recv()
+        for copy in near(False, False, True):
+            copy.start()
+
+    def share():
+        for copy in near(True, True, True):
+            copy.wait_recv()
+        for copy in across(False, False, True):
+            copy.start()
+
+    def arrive():
+        for copy in across(True, True, True):
+            copy.wait_recv()
+        local().wait()
+
+    def drain():
+        for copy in far(False) + near(False, True, True) + across(False, True, True):
+            copy.wait_send()
+
+    return start, relay, share, arrive, drain
+
+
+def masks(lens, first, count):
+    at = first + lax.broadcasted_iota(jnp.int32, (count, 1), 0)
+    valid = (at < lens[0] + lens[1]).astype(F32)
+    starts = ((at == 0) | (at == lens[0])).astype(F32)
+    return valid, starts
+
+
 def mixer_forward(
     n, t, width,
-    normed, x, w1, crow, gmid, valid, starts,
-    ipre, fpre, opre, feff, states, gated, nmid, mixed, invst, invmid,
-    prod, ssq, part, cslots, zslots, send, buf,
-    cs, cr, zs, zr, s_in, s_out, r_buf,
+    lens, x_h, wi_h, wf_h, wo_h, wx_h, wg_h, wu_h, wd_h, consts,
+    ipre_h, fpre_h, opre_h, feff_h, states_h, gated_h, normed_h, nmid_h, mixed_h, w1_h, w2_h,
+    invst, invmid, invin,
+    x, normed, ipre, fpre, opre, feff, states, gated, nmid, w1, prod, ssq, part, cslots, zslots, send, buf,
+    s_x, s_st, s_w, s_n, s_m, cs, cr, zs, zr, s_in, s_out, r_buf, *sems,
 ):
     seq, tp = lax.axis_index("seq"), lax.axis_index("tp")
+    load = pltpu.make_async_copy(x_h, x, s_x)
+    load.start()
+    sems1, sems2 = sems[:6], sems[6:]
+    one = [
+        grid_gather(n, seq, tp, j, src, w1.at[j], sems1)
+        for j, src in enumerate((wi_h, wf_h, wo_h, wx_h))
+    ]
+    two = [
+        grid_gather(n, seq, tp, j, src, w2_h.at[j], sems2)
+        for j, src in enumerate((wg_h, wu_h, wd_h))
+    ]
+    START, RELAY, SHARE, ARRIVE, DRAIN = range(5)
     greet_all(n, t, seq, tp)
+    one[0][START]()
     rows, depth = normed.shape
     chan = ipre.shape[1]
     tile = row_tile(rows)
-    bias, sgain, bound = crow[0:1, :], crow[1:2, :], crow[2:3, :]
-
-    def project(i, c):
+    mine = pl.ds(pl.multiple_of(tp * chan, LANE), chan)
+    bias, sgain, bound = consts[0:1, mine], consts[1:2, mine], consts[2:3, mine]
+
+    def stores():
+        pairs = (
+            (ipre, ipre_h), (fpre, fpre_h), (opre, opre_h), (feff, feff_h), (states, states_h),
+            (gated, gated_h), (normed, normed_h),
+        )
+        return [pltpu.make_async_copy(v, o, s_st.at[i]) for i, (v, o) in enumerate(pairs)]
+
+    def keep(j):
+        return pltpu.make_async_copy(w1.at[j], w1_h.at[j], s_w.at[j])
+
+    load.wait()
+
+    def norm(i, c):
         at = pl.ds(pl.multiple_of(i * tile, tile), tile)
-        pre = nn(normed[at, :], w1[:, : 3 * chan])
-        a = pre[:, :chan]
-        f = pre[:, chan : 2 * chan] + bias
-        ipre[at, :] = a
+        v = x[at, :].astype(F32)
+        inv = lax.rsqrt(jnp.mean(v * v, axis=-1, keepdims=True) + EPS)
+        invin[at, :] = inv
+        normed[at, :] = (v * inv * consts[4:5, :]).astype(BF)
+        return c
+
+    lax.fori_loop(0, rows // tile, norm, 0)
+    one[0][RELAY]()
+    one[1][START]()
+    one[0][SHARE]()
+    one[1][RELAY]()
+    one[2][START]()
+    one[0][ARRIVE]()
+    keep(0).start()
+
+    def first(i, c):
+        at = pl.ds(pl.multiple_of(i * tile, tile), tile)
+        ipre[at, :] = nn(normed[at, :], w1[0])
+        return c
+
+    lax.fori_loop(0, rows // tile, first, 0)
+    one[1][SHARE]()
+    one[2][RELAY]()
+    one[3][START]()
+    one[1][ARRIVE]()
+    keep(1).start()
+
+    def second(i, c):
+        at = pl.ds(pl.multiple_of(i * tile, tile), tile)
+        f = nn(normed[at, :], w1[1]) + bias
         fpre[at, :] = f
-        opre[at, :] = pre[:, 2 * chan :]
+        valid, starts = masks(lens, seq * rows + i * tile, tile)
         gate = bound + (1.0 - bound) * jax.nn.sigmoid(f)
-        put(feff, at, gate * (1.0 - starts[at, :]))
+        put(feff, at, gate * (1.0 - starts))
         shifted = pl.ds(pl.multiple_of(i * tile + 8, 8), tile)
-        put(states, shifted, a * jax.nn.sigmoid(a) * (1.0 - gate) * valid[at, :])
-        return c
-
-    lax.fori_loop(0, rows // tile, project, 0)
+        v = ipre[at, :]
+        put(states, shifted, v * jax.nn.sigmoid(v) * (1.0 - gate) * valid)
+        return c
+
+    lax.fori_loop(0, rows // tile, second, 0)
     put(feff, slice(rows, rows + 8), jnp.ones((8, chan), F32))
 
     length = rows // SEG
@@ -542,7 +734,13 @@
     for s in range(1, SEG):
         block_h = h[s : s + 1] + p[s : s + 1] * block_h
         block_p = p[s : s + 1] * block_p
-    arriving = carry_over_seq(block_p, block_h, n, seq, tp, cslots, cs, cr, False)
+
+    def travel():
+        one[2][SHARE]()
+        one[3][RELAY]()
+        two[0][START]()
+
+    arriving = carry_over_seq(block_p, block_h, n, seq, tp, cslots, cs, cr, False, travel)
     put(states, slice(0, 8), jnp.broadcast_to(arriving, (8, chan)))
     for s in range(SEG):
         at = slice(s * length, (s + 1) * length)
@@ -551,7 +749,20 @@
         put(states, shifted, whole)
         ssq[at, :] = whole * whole
         arriving = h[s : s + 1] + p[s : s + 1] * arriving
-    total = sum_over_tp(row_sums(ssq[...]), t, seq, tp, zslots, zs, zr)
+
+    def outgate():
+        one[3][SHARE]()
+        one[2][ARRIVE]()
+        keep(2).start()
+
+        def third(i, c):
+            at = pl.ds(pl.multiple_of(i * tile, tile), tile)
+            opre[at, :] = nn(normed[at, :], w1[2])
+            return c
+
+        lax.fori_loop(0, rows // tile, third, 0)
+
+    total = sum_over_tp(row_sums(ssq[...]), t, seq, tp, zslots, zs, zr, outgate)
     invst[...] = lax.rsqrt(total / width + EPS)
 
     def gating(i, c):
@@ -564,29 +775,73 @@
         return c
 
     lax.fori_loop(0, rows // tile, gating, 0)
+    one[3][ARRIVE]()
+    keep(3).start()
+    for copy in stores():
+        copy.start()
 
     step = rows // CHUNKS
-
     group = part.shape[0] // step
 
     def partial(k):
         @pl.when(lax.rem(k, group) == 0)
         def _():
             big = pl.ds(pl.multiple_of(k * step, step), step * group)
-            part[...] = nt(gated[big, :], w1[:, 3 * chan :])
+            part[...] = nt(gated[big, :], w1[3])
 
         return part[pl.ds(pl.multiple_of(lax.rem(k, group) * step, step), step), :]
+
+    def store_n(k):
+        at = pl.ds(pl.multiple_of(k * step, step), step)
+        return pltpu.make_async_copy(nmid.at[at], nmid_h.at[at], s_n.at[k])
+
+    def store_m(k):
+        at = pl.ds(pl.multiple_of(k * step, step), step)
+        return pltpu.make_async_copy(buf.at[1, at], mixed_h.at[at], s_m.at[k])
 
     def finish(k):
         at = pl.ds(pl.multiple_of(k * step, step), step)
-        total = buf[1, at, :]
-        mixed[at, :] = total
-        resid = x[at, :].astype(F32) + total.astype(F32)
+        store_m(k).start()
+        resid = x[at, :].astype(F32) + buf[1, at, :].astype(F32)
         inv = lax.rsqrt(jnp.mean(resid * resid, axis=-1, keepdims=True) + EPS)
         invmid[at, :] = inv
-        nmid[at, :] = (resid * inv * gmid[...]).astype(BF)
-
-    line_all_reduce(t, seq, tp, rows, CHUNKS, partial, send, buf, (s_in, s_out, r_buf), finish)
+        nmid[at, :] = (resid * inv * consts[3:4, :]).astype(BF)
+        store_n(k).start()
+
+    turns = [
+        (2, lambda: (two[0][RELAY](), two[1][START]())),
+        (4, lambda: two[0][SHARE]()),
+        (7, lambda: (two[1][RELAY](), two[2][START]())),
+        (9, lambda: two[1][SHARE]()),
+        (13, lambda: two[2][RELAY]()),
+        (16, lambda: two[2][SHARE]()),
+    ]
+
+    def beside(k):
+        for turn, work in turns:
+
+            @pl.when(k == turn)
+            def _(work=work):
+                work()
+
+    line_all_reduce(
+        t, seq, tp, rows, CHUNKS, partial, send, buf, (s_in, s_out, r_buf), finish, beside
+    )
+    for g in two:
+        g[ARRIVE]()
+    for g in one + two:
+        g[DRAIN]()
+    for copy in stores():
+        copy.wait()
+    for j in range(4):
+        keep(j).wait()
+
+    def stored(k, c):
+        store_n(k).wait()
+        store_m(k).wait()
+        return c
+
+    lax.fori_loop(0, CHUNKS, stored, 0)
 
 
 def feed_forward(
@@ -602,13 +857,13 @@
         pltpu.make_async_copy(cot_h, cot, s_a.at[1]),
     ]
     w_copies = [
-        pltpu.make_async_copy(w2_h.at[:, pl.ds(j * ff, ff)], w, s_w.at[j])
+        pltpu.make_async_copy(w2_h.at[j], w, s_w.at[j])
         for j, w in enumerate((wg, wu, wd))
     ]
     for copy in (act_copies[0], w_copies[0], w_copies[1], act_copies[1], w_copies[2]):
         copy.start()
-    for copy in (act_copies[0], w_copies[0], w_copies[1], act_copies[1], w_copies[2]):
-        copy.wait()
+    act_copies[0].wait()
+    w_copies[0].wait()
 
     def out_copy(i, which):
         at = pl.ds(pl.multiple_of(i * tile, tile), tile)
@@ -619,6 +874,13 @@
     def block(i, c):
         at = pl.ds(pl.multiple_of(i * tile, tile), tile)
         g = nn(nmid[at, :], wg[...])
+
+        @pl.when(i == 0)
+        def _():
+            w_copies[1].wait()
+            act_copies[1].wait()
+            w_copies[2].wait()
+
         u = nn(nmid[at, :], wu[...])
         gh = nn(cot[at, :], wd[...])
         sig = jax.nn.sigmoid(g)
@@ -676,13 +938,17 @@
 
 def mid_backward(
     n, t, width,
-    gnm_h, dw2_h, x, mixed, invmid, cot, gmid,
-    gmix, gres, ggain, sums,
-    send, buf, wide, s_g, s_in, s_out, r_buf, *bufs,
+    gnm_h, dw2_h, x_h, mixed_h, cot_h, invmid, consts,
+    gmix_h, gres_h, ggain, sums_h,
+    x, mixed, cot, gmix, gres, sums, send, buf, wide, s_g, s_x, s_o, s_s, s_in, s_out, r_buf, *bufs,
 ):
     seq, tp = lax.axis_index("seq"), lax.axis_index("tp")
     load = pltpu.make_async_copy(gnm_h, send, s_g)
     load.start()
+    fetches = [
+        pltpu.make_async_copy(src, dst, s_x.at[i])
+        for i, (src, dst) in enumerate(((x_h, x), (mixed_h, mixed), (cot_h, cot)))
+    ]
     greet_all(n, t, seq, tp)
     rows = x.shape[0]
     chan = gres.shape[1]
@@ -694,36 +960,55 @@
         sums[j, half * (shard // 2) : (half + 1) * (shard // 2), :] = values
 
     start, stage1, stage2, stage3, drain = grid_reduce(n, seq, tp, dw2_h, pieces, cols, bufs, out)
+    load.wait()
     start(0)
-    load.wait()
+    for copy in fetches:
+        copy.start()
+
+    def summed(j):
+        return pltpu.make_async_copy(sums.at[j], sums_h.at[j], s_s.at[j])
+
+    def stored(k):
+        at = pl.ds(pl.multiple_of(k * step, step), step)
+        return (
+            pltpu.make_async_copy(gmix.at[at], gmix_h.at[at], s_o.at[0, k]),
+            pltpu.make_async_copy(gres.at[at], gres_h.at[at], s_o.at[1, k]),
+        )
 
     def partial(k):
         at = pl.ds(pl.multiple_of(k * step, step), step)
         return send[at, :].astype(F32)
 
     def finish(k):
+        @pl.when(k == 0)
+        def _():
+            for copy in fetches:
+                copy.wait()
+
         at = pl.ds(pl.multiple_of(k * step, step), step)
         g = buf[1, at, :].astype(F32)
         inv = invmid[at, :]
         hat = (x[at, :].astype(F32) + mixed[at, :].astype(F32)) * inv
         ggain[0:1, :] += jnp.sum(g * hat, axis=0, keepdims=True)
-        e = g * gmid[...]
+        e = g * consts[3:4, :]
         mean = jnp.mean(e * hat, axis=-1, keepdims=True)
-        out = cot[at, :].astype(F32) + inv * (e - hat * mean)
-        wide[...] = out
-        gmix[at, :] = out.astype(BF)
+        result = cot[at, :].astype(F32) + inv * (e - hat * mean)
+        wide[...] = result
+        gmix[at, :] = result.astype(BF)
         gres[at, :] = wide[:, pl.ds(pl.multiple_of(tp * chan, LANE), chan)]
+        for copy in stored(k):
+            copy.start()
 
     turns = [
         (1, lambda: (stage1(0), start(1))),
         (4, lambda: (stage1(1), start(2))),
         (5, lambda: stage2(0)),
         (8, lambda: stage1(2)),
-        (9, lambda: stage3(0)),
+        (9, lambda: (stage3(0), summed(0).start())),
         (10, lambda: stage2(1)),
-        (13, lambda: stage3(1)),
+        (13, lambda: (stage3(1), summed(1).start())),
         (14, lambda: stage2(2)),
-        (16, lambda: stage3(2)),
+        (17, lambda: (stage3(2), summed(2).start())),
     ]
 
     def beside(k):
@@ -737,15 +1022,25 @@
         t, seq, tp, rows, CHUNKS, partial, send, buf, (s_in, s_out, r_buf), finish, beside
     )
     drain()
+    for j in range(pieces):
+        summed(j).wait()
+
+    def ended(k, c):
+        for copy in stored(k):
+            copy.wait()
+        return c
+
+    lax.fori_loop(0, CHUNKS, ended, 0)
 
 
 def mixer_backward(
     n, t, width,
-    glu_h, x_h, mixed_h,
-    gmix, normed, w1, gated, states, feff, ipre, fpre, opre, invst, valid, starts, crow,
+    lens, glu_h, x_h, mixed_h, gmix_h, normed_h, w1_h, gated_h, states_h, feff_h, ipre_h, fpre_h, opre_h,
+    invst, consts,
     gni_h, dw1_h, vecs, out,
+    gmix, normed, w1, gated, states, feff, ipre, fpre, opre,
     weighted, prod, inner, out3, cslots, zslots, xc, mc, own, inbox, gni, stage,
-    cs, cr, zs, zr, s_x, sr, rr, sl, rl, s_o, s_d,
+    s_f, cs, cr, zs, zr, s_x, sr, rr, sl, rl, s_o, s_d,
 ):
     seq, tp = lax.axis_index("seq"), lax.axis_index("tp")
     rows = gmix.shape[0]
@@ -756,19 +1051,28 @@
         pltpu.make_async_copy(x_h.at[:, mine], xc, s_x.at[1]),
         pltpu.make_async_copy(mixed_h.at[:, mine], mc, s_x.at[2]),
     ]
-    for copy in fetches:
+    pairs = [
+        (gmix_h, gmix),
+        (w1_h.at[3], w1.at[:, pl.ds(3 * chan, chan)]),
+        (states_h, states), (opre_h, opre), (feff_h, feff), (ipre_h, ipre), (fpre_h, fpre),
+    ] + [(w1_h.at[j], w1.at[:, pl.ds(j * chan, chan)]) for j in range(3)] + [
+        (normed_h, normed), (gated_h, gated),
+    ]
+    inputs = [pltpu.make_async_copy(src, dst, s_f.at[i]) for i, (src, dst) in enumerate(pairs)]
+    fetches[0].start()
+    for copy in inputs[:4]:
         copy.start()
     greet_all(n, t, seq, tp)
+    for copy in fetches[1:] + inputs[4:]:
+        copy.start()
     tile = row_tile(rows)
-    sgain, bound = crow[1:2, :], crow[2:3, :]
+    sgain, bound = consts[1:2, mine], consts[2:3, mine]
     vecs[...] = jnp.zeros_like(vecs)
-    for copy in fetches:
-        copy.wait()
     step = rows // SHARD_CHUNKS
 
     def finish(k, values):
         at = pl.ds(pl.multiple_of(k * step, step), step)
-        ok = valid[at, :]
+        ok, _ = masks(lens, seq * rows + k * step, step)
         m = mc[at, :].astype(F32)
         full = xc[at, :].astype(F32) + m + values
         out[at, :] = full.astype(BF)
@@ -776,19 +1080,24 @@
         vecs[5:6, :] += jnp.sum(ok * values * values, axis=0, keepdims=True)
         vecs[6:7, :] += jnp.sum(ok * full * full, axis=0, keepdims=True)
 
-    steps, step_of, last, drain = line_reduce_scatter(t, seq, tp, own, inbox, (sr, rr, sl, rl), finish)
+    turns, turn, last, drain = line_reduce_scatter(t, seq, tp, own, inbox, (sr, rr, sl, rl), finish)
+    slots = 20
 
     def pump(slot):
         def one(i, c):
-            step_of(i)
+            turn(i)
             return c
 
-        lax.fori_loop(slot * steps // 12, (slot + 1) * steps // 12, one, 0)
+        lax.fori_loop(slot * turns // slots, (slot + 1) * turns // slots, one, 0)
+
+    fetches[0].wait()
+    for copy in inputs[:4]:
+        copy.wait()
 
     def gates(i, c):
+        pump(i)
         at = pl.ds(pl.multiple_of(i * tile, tile), tile)
         shifted = pl.ds(pl.multiple_of(i * tile + 8, 8), tile)
-        pump(i)
         g = nn(gmix[at, :], w1[:, 3 * chan :])
         hat = get(states, shifted) * invst[at, :]
         o = opre[at, :]
@@ -801,10 +1110,9 @@
         inner[at, :] = w * hat
         return c
 
-    lax.fori_loop(0, rows // tile, gates, 0)
-    dot = sum_over_tp(row_sums(inner[...]), t, seq, tp, zslots, zs, zr) / width
+    lax.fori_loop(0, 3, gates, 0)
+    dot = sum_over_tp(row_sums(inner[...]), t, seq, tp, zslots, zs, zr, lambda: pump(3)) / width
     inner[:, 0:1] = dot
-    pump(rows // tile)
 
     def leaving(i, c):
         at = pl.ds(pl.multiple_of(i * tile, tile), tile)
@@ -813,7 +1121,8 @@
         put(weighted, at, inv * (get(weighted, at) - get(states, shifted) * inv * inner[at, 0:1]))
         return c
 
-    lax.fori_loop(0, rows // tile, leaving, 0)
+    lax.fori_loop(0, 3, leaving, 0)
+    inputs[4].wait()
 
     length = rows // SEG
 
@@ -835,11 +1144,15 @@
     for s in range(SEG - 2, -1, -1):
         block_h = h[s : s + 1] + p[s : s + 1] * block_h
         block_p = p[s : s + 1] * block_p
-    pump(rows // tile + 1)
     first = get(feff, slice(0, 1))
-    arriving = carry_over_seq(first * block_p, first * block_h, n, seq, tp, cslots, cs, cr, True)
+    arriving = carry_over_seq(
+        first * block_p, first * block_h, n, seq, tp, cslots, cs, cr, True, lambda: pump(4)
+    )
+    inputs[5].wait()
+    inputs[6].wait()
     bias_sum = jnp.zeros((1, chan), F32)
     for s in range(SEG - 1, -1, -1):
+        pump(12 - s)
         at = slice(s * length, (s + 1) * length)
         gs = get(weighted, at) + get(prod, at) * arriving
         arriving = h[s : s + 1] + p[s : s + 1] * arriving
@@ -848,29 +1161,30 @@
         act = a * sa
         sf = jax.nn.sigmoid(fpre[at, :])
         gate = bound + (1.0 - bound) * sf
-        ok = valid[at, :]
+        ok, starts = masks(lens, seq * rows + s * length, length)
         out3[at, :chan] = (gs * (1.0 - gate) * ok * (sa * (1.0 + a * (1.0 - sa)))).astype(BF)
         before = get(states, slice(s * length + 7, (s + 1) * length + 7))
-        gate_grad = gs * before * (1.0 - starts[at, :]) - gs * act * ok
+        gate_grad = gs * before * (1.0 - starts) - gs * act * ok
         gf = (gate_grad * (1.0 - bound) * sf * (1.0 - sf)).astype(BF)
         out3[at, chan : 2 * chan] = gf
         bias_sum = bias_sum + jnp.sum(gf.astype(F32), axis=0, keepdims=True)
-        if s % 2 == 0:
-            pump(rows // tile + 5 - s // 2)
     vecs[1:2, :] = bias_sum
 
     def gni_copy(i):
         at = pl.ds(pl.multiple_of(i * tile, tile), tile)
         return pltpu.make_async_copy(gni.at[:, at], gni_h.at[:, at], s_o.at[i])
+
+    for copy in inputs[7:]:
+        copy.wait()
 
     def spread_in(i, c):
         at = pl.ds(pl.multiple_of(i * tile, tile), tile)
         put_shards(gni, at, nt(out3[at, :], w1[:, : 3 * chan]).astype(BF))
         gni_copy(i).start()
-        pump(12 - rows // tile + i)
-        return c
-
-    lax.fori_loop(0, rows // tile, spread_in, 0)
+        pump(13 + i)
+        return c
+
+    lax.fori_loop(0, 3, spread_in, 0)
 
     ga, gb, h = dw1_h.shape[2:5]
     span = 4 * h
@@ -891,9 +1205,18 @@
         put_blocks(stage.at[slot, :, :, :, pl.ds(0, 3 * chan)], h, tn(normed[:, at], out3[...]))
         put_blocks(stage.at[slot, :, :, :, pl.ds(3 * chan, chan)], h, tn(gmix[:, at], gated[...]))
         d_copy(r, slot).start()
+
+        @pl.when(r < 4)
+        def _():
+            pump(16 + r)
+
         return c
 
     lax.fori_loop(0, ga * gb, slab, 0)
+    for r in range(ga * gb, 4):
+        pump(16 + r)
+    for copy in fetches[1:]:
+        copy.wait()
 
     def ending(k, c):
         last(k)
@@ -907,20 +1230,25 @@
         gni_copy(i).wait()
         return c
 
-    lax.fori_loop(0, rows // tile, stored, 0)
+    lax.fori_loop(0, 3, stored, 0)
     drain()
 
 
 def closing(
     n, t, width,
-    gni_h, dw1_h, xc, gres, invin, gain_in, vecs, ggain,
+    gni_h, dw1_h, x_h, gres_h, invin, consts, vecs, ggain,
     gin, allvec, sums,
-    own, inbox, scaled, inner, zslots, vslots,
-    s_own, sr, rr, sl, rl, zs, zr, vs, vr, ts, tr, *bufs,
+    xc, gres, own, inbox, scaled, inner, zslots, vslots,
+    s_own, s_x, sr, rr, sl, rl, zs, zr, vs, vr, ts, tr, *bufs,
 ):
     seq, tp = lax.axis_index("seq"), lax.axis_index("tp")
     rows, chan = gres.shape
+    mine = pl.ds(pl.multiple_of(tp * chan, LANE), chan)
     fetch = pltpu.make_async_copy(gni_h, own, s_own)
+    fetches = [
+        pltpu.make_async_copy(x_h.at[:, mine], xc, s_x.at[0]),
+        pltpu.make_async_copy(gres_h, gres, s_x.at[1]),
+    ]
     fetch.start()
     greet_all(n, t, seq, tp)
     pieces, shard, cols = sums.shape
@@ -931,60 +1259,68 @@
     start, stage1, stage2, stage3, drain_grid = grid_reduce(
         n, seq, tp, dw1_h, pieces, cols, bufs, out
     )
+    fetch.wait()
     start(0)
-    start(1)
-    fetch.wait()
+    for copy in fetches:
+        copy.start()
     step = rows // SHARD_CHUNKS
+    gain_in = consts[4:5, mine]
     vslots[seq] = vecs[...]
-    vslots[seq, 3:4, :] = ggain[0:1, :]
+    vslots[seq, 3:4, :] = ggain[0:1, mine]
 
     def finish(k, values):
         at = pl.ds(pl.multiple_of(k * step, step), step)
         hat = xc[at, :].astype(F32) * invin[at, :]
-        s = values * gain_in[...]
+        s = values * gain_in
         scaled[at, :] = s
         inner[at, :] = s * hat
         vslots[seq, 0:1, :] += jnp.sum(values * hat, axis=0, keepdims=True)
 
-    steps, step_of, last, drain = line_reduce_scatter(t, seq, tp, own, inbox, (sr, rr, sl, rl), finish)
-    turns = [
-        (2, lambda: stage1(0)),
-        (4, lambda: stage1(1)),
+    turns, turn, last, drain = line_reduce_scatter(t, seq, tp, own, inbox, (sr, rr, sl, rl), finish)
+    works = [
+        (2, lambda: (stage1(0), start(1))),
+        (5, lambda: stage1(1)),
         (6, lambda: stage2(0)),
         (9, lambda: stage3(0)),
         (10, lambda: stage2(1)),
-        (11, lambda: stage3(1)),
+        (13, lambda: stage3(1)),
     ]
+    slots = 16
 
     def turn_of(slot, c):
         def one(i, c):
-            step_of(i)
+            turn(i)
             return c
 
-        lax.fori_loop(slot * steps // 12, (slot + 1) * steps // 12, one, 0)
-        for turn, work in turns:
-
-            @pl.when(slot == turn)
+        lax.fori_loop(slot * turns // slots, (slot + 1) * turns // slots, one, 0)
+        for when, work in works:
+
+            @pl.when(slot == when)
             def _(work=work):
                 work()
 
         return c
 
-    lax.fori_loop(0, 12, turn_of, 0)
+    lax.fori_loop(0, slots, turn_of, 0)
+    for copy in fetches:
+        copy.wait()
 
     def ending(k, c):
         last(k)
         return c
 
     lax.fori_loop(0, SHARD_CHUNKS, ending, 0)
-    dot = sum_over_tp(row_sums(inner[...]), t, seq, tp, zslots, zs, zr) / width
-    gin[...] = gres[...] + invin[...] * (scaled[...] - xc[...].astype(F32) * invin[...] * dot)
-    spread(n, seq, vslots, vs, vr, lambda k: (k, tp))
+    go_v, done_v = spread(n, seq, vslots, vs, vr, lambda k: (k, tp))
+    dot = sum_over_tp(row_sums(inner[...]), t, seq, tp, zslots, zs, zr, go_v) / width
+    done_v()
     total = vslots[0]
     for k in range(1, n):
         total = total + vslots[k]
     allvec[tp] = total
-    spread(t, tp, allvec, ts, tr, lambda k: (seq, k))
+    go_t, done_t = spread(t, tp, allvec, ts, tr, lambda k: (seq, k))
+    go_t()
+    gin[...] = gres[...] + invin[...] * (scaled[...] - xc[...].astype(F32) * invin[...] * dot)
+    done_t()
     drain()
     drain_grid()
 
@@ -1010,76 +1346,69 @@
     chan = w_input.shape[1]
     ff = w_gate.shape[1]
     ffp = -(-ff // LANE) * LANE
-    tp = lax.axis_index("tp")
-    offset = tp * chan
 
     def padded(w):
         return w if ffp == ff else jnp.pad(w, ((0, 0), (0, ffp - ff)))
 
-    w1 = lax.all_gather(
-        jnp.concatenate([w_input, w_forget, w_outgate, w_output.T], axis=1), "seq", axis=0, tiled=True
+    total = lengths[0] + lengths[1]
+    bound = layer_index[0].astype(F32) / LAYERS
+    consts = jnp.stack(
+        [
+            forget_bias,
+            state_gain.astype(F32),
+            jnp.broadcast_to(bound, (width,)),
+            gain_mid.astype(F32),
+            gain_in.astype(F32),
+        ]
+        + [jnp.zeros((width,), F32)] * 3
     )
-    w2 = lax.all_gather(
-        jnp.concatenate([padded(w_gate), padded(w_up), padded(w_down.T)], axis=1),
-        "seq", axis=0, tiled=True,
-    )
-
-    positions = lax.axis_index("seq") * rows + jnp.arange(rows, dtype=jnp.int32)
-    total = lengths[0] + lengths[1]
-    valid = (positions < total).astype(F32)[:, None]
-    starts = ((positions == 0) | (positions == lengths[0])).astype(F32)[:, None]
-    bound = layer_index[0].astype(F32) / LAYERS
-    inputs_f = hidden_in.astype(F32)
-    inv_in = lax.rsqrt(jnp.mean(inputs_f * inputs_f, axis=-1, keepdims=True) + EPS)
-    normed_in = (inputs_f * inv_in * gain_in.astype(F32)).astype(BF)
-
-    def cols(vector):
-        return lax.dynamic_slice_in_dim(vector, offset, chan, 0).astype(F32)
-
-    crow = jnp.concatenate(
-        [
-            cols(forget_bias)[None],
-            cols(state_gain)[None],
-            jnp.broadcast_to(bound, (1, chan)),
-            jnp.zeros((5, chan), F32),
-        ],
-        axis=0,
-    )
-    gmid = gain_mid.astype(F32)[None]
     plane = shape((rows, chan), F32)
+    plane16 = shape((rows, chan), BF)
     column = shape((rows, 1), F32)
+    wide16 = shape((rows, width), BF)
+    shards16 = shape((t, rows, chan), BF)
     ga, gb = chip_grid(n)
     h = width // n // 2
-    shards16 = shape((t, rows, chan), BF)
 
     def groups(more=0):
         return shape((chan // LANE, rows + more, LANE), F32)
 
-    wide16 = shape((rows, width), BF)
-
-    ipre, fpre, opre, feff, states, gated, nmid, mixed, invst, invmid = pl.pallas_call(
+    def vm(*arrays):
+        return [pltpu.VMEM(a.shape, a.dtype) for a in arrays]
+
+    SM = pl.BlockSpec(memory_space=pltpu.SMEM)
+    w1s, w2s = shape((4, width, chan), BF), shape((3, width, ffp), BF)
+    zslot, vslot = pltpu.VMEM((t, 8, rows), F32), pltpu.VMEM((n, 8, chan), F32)
+    small = [DMA((n,)), DMA((n,)), DMA((t,)), DMA((t,))]
+    saved = [plane, plane, plane, groups(8), groups(8), plane16, wide16]
+
+    (
+        ipre, fpre, opre, feff, states, gated, normed_in, nmid, mixed, w1, w2, invst, invmid, inv_in,
+    ) = pl.pallas_call(
         functools.partial(mixer_forward, n, t, width),
-        out_shape=[
-            plane, plane, plane,
-            groups(8), groups(8),
-            shape((rows, chan), BF), wide16, wide16, column, column,
-        ],
-        in_specs=[VM] * 7,
-        out_specs=[VM] * 10,
+        out_shape=saved + [wide16, wide16, w1s, w2s, column, column, column],
+        in_specs=[SM] + [HB] * 8 + [VM],
+        out_specs=[HB] * 11 + [VM] * 3,
         scratch_shapes=[
-            pltpu.VMEM(groups().shape, F32),
-            pltpu.VMEM((rows, chan), F32),
+            *vm(wide16, wide16, plane, plane, plane, groups(8), groups(8), plane16, wide16, w1s),
+            *vm(groups(), plane),
             pltpu.VMEM((rows // CHUNKS * 4, width), F32),
-            pltpu.VMEM((n, 8, chan), F32),
-            pltpu.VMEM((t, 8, rows), F32),
+            vslot,
+            zslot,
             pltpu.VMEM((rows, width), BF),
             pltpu.VMEM((2, rows, width), BF),
-            DMA((n,)), DMA((n,)), DMA((t,)), DMA((t,)),
+            DMA, DMA((7,)), DMA((4,)), DMA((CHUNKS,)), DMA((CHUNKS,)),
+            *small,
             *line_sems(CHUNKS),
+            *gather_sems(n, 4),
+            *gather_sems(n, 3),
         ],
         compiler_params=params(1),
         name="mixer_forward",
-    )(normed_in, hidden_in, w1, crow, gmid, valid, starts)
+    )(
+        lengths, hidden_in, w_input, w_forget, w_outgate, w_output.T,
+        padded(w_gate), padded(w_up), padded(w_down.T), consts,
+    )
 
     gnm_part, glu_part, dw2 = pl.pallas_call(
         feed_forward,
@@ -1087,99 +1416,87 @@
         in_specs=[HB] * 3,
         out_specs=[HB] * 3,
         scratch_shapes=[
-            pltpu.VMEM((rows, width), BF),
-            pltpu.VMEM((rows, width), BF),
-            pltpu.VMEM((width, ffp), BF),
-            pltpu.VMEM((width, ffp), BF),
-            pltpu.VMEM((width, ffp), BF),
-            pltpu.VMEM((rows, ffp), BF),
-            pltpu.VMEM((rows, ffp), BF),
-            pltpu.VMEM((rows, ffp), BF),
-            pltpu.VMEM((rows, width), BF),
-            pltpu.VMEM((t, rows, chan), BF),
+            *vm(wide16, wide16),
+            *[pltpu.VMEM((width, ffp), BF)] * 3,
+            *[pltpu.VMEM((rows, ffp), BF)] * 3,
+            *vm(wide16, shards16),
             pltpu.VMEM((2, 2, 2, h, ffp), BF),
-            DMA((3,)), DMA((2,)), DMA((2, rows // row_tile(rows))), DMA((2,)),
+            DMA((3,)), DMA((2,)), DMA((2, 3)), DMA((2,)),
         ],
         compiler_params=params(),
-        cost_estimate=pl.CostEstimate(
-            flops=18 * rows * width * ffp, bytes_accessed=50_000_000, transcendentals=0
-        ),
         name="feed_forward",
     )(nmid, cotangent, w2)
 
+    sums2s = shape((3, 2 * h, ffp), F32)
     gmix, gres, ggain, sums2 = pl.pallas_call(
         functools.partial(mid_backward, n, t, width),
-        out_shape=[wide16, plane, shape((8, width), F32), shape((3, 2 * h, ffp), F32)],
-        in_specs=[HB] * 2 + [VM] * 5,
-        out_specs=[VM] * 4,
+        out_shape=[wide16, plane, shape((8, width), F32), sums2s],
+        in_specs=[HB] * 5 + [VM] * 2,
+        out_specs=[HB] * 2 + [VM, HB],
         scratch_shapes=[
-            pltpu.VMEM((rows, width), BF),
+            *vm(wide16, wide16, wide16, wide16, plane, sums2s, wide16),
             pltpu.VMEM((2, rows, width), BF),
             pltpu.VMEM((rows // CHUNKS, width), F32),
-            DMA,
+            DMA, DMA((3,)), DMA((2, CHUNKS)), DMA((3,)),
             *line_sems(CHUNKS),
             *grid_buffers(n, width, 3, ffp),
         ],
         compiler_params=params(2),
         name="mid_backward",
-    )(gnm_part, dw2, hidden_in, mixed, invmid, cotangent, gmid)
+    )(gnm_part, dw2, hidden_in, mixed, cotangent, invmid, consts)
 
     shard_sems = [DMA((t, SHARD_CHUNKS))] * 4
     shard_bufs = [pltpu.VMEM((t, rows, chan), BF), pltpu.VMEM((t + 1, rows, chan), BF)]
     gni_part, dw1, vecs, block_out = pl.pallas_call(
         functools.partial(mixer_backward, n, t, width),
         out_shape=[
-            shards16, shape((2, 2, ga, gb, h, 4 * chan), BF), shape((8, chan), F32),
-            shape((rows, chan), BF),
+            shards16, shape((2, 2, ga, gb, h, 4 * chan), BF), shape((8, chan), F32), plane16,
         ],
-        in_specs=[HB] * 3 + [VM] * 13,
+        in_specs=[SM] + [HB] * 12 + [VM] * 2,
         out_specs=[HB] * 2 + [VM] * 2,
         scratch_shapes=[
-            pltpu.VMEM(groups().shape, F32),
-            pltpu.VMEM(groups().shape, F32),
-            pltpu.VMEM((rows, chan), F32),
-            pltpu.VMEM((rows, 3 * chan), BF),
-            pltpu.VMEM((n, 8, chan), F32),
-            pltpu.VMEM((t, 8, rows), F32),
-            pltpu.VMEM((rows, chan), BF),
-            pltpu.VMEM((rows, chan), BF),
+            *vm(wide16, wide16),
+            pltpu.VMEM((width, 4 * chan), BF),
+            *vm(plane16, groups(8), groups(8), plane, plane, plane),
+            *vm(groups(), groups(), plane, shape((rows, 3 * chan), BF)),
+            vslot,
+            zslot,
+            *vm(plane16, plane16),
             *shard_bufs,
-            pltpu.VMEM((t, rows, chan), BF),
+            *vm(shards16),
             pltpu.VMEM((2, 2, 2, h, 4 * chan), BF),
-            DMA((n,)), DMA((n,)), DMA((t,)), DMA((t,)), DMA((3,)),
+            DMA((12,)),
+            *small,
+            DMA((3,)),
             *shard_sems,
-            DMA((rows // row_tile(rows),)), DMA((2,)),
+            DMA((3,)), DMA((2,)),
         ],
         compiler_params=params(3),
         name="mixer_backward",
     )(
-        glu_part, hidden_in, mixed,
-        gmix, normed_in, w1, gated, states, feff, ipre, fpre, opre, invst, valid, starts, crow,
+        lengths, glu_part, hidden_in, mixed, gmix, normed_in, w1, gated, states, feff, ipre, fpre, opre,
+        invst, consts,
     )
 
-    ggain_cols = lax.dynamic_slice_in_dim(ggain, offset, chan, 1)
-    x_cols = lax.dynamic_slice_in_dim(hidden_in, offset, chan, 1)
     grad_in, allvec, sums1 = pl.pallas_call(
         functools.partial(closing, n, t, width),
         out_shape=[plane, shape((t, 8, chan), F32), shape((2, 2 * h, 2 * chan), F32)],
-        in_specs=[HB] * 2 + [VM] * 6,
+        in_specs=[HB] * 4 + [VM] * 4,
         out_specs=[VM] * 3,
         scratch_shapes=[
+            *vm(plane16, plane),
             *shard_bufs,
-            pltpu.VMEM((rows, chan), F32),
-            pltpu.VMEM((rows, chan), F32),
-            pltpu.VMEM((t, 8, rows), F32),
-            pltpu.VMEM((n, 8, chan), F32),
-            DMA,
+            *vm(plane, plane),
+            zslot,
+            vslot,
+            DMA, DMA((2,)),
             *shard_sems,
             DMA((t,)), DMA((t,)), DMA((n,)), DMA((n,)), DMA((t,)), DMA((t,)),
             *grid_buffers(n, width, 2, 2 * chan),
         ],
         compiler_params=params(4),
         name="closing",
-    )(
-        gni_part, dw1, x_cols, gres, inv_in, cols(gain_in)[None], vecs, ggain_cols,
-    )
+    )(gni_part, dw1, hidden_in, gres, inv_in, consts, vecs, ggain)
 
     def vector(r):
         return allvec[:, r, :].reshape(width)

time: 549 us -> 456 us (0.83)
  waiting for transfers between devices: 40.1 us -> 0 us
  Pallas kernels: 455 us -> 427 us
  between operations: 16.1 us -> 2.66 us
  other arithmetic: 17.9 us -> 7.02 us
    all_gather x2 -> x0, waiting for transfers between devices: 40.1 us -> none  [the longest x1 40.1 us: on_device(): lax.all_gather(jnp.concatenate([w_input, w_forget, w_outgate, w_output.T]...]
    pallas_call x1, Pallas kernels: 94.9 us -> 69.4 us  [on_device(): pl.pallas_call(functools.partial(mixer_backward, n, t, width), out_shape=...]
    pallas_call x1, Pallas kernels: 118 us -> 135 us  [on_device(): pl.pallas_call(functools.partial(mixer_forward, n, t, width), out_shape=s...]
    pallas_call x1, Pallas kernels: 84 us -> 71.3 us  [on_device(): pl.pallas_call(functools.partial(closing, n, t, width), out_shape=[plane,...]
    concatenate x3 -> x0, other arithmetic: 6.05 us -> none  [the longest x1 3.17 us: on_device(): jnp.concatenate([padded(w_gate), padded(w_up), padded(w_down.T)], axis=1)]
  transfers between devices with their start and end apart: 2 -> 0, of which waited for: 1 -> 0; matrix products, arithmetic and copies ran while one was open for 3% -> 0% of each run, Pallas kernels for 22% -> 0%
where the time goes in v3:
time: 456 us
  Pallas kernels  427 us (94%)
  local copies, waits for them, and re-layouts  18.6 us (4%)
  other arithmetic  7.02 us (2%)
    pallas_call x1, Pallas kernels, on_device(): pl.pallas_call(functools.partial(mixer_forward, n, t, width), out_shape=s...  135 us
    pallas_call x1, Pallas kernels, on_device(): pl.pallas_call(functools.partial(mid_backward, n, t, width), out_shape=[w...  96.8 us
    pallas_call x1, Pallas kernels, on_device(): pl.pallas_call(functools.partial(closing, n, t, width), out_shape=[plane,...  71.3 us
    pallas_call x1, Pallas kernels, on_device(): pl.pallas_call(functools.partial(mixer_backward, n, t, width), out_shape=...  69.4 us
    pallas_call x1, Pallas kernels, on_device(): pl.pallas_call(feed_forward, out_shape=[wide16, shards16, shape((2, 2, ga...  55.3 us
    unnamed x10, local copies, waits for them, and re-layouts  9.78 us

profile of v3, /device:TPU:0, one launch (start us, length us, event | category | flops | bytes accessed | tf_op | source)
XLA Modules:
  0.0 455.7 jit_solution(15630175635184637565)
XLA Ops:
  1.3 0.7 stack.52
  2.0 0.7 stack.53
  2.7 0.7 stack.54
  3.4 1.4 stack.47.consts
  4.8 2.2 copy.30
  7.0 1.8 copy.29
  8.8 134.6 %mixer_forward.1 = (f32[768,512]{1,0:T(8,128)}, f32[768,512]{1,0:T(8,128)}, f32[768,512]{1,0:T(8,128)}, f32[4,776,128]{2,1,0:T(8,128)}, f32[4,776,128]{2,1,0:T(8...) custom-call(s32[2]{0:T(128)} %lens.3, ...), custom_call_target="tpu_custom_call" | custom-call | tf_op jit(solution)/shard_map/mixer_forward/pallas_call | solution.py:1387
  143.4 55.3 %feed_forward.1 = (bf16[768,2048]{1,0:T(8,128)(2,1)}, bf16[4,768,512]{2,1,0:T(8,128)(2,1)}, bf16[2,2,2,2,128,4224]{5,4,3,2,1,0:T(8,128)(2,1)}) custom-call(bf16[768,2048]{1,0:T(8,128)(2,1)} %get-tuple-element.42.nmid_h, bf16[768,2048]{1,0:T(8,128)(2,1)} %cot_h.3, bf16[3,2048,1408]{2,1,0:T(8,128)(2,1)} %get-tuple-element.43.w2_h), custom_call_target="tpu_custom_call" | custom-call | tf_op jit(solution)/shard_map/feed_forward/pallas_call | solution.py:1413
  198.7 96.8 %mid_backward.1 = (bf16[768,2048]{1,0:T(8,128)(2,1)}, f32[768,512]{1,0:T(8,128)}, f32[8,2048]{1,0:T(8,128)}, f32[3,256,1408]{2,1,0:T(8,128)}) custom-call(bf16[768,2048]{1,0:T(8,128)(2,1)} %get-tuple-element.46.gnm_h, bf16[2,2,2,2,128,4224]{5,4,3,2,1,0:T(8,128)(2,1)} %get-tuple-element.47.dw2_h, bf16[768,2048]{1,0:T(8,128)(2,1)} %x_h.7, ...), custom_call_target="tpu_custom_call" | custom-call | tf_op jit(solution)/shard_map/mid_backward/pallas_call | solution.py:1431
  295.5 69.4 %mixer_backward.1 = (bf16[4,768,512]{2,1,0:T(8,128)(2,1)}, bf16[2,2,2,2,128,2048]{5,4,3,2,1,0:T(8,128)(2,1)}, f32[8,512]{1,0:T(8,128)}, bf16[768,512]{1,0:T(8,128)(2,1)}) custom-call(s32[2]{0:T(128)} %lens.3, bf16[4,768,512]{2,1,0:T(8,128)(2,1)} %get-tuple-element.44.glu_h, bf16[768,2048]{1,0:T(8,128)(2,1)} %x_h.7, ...), custom_call_target="tpu_custom_call" | custom-call | tf_op jit(solution)/shard_map/mixer_backward/pallas_call | solution.py:1450
  364.9 0.0 copy-start.1
  364.9 71.3 %closing.1 = (f32[768,512]{1,0:T(8,128)}, f32[4,8,512]{2,1,0:T(8,128)}, f32[2,256,1024]{2,1,0:T(8,128)}) custom-call(bf16[4,768,512]{2,1,0:T(8,128)(2,1)} %get-tuple-element.60.gni_h, bf16[2,2,2,2,128,2048]{5,4,3,2,1,0:T(8,128)(2,1)} %get-tuple-element.61.dw1_h, bf16[768,2048]{1,0:T(8,128)(2,1)} %x_h.7, f32[768,512]{1,0:T(8,128)} %get-tuple-element.62.gres_h, ...), custom_call_target="tpu_custom_call" | custom-call | tf_op jit(solution)/shard_map/closing/pallas_call | solution.py:1481
  436.3 2.4 slice_reduce_fusion.2
  438.7 0.0 copy-done.1
  438.7 0.6 fusion.1
  440.6 2.5 fusion
  443.1 2.7 slice_bitcast_fusion.3
  445.8 1.0 copy.31
  446.8 4.1 slice_bitcast_fusion
  450.9 0.0 copy-start
  450.9 1.5 copy.32
  452.4 2.1 copy.36
  454.5 0.0 copy-done
  454.5 1.1 copy.37
  (3 shorter events, 0.0 us)
Async XLA Ops:
  364.9 73.8 %copy-start.1 = (s32[2]{0:T(128)S(1)}, s32[2]{0:T(128)}, u32[]{:S(2)}) copy-start(s32[2]{0:T(128)} %lens.3) | copy-start | bytes 28
  450.9 3.6 copy-start

commit v4 on v3

--- a/solution.py
+++ b/solution.py
@@ -17,10 +17,11 @@
 HB = pl.BlockSpec(memory_space=pl.ANY)
 LANE = 128
 SEG = 8
+TILES = 4
+K2_LAGS = (2, 2, 3)
 CHUNKS = 16
 SHARD_CHUNKS = 4
 HOP_LAG = 2
-ROUND_TRIP = 3
 VMEM_LIMIT = 60 * 1024 * 1024
 
 
@@ -53,13 +54,6 @@
     k = ref.shape[2]
     for q in range(ref.shape[0]):
         ref[q, at, :] = values[:, q * k : (q + 1) * k]
-
-
-def put_blocks(ref, h, values):
-    for core in range(2):
-        for half in range(2):
-            first = (core * 2 + half) * h
-            ref[core, half] = values[first : first + h].astype(ref.dtype)
 
 
 def row_tile(rows):
@@ -165,7 +159,7 @@
     return lax.fori_loop(0, n, hop, jnp.zeros_like(prod))
 
 
-def line_all_reduce(t, seq, tp, rows, chunks, partial, send, buf, sems, finish, beside=None):
+def line_all_reduce(t, seq, tp, rows, chunks, partial, send, buf, sems, finish, lags):
     s_in, s_out, r_buf = sems
     step = rows // chunks
     half = t // 2
@@ -174,6 +168,9 @@
     outer = jnp.where(tp < half, tp - 1, tp + 1)
     outer = jnp.where(depth > 0, outer, inner)
     middle = (depth == half - 1).astype(jnp.int32)
+    lag_in, lag_turn, lag_out = lags
+    lag_first = lag_in * depth
+    lag_second = lag_in * (half - 1) + lag_turn + lag_out * (half - 1 - depth)
 
     def part_of(k):
         return pl.ds(pl.multiple_of(k * step, step), step)
@@ -199,16 +196,19 @@
         )
 
     def first(k):
-        part = partial(k)
+        part = None if partial is None else partial(k)
 
         @pl.when(depth > 0)
         def _():
             inward(k, 0).wait_recv()
-            send[part_of(k), :] = (part + buf[0, part_of(k), :].astype(F32)).astype(BF)
-
-        @pl.when(depth == 0)
-        def _():
-            send[part_of(k), :] = part.astype(BF)
+            mine = send[part_of(k), :].astype(F32) if part is None else part
+            send[part_of(k), :] = (mine + buf[0, part_of(k), :].astype(F32)).astype(BF)
+
+        if part is not None:
+
+            @pl.when(depth == 0)
+            def _():
+                send[part_of(k), :] = part.astype(BF)
 
         inward(k, middle).start()
 
@@ -226,33 +226,28 @@
 
         finish(k)
 
-    lag = 1 + ROUND_TRIP * (half - 1 - depth)
-
-    def both(k, c):
-        @pl.when(k < chunks)
-        def _():
-            first(k)
-
-        @pl.when((k >= lag) & (k - lag < chunks))
-        def _():
-            second(k - lag)
-
-        if beside is not None:
-            beside(k)
-        return c
-
-    lax.fori_loop(0, chunks + 1 + ROUND_TRIP * (half - 1), both, 0)
-
-    def drain(k, c):
-        inward(k, middle).wait_send()
-
-        @pl.when(depth > 0)
-        def _():
-            outward(k).wait_send()
-
-        return c
-
-    lax.fori_loop(0, chunks, drain, 0)
+    def turn(i):
+        @pl.when((i >= lag_first) & (i - lag_first < chunks))
+        def _():
+            first(i - lag_first)
+
+        @pl.when((i >= lag_second) & (i - lag_second < chunks))
+        def _():
+            second(i - lag_second)
+
+    def drain():
+        def sent(k, c):
+            inward(k, middle).wait_send()
+
+            @pl.when(depth > 0)
+            def _():
+                outward(k).wait_send()
+
+            return c
+
+        lax.fori_loop(0, chunks, sent, 0)
+
+    return chunks + lag_in * (half - 1) + lag_turn + lag_out * (half - 1), turn, drain
 
 
 def line_reduce_scatter(t, seq, tp, own, inbox, sems, finish):
@@ -372,144 +367,120 @@
     h = width // n // 2
     pa, pb = max(ga - 1, 1), max(gb - 1, 1)
     return [
-        pltpu.VMEM((pieces, 2, ga, gb, h, cols), BF),
-        pltpu.VMEM((pieces, 2, ga, gb, h, cols), BF),
         pltpu.VMEM((pieces, pb, ga, h, cols), BF),
         pltpu.VMEM((pieces, pa, gb, h, cols), BF),
         pltpu.VMEM((pieces, pa, h, cols), BF),
         pltpu.VMEM((pieces, pb, h, cols), BF),
-        DMA((pieces,)), DMA((pieces,)), DMA((pieces,)),
-        DMA((2, pieces, pb)), DMA((2, pieces, pa)), DMA((2, pieces, pa)), DMA((2, pieces, pb)),
+        DMA((2, pieces, pb, ga)), DMA((2, pieces, pa, gb)), DMA((2, pieces, pa)), DMA((2, pieces, pb)),
     ]
 
 
-def grid_reduce(n, seq, tp, terms, pieces, cols, bufs, out):
-    acc, first, far_b, far_a, near_a, near_b, s_own, s_f, r_f, m_fb, m_fa, m_na, m_nb = bufs
+def add_cores(acc, first):
+    part = 64
+
+    def one(i, c):
+        at = pl.ds(pl.multiple_of(i * part, part), part)
+        acc[at, :] = (acc[at, :].astype(F32) + first[at, :].astype(F32)).astype(BF)
+        return c
+
+    lax.fori_loop(0, acc.shape[0] // part, one, 0)
+
+
+def grid_reduce(n, seq, tp, j, acc, bufs, out):
+    far_b, far_a, near_a, near_b, m_fb, m_fa, m_na, m_nb = bufs
     ga, gb = chip_grid(n)
     core = lax.rem(seq, 2)
     a, b = seq // 2 // gb, lax.rem(seq // 2, gb)
-
-    def device(a_, b_, core_):
-        return ((a_ * gb + b_) * 2 + core_, tp)
-
-    def columns(j):
-        return pl.ds(j * cols, cols)
-
-    def load(j):
-        return pltpu.make_async_copy(
-            terms.at[core, :, :, :, :, columns(j)], acc.at[j], s_own.at[j]
-        )
-
-    def swap(j):
+    h = near_a.shape[2]
+
+    def device(a_, b_):
+        return ((a_ * gb + b_) * 2 + core, tp)
+
+    def block(half, x, y):
+        return pl.ds(pl.multiple_of(((x * gb + y) * 2 + half) * h, h), h)
+
+    def remote(rows, dst, sems, index, target):
         return pltpu.make_async_remote_copy(
-            src_ref=terms.at[1 - core, :, :, :, :, columns(j)],
-            dst_ref=first.at[j],
-            send_sem=s_f.at[j],
-            recv_sem=r_f.at[j],
-            device_id=device(a, b, 1 - core),
-            device_id_type=MESH,
-        )
-
-    def remote(src, dst, sems, j, o, target):
-        return pltpu.make_async_remote_copy(
-            src_ref=src,
+            src_ref=acc.at[rows],
             dst_ref=dst,
-            send_sem=sems.at[0, j, o],
-            recv_sem=sems.at[1, j, o],
+            send_sem=sems.at[(0, j) + index],
+            recv_sem=sems.at[(1, j) + index],
             device_id=target,
             device_id_type=MESH,
         )
 
-    def far(j):
+    def first_way():
         copies = []
         for o in range(1, gb):
             to = lax.rem(b + o, gb)
-            copies.append(
-                remote(acc.at[j, 0, :, to], far_b.at[j, o - 1], m_fb, j, o - 1, device(a, to, core))
-            )
+            for x in range(ga):
+                dst = far_b.at[j, o - 1, x]
+                copies.append(remote(block(0, x, to), dst, m_fb, (o - 1, x), device(a, to)))
         for o in range(1, ga):
             to = lax.rem(a + o, ga)
-            copies.append(
-                remote(acc.at[j, 1, to], far_a.at[j, o - 1], m_fa, j, o - 1, device(to, b, core))
-            )
+            for y in range(gb):
+                dst = far_a.at[j, o - 1, y]
+                copies.append(remote(block(1, to, y), dst, m_fa, (o - 1, y), device(to, b)))
         return copies
 
-    def near(j):
+    def second_way():
         copies = []
         for o in range(1, ga):
             to = lax.rem(a + o, ga)
             copies.append(
-                remote(acc.at[j, 0, to, b], near_a.at[j, o - 1], m_na, j, o - 1, device(to, b, core))
+                remote(block(0, to, b), near_a.at[j, o - 1], m_na, (o - 1,), device(to, b))
             )
         for o in range(1, gb):
             to = lax.rem(b + o, gb)
             copies.append(
-                remote(acc.at[j, 1, a, to], near_b.at[j, o - 1], m_nb, j, o - 1, device(a, to, core))
+                remote(block(1, a, to), near_b.at[j, o - 1], m_nb, (o - 1,), device(a, to))
             )
         return copies
 
-    def start(j):
-        load(j).start()
-        swap(j).start()
-
-    def stage1(j):
-        load(j).wait()
-        swap(j).wait_recv()
-
-        def chip(i, c):
-            x, y = i // gb, lax.rem(i, gb)
-            for half in range(2):
-                acc[j, half, x, y] = (
-                    acc[j, half, x, y].astype(F32) + first[j, half, x, y].astype(F32)
-                ).astype(BF)
-            return c
-
-        lax.fori_loop(0, ga * gb, chip, 0)
-        for copy in far(j):
+    def far():
+        for copy in first_way():
             copy.start()
 
-    def stage2(j):
-        for copy in far(j):
+    def middle():
+        for copy in first_way():
             copy.wait_recv()
 
         def along_a(x, c):
-            total = acc[j, 0, x, b].astype(F32)
+            total = acc[block(0, x, b), :].astype(F32)
             for o in range(1, gb):
                 total = total + far_b[j, o - 1, x].astype(F32)
-            acc[j, 0, x, b] = total.astype(BF)
+            acc[block(0, x, b), :] = total.astype(BF)
             return c
 
         def along_b(y, c):
-            total = acc[j, 1, a, y].astype(F32)
+            total = acc[block(1, a, y), :].astype(F32)
             for o in range(1, ga):
                 total = total + far_a[j, o - 1, y].astype(F32)
-            acc[j, 1, a, y] = total.astype(BF)
+            acc[block(1, a, y), :] = total.astype(BF)
             return c
 
         lax.fori_loop(0, ga, along_a, 0)
         lax.fori_loop(0, gb, along_b, 0)
-        for copy in near(j):
+        for copy in second_way():
             copy.start()
 
-    def stage3(j):
-        for copy in near(j):
+    def near():
+        for copy in second_way():
             copy.wait_recv()
-        total = acc[j, 0, a, b].astype(F32)
+        total = acc[block(0, a, b), :].astype(F32)
         for o in range(1, ga):
             total = total + near_a[j, o - 1].astype(F32)
-        out(j, 0, total)
-        total = acc[j, 1, a, b].astype(F32)
+        out(0, total)
+        total = acc[block(1, a, b), :].astype(F32)
         for o in range(1, gb):
             total = total + near_b[j, o - 1].astype(F32)
-        out(j, 1, total)
+        out(1, total)
 
     def drain():
-        for j in range(pieces):
-            swap(j).wait_send()
-            for copy in far(j) + near(j):
-                copy.wait_send()
-
-    return start, stage1, stage2, stage3, drain
+        for copy in first_way() + second_way():
+            copy.wait_send()
+
+    return far, middle, near, drain
 
 
 def gather_sems(n, pieces):
@@ -621,6 +592,20 @@
             copy.wait_send()
 
     return start, relay, share, arrive, drain
+
+
+def loop_with(first, last, body, works):
+    def one(i, c):
+        body(i)
+        for when, work in works:
+
+            @pl.when(i == when)
+            def _(work=work):
+                work()
+
+        return c
+
+    lax.fori_loop(first, last, one, 0)
 
 
 def masks(lens, first, count):
@@ -817,16 +802,11 @@
         (16, lambda: two[2][SHARE]()),
     ]
 
-    def beside(k):
-        for turn, work in turns:
-
-            @pl.when(k == turn)
-            def _(work=work):
-                work()
-
-    line_all_reduce(
-        t, seq, tp, rows, CHUNKS, partial, send, buf, (s_in, s_out, r_buf), finish, beside
+    count, turn, drain = line_all_reduce(
+        t, seq, tp, rows, CHUNKS, partial, send, buf, (s_in, s_out, r_buf), finish, (0, 1, 3)
     )
+    loop_with(0, count, turn, turns)
+    drain()
     for g in two:
         g[ARRIVE]()
     for g in one + two:
@@ -845,35 +825,86 @@
 
 
 def feed_forward(
-    nmid_h, cot_h, w2_h, gnm_h, glu_h, dw2_h,
-    nmid, cot, wg, wu, wd, hid, gg, gu, gnm, glu, stage,
-    s_w, s_a, s_o, s_d,
+    n, t, width,
+    nmid_h, cot_h, w2_h, x_h, mixed_h, invmid, consts,
+    gmix_h, gres_h, glu_h, ggain, sums_h, down_h,
+    nmid, cot, pool, hid, gg, gu, glu, xs, ms, gmix, gres, wide, sums, stage, send, buf,
+    s_a, s_w, s_x, s_o, s_g, s_s, s_d, m_core, ready, s_in, s_out, r_buf, *bufs,
 ):
-    rows, width = nmid.shape
-    ff = wg.shape[1]
-    tile = row_tile(rows)
+    seq, tp = lax.axis_index("seq"), lax.axis_index("tp")
+    core = lax.rem(seq, 2)
+    sibling = (seq + 1 - 2 * core, tp)
     act_copies = [
         pltpu.make_async_copy(nmid_h, nmid, s_a.at[0]),
         pltpu.make_async_copy(cot_h, cot, s_a.at[1]),
     ]
-    w_copies = [
-        pltpu.make_async_copy(w2_h.at[j], w, s_w.at[j])
-        for j, w in enumerate((wg, wu, wd))
-    ]
-    for copy in (act_copies[0], w_copies[0], w_copies[1], act_copies[1], w_copies[2]):
+    w_copies = [pltpu.make_async_copy(w2_h.at[j], pool.at[j], s_w.at[j]) for j in range(3)]
+    act_copies[0].start()
+    w_copies[0].start()
+    greet_all(n, t, seq, tp)
+    for copy in (w_copies[1], act_copies[1], w_copies[2]):
         copy.start()
+    rows, chan = nmid.shape[0], gres.shape[2]
+    step = rows // CHUNKS
+    tile = rows // TILES
+    ggain[...] = jnp.zeros_like(ggain)
+
+    def fetch(k):
+        at, slot = pl.ds(pl.multiple_of(k * step, step), step), lax.rem(k, 2)
+        return (
+            pltpu.make_async_copy(x_h.at[at], xs.at[slot], s_x.at[0, slot]),
+            pltpu.make_async_copy(mixed_h.at[at], ms.at[slot], s_x.at[1, slot]),
+        )
+
+    def stored(k):
+        at, slot = pl.ds(pl.multiple_of(k * step, step), step), lax.rem(k, 2)
+        return (
+            pltpu.make_async_copy(gmix.at[slot], gmix_h.at[at], s_o.at[0, slot]),
+            pltpu.make_async_copy(gres.at[slot], gres_h.at[at], s_o.at[1, slot]),
+        )
+
+    for copy in fetch(0):
+        copy.start()
+
+    def finish(k):
+        for copy in fetch(k):
+            copy.wait()
+
+        @pl.when(k + 1 < CHUNKS)
+        def _():
+            for copy in fetch(k + 1):
+                copy.start()
+
+        @pl.when(k >= 2)
+        def _():
+            for copy in stored(k - 2):
+                copy.wait()
+
+        at, slot = pl.ds(pl.multiple_of(k * step, step), step), lax.rem(k, 2)
+        g = buf[1, at, :].astype(F32)
+        inv = invmid[at, :]
+        hat = (xs[slot].astype(F32) + ms[slot].astype(F32)) * inv
+        ggain[0:1, :] += jnp.sum(g * hat, axis=0, keepdims=True)
+        e = g * consts[3:4, :]
+        mean = jnp.mean(e * hat, axis=-1, keepdims=True)
+        result = cot[at, :].astype(F32) + inv * (e - hat * mean)
+        wide[...] = result
+        gmix[slot] = result.astype(BF)
+        gres[slot] = wide[:, pl.ds(pl.multiple_of(tp * chan, LANE), chan)]
+        for copy in stored(k):
+            copy.start()
+
+    count, turn, drain = line_all_reduce(
+        t, seq, tp, rows, CHUNKS, None, send, buf, (s_in, s_out, r_buf), finish, K2_LAGS
+    )
+
     act_copies[0].wait()
     w_copies[0].wait()
-
-    def out_copy(i, which):
-        at = pl.ds(pl.multiple_of(i * tile, tile), tile)
-        if which == 0:
-            return pltpu.make_async_copy(gnm.at[at], gnm_h.at[at], s_o.at[0, i])
-        return pltpu.make_async_copy(glu.at[:, at], glu_h.at[:, at], s_o.at[1, i])
+    per = 2
 
     def block(i, c):
         at = pl.ds(pl.multiple_of(i * tile, tile), tile)
-        g = nn(nmid[at, :], wg[...])
+        g = nn(nmid[at, :], pool[0])
 
         @pl.when(i == 0)
         def _():
@@ -881,168 +912,163 @@
             act_copies[1].wait()
             w_copies[2].wait()
 
-        u = nn(nmid[at, :], wu[...])
-        gh = nn(cot[at, :], wd[...])
+        u = nn(nmid[at, :], pool[1])
+        gh = nn(cot[at, :], pool[2])
         sig = jax.nn.sigmoid(g)
         act = g * sig
         hid[at, :] = (act * u).astype(BF)
         gg[at, :] = (gh * u * (sig * (1.0 + g * (1.0 - sig)))).astype(BF)
         gu[at, :] = (gh * act).astype(BF)
-        gnm[at, :] = (nt(gg[at, :], wg[...]) + nt(gu[at, :], wu[...])).astype(BF)
-        out_copy(i, 0).start()
-        put_shards(glu, at, nt(hid[at, :], wd[...]).astype(BF))
-        out_copy(i, 1).start()
-        return c
-
-    lax.fori_loop(0, rows // tile, block, 0)
-
-    ga, gb, h = dw2_h.shape[2:5]
-    span = 4 * h
-    pieces = ga * gb
-
-    def d_copy(i, slot):
-        j = i // pieces
-        r = lax.rem(i, pieces)
-        return pltpu.make_async_copy(
-            stage.at[slot],
-            dw2_h.at[:, :, r // gb, lax.rem(r, gb), :, pl.ds(pl.multiple_of(j * ff, LANE), ff)],
-            s_d.at[slot],
+
+        @pl.when(i > 0)
+        def _():
+            turn((i - 1) * per)
+
+        send[at, :] = (nt(gg[at, :], pool[0]) + nt(gu[at, :], pool[1])).astype(BF)
+
+        @pl.when(i > 0)
+        def _():
+            turn((i - 1) * per + 1)
+
+        return c
+
+    lax.fori_loop(0, TILES, block, 0)
+    done = (TILES - 1) * per
+
+    ga, gb = chip_grid(n)
+    chips = ga * gb
+    shard = width // n
+    half_pool = pl.ds(0, width // 2)
+    other_half = pl.ds(width // 2, width // 2)
+
+    def give(i):
+        j, r = i // chips, lax.rem(i, chips)
+        return pltpu.make_async_remote_copy(
+            src_ref=stage.at[lax.rem(i, 2), 1 - core],
+            dst_ref=pool.at[j, pl.ds(pl.multiple_of(width // 2 + r * shard, shard), shard)],
+            send_sem=s_g.at[lax.rem(i, 2)],
+            recv_sem=m_core.at[i],
+            device_id=sibling,
+            device_id_type=MESH,
         )
 
-    for j, (left, right) in enumerate(((nmid, gg), (nmid, gu), (cot, hid))):
-
-        def slab(r, c, j=j, left=left, right=right):
-            i = j * pieces + r
+    def gradient(j, left, right, first_turn, turns):
+        pl.semaphore_signal(ready, inc=1, device_id=sibling, device_id_type=MESH)
+        pl.semaphore_wait(ready, 1)
+
+        def slab(r, c):
+            i = j * chips + r
             slot = lax.rem(i, 2)
 
             @pl.when(i >= 2)
             def _():
-                d_copy(i - 2, slot).wait()
-
-            at = pl.ds(pl.multiple_of(r * span, span), span)
-            put_blocks(stage.at[slot], h, tn(left[:, at], right[...]))
-            d_copy(i, slot).start()
+                give(i - 2).wait_send()
+
+            at = pl.ds(pl.multiple_of(r * 2 * shard, 2 * shard), 2 * shard)
+            values = tn(left[:, at], right[...]).astype(BF)
+            for k in range(2):
+                stage[slot, k] = values[k * shard : (k + 1) * shard]
+            give(i).start()
+            pool[j, pl.ds(pl.multiple_of(r * shard, shard), shard), :] = stage[slot, core]
+            loop_with(first_turn + r * turns // chips, first_turn + (r + 1) * turns // chips, turn, ())
             return c
 
-        lax.fori_loop(0, pieces, slab, 0)
-    d_copy(3 * pieces - 2, (3 * pieces) % 2).wait()
-    d_copy(3 * pieces - 1, (3 * pieces + 1) % 2).wait()
-
-    def drain(i, c):
-        out_copy(i, 0).wait()
-        out_copy(i, 1).wait()
-        return c
-
-    lax.fori_loop(0, rows // tile, drain, 0)
-
-
-def mid_backward(
-    n, t, width,
-    gnm_h, dw2_h, x_h, mixed_h, cot_h, invmid, consts,
-    gmix_h, gres_h, ggain, sums_h,
-    x, mixed, cot, gmix, gres, sums, send, buf, wide, s_g, s_x, s_o, s_s, s_in, s_out, r_buf, *bufs,
-):
-    seq, tp = lax.axis_index("seq"), lax.axis_index("tp")
-    load = pltpu.make_async_copy(gnm_h, send, s_g)
-    load.start()
-    fetches = [
-        pltpu.make_async_copy(src, dst, s_x.at[i])
-        for i, (src, dst) in enumerate(((x_h, x), (mixed_h, mixed), (cot_h, cot)))
+        lax.fori_loop(0, chips, slab, 0)
+
+    def cores(j):
+        def arrived(r, c):
+            give(j * chips + r).wait_recv()
+            return c
+
+        lax.fori_loop(0, chips, arrived, 0)
+        add_cores(pool.at[j, half_pool], pool.at[j, other_half])
+
+    def summed(j):
+        return pltpu.make_async_copy(sums, sums_h.at[j], s_s.at[j])
+
+    def out(half, values):
+        sums[half * (shard // 2) : (half + 1) * (shard // 2), :] = values
+
+    reduces = [
+        grid_reduce(n, seq, tp, j, pool.at[j, half_pool], bufs, out) for j in range(2)
     ]
-    greet_all(n, t, seq, tp)
-    rows = x.shape[0]
-    chan = gres.shape[1]
-    step = rows // CHUNKS
-    pieces, shard, cols = sums.shape
-    ggain[...] = jnp.zeros_like(ggain)
-
-    def out(j, half, values):
-        sums[j, half * (shard // 2) : (half + 1) * (shard // 2), :] = values
-
-    start, stage1, stage2, stage3, drain = grid_reduce(n, seq, tp, dw2_h, pieces, cols, bufs, out)
-    load.wait()
-    start(0)
-    for copy in fetches:
-        copy.start()
-
-    def summed(j):
-        return pltpu.make_async_copy(sums.at[j], sums_h.at[j], s_s.at[j])
-
-    def stored(k):
-        at = pl.ds(pl.multiple_of(k * step, step), step)
-        return (
-            pltpu.make_async_copy(gmix.at[at], gmix_h.at[at], s_o.at[0, k]),
-            pltpu.make_async_copy(gres.at[at], gres_h.at[at], s_o.at[1, k]),
-        )
-
-    def partial(k):
-        at = pl.ds(pl.multiple_of(k * step, step), step)
-        return send[at, :].astype(F32)
-
-    def finish(k):
-        @pl.when(k == 0)
-        def _():
-            for copy in fetches:
-                copy.wait()
-
-        at = pl.ds(pl.multiple_of(k * step, step), step)
-        g = buf[1, at, :].astype(F32)
-        inv = invmid[at, :]
-        hat = (x[at, :].astype(F32) + mixed[at, :].astype(F32)) * inv
-        ggain[0:1, :] += jnp.sum(g * hat, axis=0, keepdims=True)
-        e = g * consts[3:4, :]
-        mean = jnp.mean(e * hat, axis=-1, keepdims=True)
-        result = cot[at, :].astype(F32) + inv * (e - hat * mean)
-        wide[...] = result
-        gmix[at, :] = result.astype(BF)
-        gres[at, :] = wide[:, pl.ds(pl.multiple_of(tp * chan, LANE), chan)]
-        for copy in stored(k):
-            copy.start()
-
-    turns = [
-        (1, lambda: (stage1(0), start(1))),
-        (4, lambda: (stage1(1), start(2))),
-        (5, lambda: stage2(0)),
-        (8, lambda: stage1(2)),
-        (9, lambda: (stage3(0), summed(0).start())),
-        (10, lambda: stage2(1)),
-        (13, lambda: (stage3(1), summed(1).start())),
-        (14, lambda: stage2(2)),
-        (17, lambda: (stage3(2), summed(2).start())),
-    ]
-
-    def beside(k):
-        for turn, work in turns:
-
-            @pl.when(k == turn)
-            def _(work=work):
-                work()
-
-    line_all_reduce(
-        t, seq, tp, rows, CHUNKS, partial, send, buf, (s_in, s_out, r_buf), finish, beside
+    gradient(0, nmid, gg, done, 2)
+    cores(0)
+    reduces[0][0]()
+    gradient(1, nmid, gu, done + 2, 2)
+    cores(1)
+    reduces[1][0]()
+
+    def glu_copy(i):
+        at, slot = pl.ds(pl.multiple_of(i * tile, tile), tile), lax.rem(i, 2)
+        return pltpu.make_async_copy(glu.at[slot], glu_h.at[:, at], s_d.at[slot])
+
+    def forward(i, c):
+        @pl.when(i >= 2)
+        def _():
+            glu_copy(i - 2).wait()
+
+        at, slot = pl.ds(pl.multiple_of(i * tile, tile), tile), lax.rem(i, 2)
+        values = nt(hid[at, :], pool[2]).astype(BF)
+        for q in range(t):
+            glu[slot, q] = values[:, q * chan : (q + 1) * chan]
+        glu_copy(i).start()
+
+        @pl.when(lax.rem(i, 2) == 1)
+        def _():
+            turn(done + 4 + i // 2)
+
+        return c
+
+    lax.fori_loop(0, TILES, forward, 0)
+    glu_copy(TILES - 2).wait()
+    glu_copy(TILES - 1).wait()
+    reduces[0][1]()
+    gradient(2, cot, hid, done + 4 + TILES // 2, 2)
+    cores(2)
+    down = pltpu.make_async_copy(pool.at[2, half_pool], down_h, s_s.at[2])
+    down.start()
+
+    def second_sum():
+        summed(0).wait()
+        reduces[1][2]()
+        summed(1).start()
+
+    now = done + 6 + TILES // 2
+    loop_with(
+        now,
+        count,
+        turn,
+        (
+            (now + 1, lambda: (reduces[0][2](), summed(0).start())),
+            (now + 2, lambda: reduces[1][1]()),
+            (now + 5, second_sum),
+        ),
     )
     drain()
-    for j in range(pieces):
-        summed(j).wait()
-
-    def ended(k, c):
+    for r in reduces:
+        r[3]()
+    give(3 * chips - 2).wait_send()
+    give(3 * chips - 1).wait_send()
+    summed(1).wait()
+    down.wait()
+    for k in (CHUNKS - 2, CHUNKS - 1):
         for copy in stored(k):
             copy.wait()
-        return c
-
-    lax.fori_loop(0, CHUNKS, ended, 0)
 
 
 def mixer_backward(
     n, t, width,
     lens, glu_h, x_h, mixed_h, gmix_h, normed_h, w1_h, gated_h, states_h, feff_h, ipre_h, fpre_h, opre_h,
-    invst, consts,
-    gni_h, dw1_h, vecs, out,
-    gmix, normed, w1, gated, states, feff, ipre, fpre, opre,
+    down_h, invst, consts,
+    gni_h, dw1_h, vecs, out, sums,
+    acc, gmix, normed, w1, gated, states, feff, ipre, fpre, opre,
     weighted, prod, inner, out3, cslots, zslots, xc, mc, own, inbox, gni, stage,
-    s_f, cs, cr, zs, zr, s_x, sr, rr, sl, rl, s_o, s_d,
+    s_f, cs, cr, zs, zr, s_x, sr, rr, sl, rl, s_o, s_d, s_acc, *bufs,
 ):
     seq, tp = lax.axis_index("seq"), lax.axis_index("tp")
+    down = pltpu.make_async_copy(down_h, acc, s_acc)
+    down.start()
     rows = gmix.shape[0]
     chan = ipre.shape[1]
     mine = pl.ds(pl.multiple_of(tp * chan, LANE), chan)
@@ -1065,6 +1091,14 @@
     greet_all(n, t, seq, tp)
     for copy in fetches[1:] + inputs[4:]:
         copy.start()
+
+    def down_out(half, values):
+        size = sums.shape[0] // 2
+        sums[half * size : (half + 1) * size, :] = values
+
+    far, middle, near, drain_grid = grid_reduce(n, seq, tp, 0, acc, bufs, down_out)
+    down.wait()
+    far()
     tile = row_tile(rows)
     sgain, bound = consts[1:2, mine], consts[2:3, mine]
     vecs[...] = jnp.zeros_like(vecs)
@@ -1150,6 +1184,7 @@
     )
     inputs[5].wait()
     inputs[6].wait()
+    middle()
     bias_sum = jnp.zeros((1, chan), F32)
     for s in range(SEG - 1, -1, -1):
         pump(12 - s)
@@ -1186,13 +1221,17 @@
 
     lax.fori_loop(0, 3, spread_in, 0)
 
-    ga, gb, h = dw1_h.shape[2:5]
-    span = 4 * h
+    near()
+    shard = width // n
+    chips = n // 2
 
     def d_copy(r, slot):
-        return pltpu.make_async_copy(
-            stage.at[slot], dw1_h.at[:, :, r // gb, lax.rem(r, gb)], s_d.at[slot]
-        )
+        at = pl.ds(pl.multiple_of(r * shard, shard), shard)
+        return pltpu.make_async_copy(stage.at[slot], dw1_h.at[:, at], s_d.at[slot])
+
+    def keep(slot, first, values):
+        for k in range(2):
+            stage[slot, k, :, first : first + values.shape[1]] = values[k * shard : (k + 1) * shard]
 
     def slab(r, c):
         slot = lax.rem(r, 2)
@@ -1201,9 +1240,9 @@
         def _():
             d_copy(r - 2, slot).wait()
 
-        at = pl.ds(pl.multiple_of(r * span, span), span)
-        put_blocks(stage.at[slot, :, :, :, pl.ds(0, 3 * chan)], h, tn(normed[:, at], out3[...]))
-        put_blocks(stage.at[slot, :, :, :, pl.ds(3 * chan, chan)], h, tn(gmix[:, at], gated[...]))
+        at = pl.ds(pl.multiple_of(r * 2 * shard, 2 * shard), 2 * shard)
+        keep(slot, 0, tn(normed[:, at], out3[...]).astype(BF))
+        keep(slot, 3 * chan, tn(gmix[:, at], gated[...]).astype(BF))
         d_copy(r, slot).start()
 
         @pl.when(r < 4)
@@ -1212,8 +1251,8 @@
 
         return c
 
-    lax.fori_loop(0, ga * gb, slab, 0)
-    for r in range(ga * gb, 4):
+    lax.fori_loop(0, chips, slab, 0)
+    for r in range(chips, 4):
         pump(16 + r)
     for copy in fetches[1:]:
         copy.wait()
@@ -1223,7 +1262,7 @@
         return c
 
     lax.fori_loop(0, SHARD_CHUNKS, ending, 0)
-    for r in range(max(ga * gb - 2, 0), ga * gb):
+    for r in range(max(chips - 2, 0), chips):
         d_copy(r, r % 2).wait()
 
     def stored(i, c):
@@ -1232,14 +1271,15 @@
 
     lax.fori_loop(0, 3, stored, 0)
     drain()
+    drain_grid()
 
 
 def closing(
     n, t, width,
     gni_h, dw1_h, x_h, gres_h, invin, consts, vecs, ggain,
     gin, allvec, sums,
-    xc, gres, own, inbox, scaled, inner, zslots, vslots,
-    s_own, s_x, sr, rr, sl, rl, zs, zr, vs, vr, ts, tr, *bufs,
+    acc, other, xc, gres, own, inbox, scaled, inner, zslots, vslots,
+    s_acc, m_core, s_own, s_x, sr, rr, sl, rl, zs, zr, vs, vr, ts, tr, *bufs,
 ):
     seq, tp = lax.axis_index("seq"), lax.axis_index("tp")
     rows, chan = gres.shape
@@ -1253,12 +1293,47 @@
     greet_all(n, t, seq, tp)
     pieces, shard, cols = sums.shape
 
-    def out(j, half, values):
-        sums[j, half * (shard // 2) : (half + 1) * (shard // 2), :] = values
-
-    start, stage1, stage2, stage3, drain_grid = grid_reduce(
-        n, seq, tp, dw1_h, pieces, cols, bufs, out
-    )
+    core = lax.rem(seq, 2)
+
+    def load(j):
+        return pltpu.make_async_copy(
+            dw1_h.at[core, :, pl.ds(j * cols, cols)], acc.at[j], s_acc.at[j]
+        )
+
+    def swap(j):
+        return pltpu.make_async_remote_copy(
+            src_ref=dw1_h.at[1 - core, :, pl.ds(j * cols, cols)],
+            dst_ref=other.at[j],
+            send_sem=m_core.at[0, j],
+            recv_sem=m_core.at[1, j],
+            device_id=(seq + 1 - 2 * core, tp),
+            device_id_type=MESH,
+        )
+
+    def start(j):
+        load(j).start()
+        swap(j).start()
+
+    reduces = []
+    for j in range(pieces):
+
+        def out(half, values, j=j):
+            sums[j, half * (shard // 2) : (half + 1) * (shard // 2), :] = values
+
+        reduces.append(grid_reduce(n, seq, tp, j, acc.at[j], bufs, out))
+
+    def stage1(j):
+        load(j).wait()
+        swap(j).wait_recv()
+        add_cores(acc.at[j], other.at[j])
+        reduces[j][0]()
+
+    def stage2(j):
+        reduces[j][1]()
+
+    def stage3(j):
+        reduces[j][2]()
+
     fetch.wait()
     start(0)
     for copy in fetches:
@@ -1287,21 +1362,14 @@
     ]
     slots = 16
 
-    def turn_of(slot, c):
+    def turn_of(slot):
         def one(i, c):
             turn(i)
             return c
 
         lax.fori_loop(slot * turns // slots, (slot + 1) * turns // slots, one, 0)
-        for when, work in works:
-
-            @pl.when(slot == when)
-            def _(work=work):
-                work()
-
-        return c
-
-    lax.fori_loop(0, slots, turn_of, 0)
+
+    loop_with(0, slots, turn_of, works)
     for copy in fetches:
         copy.wait()
 
@@ -1322,7 +1390,9 @@
     gin[...] = gres[...] + invin[...] * (scaled[...] - xc[...].astype(F32) * invin[...] * dot)
     done_t()
     drain()
-    drain_grid()
+    for j in range(pieces):
+        swap(j).wait_send()
+        reduces[j][3]()
 
 
 def params(collective=None, limit=VMEM_LIMIT):
@@ -1367,8 +1437,6 @@
     column = shape((rows, 1), F32)
     wide16 = shape((rows, width), BF)
     shards16 = shape((t, rows, chan), BF)
-    ga, gb = chip_grid(n)
-    h = width // n // 2
 
     def groups(more=0):
         return shape((chan // LANE, rows + more, LANE), F32)
@@ -1410,51 +1478,50 @@
         padded(w_gate), padded(w_up), padded(w_down.T), consts,
     )
 
-    gnm_part, glu_part, dw2 = pl.pallas_call(
-        feed_forward,
-        out_shape=[wide16, shards16, shape((2, 2, ga, gb, h, 3 * ffp), BF)],
-        in_specs=[HB] * 3,
-        out_specs=[HB] * 3,
+    shard, chips, tile, step = width // n, n // 2, rows // TILES, rows // CHUNKS
+    piece = shape((shard, ffp), F32)
+    ffs = shape((rows, ffp), BF)
+    gmix, gres, glu_part, ggain, sums2, down = pl.pallas_call(
+        functools.partial(feed_forward, n, t, width),
+        out_shape=[
+            wide16, plane, shards16, shape((8, width), F32), shape((2, shard, ffp), F32),
+            shape((width // 2, ffp), BF),
+        ],
+        in_specs=[HB] * 5 + [VM] * 2,
+        out_specs=[HB] * 3 + [VM] + [HB] * 2,
         scratch_shapes=[
-            *vm(wide16, wide16),
-            *[pltpu.VMEM((width, ffp), BF)] * 3,
-            *[pltpu.VMEM((rows, ffp), BF)] * 3,
-            *vm(wide16, shards16),
-            pltpu.VMEM((2, 2, 2, h, ffp), BF),
-            DMA((3,)), DMA((2,)), DMA((2, 3)), DMA((2,)),
-        ],
-        compiler_params=params(),
-        name="feed_forward",
-    )(nmid, cotangent, w2)
-
-    sums2s = shape((3, 2 * h, ffp), F32)
-    gmix, gres, ggain, sums2 = pl.pallas_call(
-        functools.partial(mid_backward, n, t, width),
-        out_shape=[wide16, plane, shape((8, width), F32), sums2s],
-        in_specs=[HB] * 5 + [VM] * 2,
-        out_specs=[HB] * 2 + [VM, HB],
-        scratch_shapes=[
-            *vm(wide16, wide16, wide16, wide16, plane, sums2s, wide16),
+            *vm(wide16, wide16, w2s, ffs, ffs, ffs),
+            pltpu.VMEM((2, t, tile, chan), BF),
+            pltpu.VMEM((2, step, width), BF),
+            pltpu.VMEM((2, step, width), BF),
+            pltpu.VMEM((2, step, width), BF),
+            pltpu.VMEM((2, step, chan), F32),
+            pltpu.VMEM((step, width), F32),
+            *vm(piece),
+            pltpu.VMEM((2, 2, shard, ffp), BF),
+            *vm(wide16),
             pltpu.VMEM((2, rows, width), BF),
-            pltpu.VMEM((rows // CHUNKS, width), F32),
-            DMA, DMA((3,)), DMA((2, CHUNKS)), DMA((3,)),
+            DMA((2,)), DMA((3,)), DMA((2, 2)), DMA((2, 2)), DMA((2,)), DMA((3,)), DMA((2,)),
+            DMA((3 * chips,)),
+            pltpu.SemaphoreType.REGULAR,
             *line_sems(CHUNKS),
-            *grid_buffers(n, width, 3, ffp),
+            *grid_buffers(n, width, 2, ffp),
         ],
         compiler_params=params(2),
-        name="mid_backward",
-    )(gnm_part, dw2, hidden_in, mixed, cotangent, invmid, consts)
+        name="feed_forward",
+    )(nmid, cotangent, w2, hidden_in, mixed, invmid, consts)
 
     shard_sems = [DMA((t, SHARD_CHUNKS))] * 4
     shard_bufs = [pltpu.VMEM((t, rows, chan), BF), pltpu.VMEM((t + 1, rows, chan), BF)]
-    gni_part, dw1, vecs, block_out = pl.pallas_call(
+    gni_part, dw1, vecs, block_out, sum_down = pl.pallas_call(
         functools.partial(mixer_backward, n, t, width),
         out_shape=[
-            shards16, shape((2, 2, ga, gb, h, 4 * chan), BF), shape((8, chan), F32), plane16,
+            shards16, shape((2, width // 2, 4 * chan), BF), shape((8, chan), F32), plane16, piece,
         ],
-        in_specs=[SM] + [HB] * 12 + [VM] * 2,
-        out_specs=[HB] * 2 + [VM] * 2,
+        in_specs=[SM] + [HB] * 13 + [VM] * 2,
+        out_specs=[HB] * 2 + [VM] * 3,
         scratch_shapes=[
+            pltpu.VMEM((width // 2, ffp), BF),
             *vm(wide16, wide16),
             pltpu.VMEM((width, 4 * chan), BF),
             *vm(plane16, groups(8), groups(8), plane, plane, plane),
@@ -1464,32 +1531,35 @@
             *vm(plane16, plane16),
             *shard_bufs,
             *vm(shards16),
-            pltpu.VMEM((2, 2, 2, h, 4 * chan), BF),
+            pltpu.VMEM((2, 2, shard, 4 * chan), BF),
             DMA((12,)),
             *small,
             DMA((3,)),
             *shard_sems,
-            DMA((3,)), DMA((2,)),
+            DMA((3,)), DMA((2,)), DMA,
+            *grid_buffers(n, width, 1, ffp),
         ],
         compiler_params=params(3),
         name="mixer_backward",
     )(
         lengths, glu_part, hidden_in, mixed, gmix, normed_in, w1, gated, states, feff, ipre, fpre, opre,
-        invst, consts,
+        down, invst, consts,
     )
 
     grad_in, allvec, sums1 = pl.pallas_call(
         functools.partial(closing, n, t, width),
-        out_shape=[plane, shape((t, 8, chan), F32), shape((2, 2 * h, 2 * chan), F32)],
+        out_shape=[plane, shape((t, 8, chan), F32), shape((2, shard, 2 * chan), F32)],
         in_specs=[HB] * 4 + [VM] * 4,
         out_specs=[VM] * 3,
         scratch_shapes=[
+            pltpu.VMEM((2, width // 2, 2 * chan), BF),
+            pltpu.VMEM((2, width // 2, 2 * chan), BF),
             *vm(plane16, plane),
             *shard_bufs,
             *vm(plane, plane),
             zslot,
             vslot,
-            DMA, DMA((2,)),
+            DMA((2,)), DMA((2, 2)), DMA, DMA((2,)),
             *shard_sems,
             DMA((t,)), DMA((t,)), DMA((n,)), DMA((n,)), DMA((t,)), DMA((t,)),
             *grid_buffers(n, width, 2, 2 * chan),
@@ -1517,7 +1587,7 @@
         vector(3),
         sums2[0, :, :ff],
         sums2[1, :, :ff],
-        sums2[2, :, :ff].T,
+        sum_down[:, :ff].T,
         rms_stats,
     )
 

time: 456 us -> 416 us (0.912)
  Pallas kernels: 427 us -> 388 us
    pallas_call x2 -> x1, Pallas kernels: 152 us -> 111 us  [on_device(): pl.pallas_call(functools.partial(feed_forward, n, t, width), out_shape=[w...]
    unnamed x10 -> x14, local copies, waits for them, and re-layouts: 9.78 us -> 10.8 us
where the time goes in v4:
time: 416 us; the launch traced here: 415 us
  Pallas kernels  388 us (93%)
  local copies, waits for them, and re-layouts  17.3 us (4%)
  other arithmetic  7.02 us (2%)
    pallas_call x1, Pallas kernels, on_device(): pl.pallas_call(functools.partial(mixer_forward, n, t, width), out_shape=s...  135 us
    pallas_call x1, Pallas kernels, on_device(): pl.pallas_call(functools.partial(feed_forward, n, t, width), out_shape=[w...  111 us
    pallas_call x1, Pallas kernels, on_device(): pl.pallas_call(functools.partial(closing, n, t, width), out_shape=[plane,...  71.5 us
    pallas_call x1, Pallas kernels, on_device(): pl.pallas_call(functools.partial(mixer_backward, n, t, width), out_shape=...  71.1 us
    unnamed x14, local copies, waits for them, and re-layouts  10.8 us

profile of v4, /device:TPU:0, one launch (start us, length us, event | category | flops | bytes accessed | tf_op | source)
XLA Modules:
  0.0 415.3 jit_solution(7589447382780291965)
XLA Ops:
  1.3 0.7 stack.52
  2.0 0.7 stack.53
  2.7 0.7 stack.54
  3.4 1.4 stack.47.consts
  4.8 2.2 copy.30
  7.0 1.8 copy.29
  8.8 134.5 %mixer_forward.1 = (f32[768,512]{1,0:T(8,128)}, f32[768,512]{1,0:T(8,128)}, f32[768,512]{1,0:T(8,128)}, f32[4,776,128]{2,1,0:T(8,128)}, f32[4,776,128]{2,1,0:T(8...) custom-call(s32[2]{0:T(128)} %lens.3, ...), custom_call_target="tpu_custom_call" | custom-call | tf_op jit(solution)/shard_map/mixer_forward/pallas_call | solution.py:1455
  143.4 111.3 %feed_forward.1 = (bf16[768,2048]{1,0:T(8,128)(2,1)}, f32[768,512]{1,0:T(8,128)}, bf16[4,768,512]{2,1,0:T(8,128)(2,1)}, f32[8,2048]{1,0:T(8,128)}, f32[2,256,1408]{2,1,0:T(8,128)}, /*index=5*/bf16[1024,1408]{1,0:T(8,128)(2,1)}) custom-call(bf16[768,2048]{1,0:T(8,128)(2,1)} %get-tuple-element.42.nmid_h, bf16[768,2048]{1,0:T(8,128)(2,1)} %cot_h.1, ...), custom_call_target="tpu_custom_call" | custom-call | tf_op jit(solution)/shard_map/feed_forward/pallas_call | solution.py:1484
  254.7 71.1 %mixer_backward.1 = (bf16[4,768,512]{2,1,0:T(8,128)(2,1)}, bf16[2,1024,2048]{2,1,0:T(8,128)(2,1)}, f32[8,512]{1,0:T(8,128)}, bf16[768,512]{1,0:T(8,128)(2,1)}, f32[256,1408]{1,0:T(8,128)}) custom-call(s32[2]{0:T(128)} %lens.3, bf16[4,768,512]{2,1,0:T(8,128)(2,1)} %get-tuple-element.46.glu_h, bf16[768,2048]{1,0:T(8,128)(2,1)} %x_h.7, ...), custom_call_target="tpu_custom_call" | custom-call | tf_op jit(solution)/shard_map/mixer_backward/pallas_call | solution.py:1516
  325.8 0.0 copy-start.3
  325.8 71.5 %closing.1 = (f32[768,512]{1,0:T(8,128)}, f32[4,8,512]{2,1,0:T(8,128)}, f32[2,256,1024]{2,1,0:T(8,128)}) custom-call(bf16[4,768,512]{2,1,0:T(8,128)(2,1)} %get-tuple-element.59.gni_h, bf16[2,1024,2048]{2,1,0:T(8,128)(2,1)} %get-tuple-element.60.dw1_h, bf16[768,2048]{1,0:T(8,128)(2,1)} %x_h.7, f32[768,512]{1,0:T(8,128)} %get-tuple-element.61.gres_h, ...), custom_call_target="tpu_custom_call" | custom-call | tf_op jit(solution)/shard_map/closing/pallas_call | solution.py:1549
  397.2 2.4 slice_reduce_fusion.2
  399.7 0.0 copy-done.3
  399.7 0.6 fusion.1
  401.5 2.5 fusion
  404.1 2.7 slice_bitcast_fusion.2
  406.8 0.0 copy-start
  406.8 1.0 copy.31
  407.8 3.0 copy.32
  410.7 0.0 copy-done
  410.7 0.0 copy-start.2
  410.7 1.8 slice_bitcast_fusion
  412.5 0.0 copy-start.1
  412.5 0.0 copy-done.2
  412.5 0.9 copy.36
  413.4 0.8 copy-done.1
  414.2 1.1 copy.37
  (3 shorter events, 0.0 us)
Async XLA Ops:
  325.8 73.9 %copy-start.3 = (s32[2]{0:T(128)S(1)}, s32[2]{0:T(128)}, u32[]{:S(2)}) copy-start(s32[2]{0:T(128)} %lens.3) | copy-start | bytes 28
  406.8 4.0 copy-start
  410.7 1.8 copy-start.2
  412.5 1.7 copy-start.1

commit v5 on v4

--- a/solution.py
+++ b/solution.py
@@ -18,7 +18,7 @@
 LANE = 128
 SEG = 8
 TILES = 4
-K2_LAGS = (2, 2, 3)
+K2_LAGS = (1, 2, 3)
 CHUNKS = 16
 SHARD_CHUNKS = 4
 HOP_LAG = 2
@@ -617,23 +617,25 @@
 
 def mixer_forward(
     n, t, width,
-    lens, x_h, wi_h, wf_h, wo_h, wx_h, wg_h, wu_h, wd_h, consts,
+    lens, layer, x_h, wi_h, wf_h, wo_h, wx_raw, wg_h, wu_h, wd_raw_h, bias_v, sgain_v, gmid_v, gin_v,
     ipre_h, fpre_h, opre_h, feff_h, states_h, gated_h, normed_h, nmid_h, mixed_h, w1_h, w2_h,
-    invst, invmid, invin,
+    invst, invmid, invin, consts,
     x, normed, ipre, fpre, opre, feff, states, gated, nmid, w1, prod, ssq, part, cslots, zslots, send, buf,
-    s_x, s_st, s_w, s_n, s_m, cs, cr, zs, zr, s_in, s_out, r_buf, *sems,
+    wx, wd, wd_raw, s_t, s_x, s_st, s_w, s_n, s_m, cs, cr, zs, zr, s_in, s_out, r_buf, *sems,
 ):
     seq, tp = lax.axis_index("seq"), lax.axis_index("tp")
     load = pltpu.make_async_copy(x_h, x, s_x)
     load.start()
+    load_down = pltpu.make_async_copy(wd_raw_h, wd_raw, s_t)
+    load_down.start()
     sems1, sems2 = sems[:6], sems[6:]
     one = [
         grid_gather(n, seq, tp, j, src, w1.at[j], sems1)
-        for j, src in enumerate((wi_h, wf_h, wo_h, wx_h))
+        for j, src in enumerate((wi_h, wf_h, wo_h, wx))
     ]
     two = [
         grid_gather(n, seq, tp, j, src, w2_h.at[j], sems2)
-        for j, src in enumerate((wg_h, wu_h, wd_h))
+        for j, src in enumerate((wg_h, wu_h, wd))
     ]
     START, RELAY, SHARE, ARRIVE, DRAIN = range(5)
     greet_all(n, t, seq, tp)
@@ -642,6 +644,10 @@
     chan = ipre.shape[1]
     tile = row_tile(rows)
     mine = pl.ds(pl.multiple_of(tp * chan, LANE), chan)
+    consts[...] = jnp.zeros_like(consts)
+    for k, vector in ((0, bias_v), (1, sgain_v), (3, gmid_v), (4, gin_v)):
+        consts[k : k + 1, :] = vector[...].astype(F32).reshape(1, width)
+    consts[2:3, :] = jnp.full((1, width), layer[0].astype(F32) / LAYERS)
     bias, sgain, bound = consts[0:1, mine], consts[1:2, mine], consts[2:3, mine]
 
     def stores():
@@ -654,6 +660,7 @@
     def keep(j):
         return pltpu.make_async_copy(w1.at[j], w1_h.at[j], s_w.at[j])
 
+    wx[...] = jnp.transpose(wx_raw[...])
     load.wait()
 
     def norm(i, c):
@@ -667,6 +674,11 @@
     lax.fori_loop(0, rows // tile, norm, 0)
     one[0][RELAY]()
     one[1][START]()
+    load_down.wait()
+    turned = jnp.transpose(wd_raw[...])
+    wd[:, : turned.shape[1]] = turned
+    if turned.shape[1] < wd.shape[1]:
+        wd[:, turned.shape[1] :] = jnp.zeros((wd.shape[0], wd.shape[1] - turned.shape[1]), BF)
     one[0][SHARE]()
     one[1][RELAY]()
     one[2][START]()
@@ -827,7 +839,7 @@
 def feed_forward(
     n, t, width,
     nmid_h, cot_h, w2_h, x_h, mixed_h, invmid, consts,
-    gmix_h, gres_h, glu_h, ggain, sums_h, down_h,
+    gmix_h, gres_h, glu_h, ggain, gate_h, up_h, down_h,
     nmid, cot, pool, hid, gg, gu, glu, xs, ms, gmix, gres, wide, sums, stage, send, buf,
     s_a, s_w, s_x, s_o, s_g, s_s, s_d, m_core, ready, s_in, s_out, r_buf, *bufs,
 ):
@@ -900,7 +912,6 @@
 
     act_copies[0].wait()
     w_copies[0].wait()
-    per = 2
 
     def block(i, c):
         at = pl.ds(pl.multiple_of(i * tile, tile), tile)
@@ -922,18 +933,14 @@
 
         @pl.when(i > 0)
         def _():
-            turn((i - 1) * per)
+            turn(2 * i - 1)
 
         send[at, :] = (nt(gg[at, :], pool[0]) + nt(gu[at, :], pool[1])).astype(BF)
-
-        @pl.when(i > 0)
-        def _():
-            turn((i - 1) * per + 1)
-
+        turn(2 * i)
         return c
 
     lax.fori_loop(0, TILES, block, 0)
-    done = (TILES - 1) * per
+    done = 2 * TILES - 1
 
     ga, gb = chip_grid(n)
     chips = ga * gb
@@ -984,7 +991,7 @@
         add_cores(pool.at[j, half_pool], pool.at[j, other_half])
 
     def summed(j):
-        return pltpu.make_async_copy(sums, sums_h.at[j], s_s.at[j])
+        return pltpu.make_async_copy(sums, (gate_h, up_h)[j], s_s.at[j])
 
     def out(half, values):
         sums[half * (shard // 2) : (half + 1) * (shard // 2), :] = values
@@ -1060,11 +1067,11 @@
 def mixer_backward(
     n, t, width,
     lens, glu_h, x_h, mixed_h, gmix_h, normed_h, w1_h, gated_h, states_h, feff_h, ipre_h, fpre_h, opre_h,
-    down_h, invst, consts,
-    gni_h, dw1_h, vecs, out, sums,
+    down_h, invst, invin, consts,
+    gni_h, dw1_h, vecs, out, dot_in, sums,
     acc, gmix, normed, w1, gated, states, feff, ipre, fpre, opre,
-    weighted, prod, inner, out3, cslots, zslots, xc, mc, own, inbox, gni, stage,
-    s_f, cs, cr, zs, zr, s_x, sr, rr, sl, rl, s_o, s_d, s_acc, *bufs,
+    weighted, prod, inner, out3, cslots, zslots, zslots2, gain_sum, gsend, gtake, x, mc, own, inbox, gni, stage,
+    s_f, cs, cr, zs, zr, zs2, zr2, gs_, gr_, s_x, sr, rr, sl, rl, s_o, s_d, s_acc, *bufs,
 ):
     seq, tp = lax.axis_index("seq"), lax.axis_index("tp")
     down = pltpu.make_async_copy(down_h, acc, s_acc)
@@ -1074,7 +1081,7 @@
     mine = pl.ds(pl.multiple_of(tp * chan, LANE), chan)
     fetches = [
         pltpu.make_async_copy(glu_h, own, s_x.at[0]),
-        pltpu.make_async_copy(x_h.at[:, mine], xc, s_x.at[1]),
+        pltpu.make_async_copy(x_h, x, s_x.at[1]),
         pltpu.make_async_copy(mixed_h.at[:, mine], mc, s_x.at[2]),
     ]
     pairs = [
@@ -1089,16 +1096,14 @@
     for copy in inputs[:4]:
         copy.start()
     greet_all(n, t, seq, tp)
-    for copy in fetches[1:] + inputs[4:]:
+    for copy in inputs[4:] + fetches[1:]:
         copy.start()
 
     def down_out(half, values):
-        size = sums.shape[0] // 2
-        sums[half * size : (half + 1) * size, :] = values
+        size = sums.shape[1] // 2
+        sums[:, half * size : (half + 1) * size] = jnp.transpose(values)
 
     far, middle, near, drain_grid = grid_reduce(n, seq, tp, 0, acc, bufs, down_out)
-    down.wait()
-    far()
     tile = row_tile(rows)
     sgain, bound = consts[1:2, mine], consts[2:3, mine]
     vecs[...] = jnp.zeros_like(vecs)
@@ -1108,14 +1113,14 @@
         at = pl.ds(pl.multiple_of(k * step, step), step)
         ok, _ = masks(lens, seq * rows + k * step, step)
         m = mc[at, :].astype(F32)
-        full = xc[at, :].astype(F32) + m + values
+        full = x[at, mine].astype(F32) + m + values
         out[at, :] = full.astype(BF)
         vecs[4:5, :] += jnp.sum(ok * m * m, axis=0, keepdims=True)
         vecs[5:6, :] += jnp.sum(ok * values * values, axis=0, keepdims=True)
         vecs[6:7, :] += jnp.sum(ok * full * full, axis=0, keepdims=True)
 
     turns, turn, last, drain = line_reduce_scatter(t, seq, tp, own, inbox, (sr, rr, sl, rl), finish)
-    slots = 20
+    slots = 23
 
     def pump(slot):
         def one(i, c):
@@ -1125,11 +1130,15 @@
         lax.fori_loop(slot * turns // slots, (slot + 1) * turns // slots, one, 0)
 
     fetches[0].wait()
+    pump(0)
+    pump(1)
+    down.wait()
+    far()
     for copy in inputs[:4]:
         copy.wait()
 
     def gates(i, c):
-        pump(i)
+        pump(2 + i)
         at = pl.ds(pl.multiple_of(i * tile, tile), tile)
         shifted = pl.ds(pl.multiple_of(i * tile + 8, 8), tile)
         g = nn(gmix[at, :], w1[:, 3 * chan :])
@@ -1145,7 +1154,7 @@
         return c
 
     lax.fori_loop(0, 3, gates, 0)
-    dot = sum_over_tp(row_sums(inner[...]), t, seq, tp, zslots, zs, zr, lambda: pump(3)) / width
+    dot = sum_over_tp(row_sums(inner[...]), t, seq, tp, zslots, zs, zr, lambda: pump(5)) / width
     inner[:, 0:1] = dot
 
     def leaving(i, c):
@@ -1157,6 +1166,7 @@
 
     lax.fori_loop(0, 3, leaving, 0)
     inputs[4].wait()
+    pump(6)
 
     length = rows // SEG
 
@@ -1180,14 +1190,14 @@
         block_p = p[s : s + 1] * block_p
     first = get(feff, slice(0, 1))
     arriving = carry_over_seq(
-        first * block_p, first * block_h, n, seq, tp, cslots, cs, cr, True, lambda: pump(4)
+        first * block_p, first * block_h, n, seq, tp, cslots, cs, cr, True, lambda: pump(7)
     )
     inputs[5].wait()
     inputs[6].wait()
     middle()
     bias_sum = jnp.zeros((1, chan), F32)
     for s in range(SEG - 1, -1, -1):
-        pump(12 - s)
+        pump(15 - s)
         at = slice(s * length, (s + 1) * length)
         gs = get(weighted, at) + get(prod, at) * arriving
         arriving = h[s : s + 1] + p[s : s + 1] * arriving
@@ -1209,18 +1219,59 @@
         at = pl.ds(pl.multiple_of(i * tile, tile), tile)
         return pltpu.make_async_copy(gni.at[:, at], gni_h.at[:, at], s_o.at[i])
 
-    for copy in inputs[7:]:
+    for copy in inputs[7:] + fetches[1:]:
         copy.wait()
+    gain_sum[...] = jnp.zeros_like(gain_sum)
 
     def spread_in(i, c):
         at = pl.ds(pl.multiple_of(i * tile, tile), tile)
-        put_shards(gni, at, nt(out3[at, :], w1[:, : 3 * chan]).astype(BF))
+        values = nt(out3[at, :], w1[:, : 3 * chan])
+        put_shards(gni, at, values.astype(BF))
         gni_copy(i).start()
-        pump(13 + i)
+        product = values * (x[at, :].astype(F32) * invin[at, :])
+        gain_sum[0:1, :] += jnp.sum(product, axis=0, keepdims=True)
+        product = product * consts[4:5, :]
+        short = product[:, :LANE]
+        for k in range(LANE, width, LANE):
+            short = short + product[:, k : k + LANE]
+        inner[at, :LANE] = short
+        pump(16 + i)
         return c
 
     lax.fori_loop(0, 3, spread_in, 0)
 
+    zslots2[tp] = row_sums(inner[:, :LANE])
+    go_z, done_z = spread(t, tp, zslots2, zs2, zr2, lambda k: (seq, k))
+    go_z()
+    gsend[...] = jnp.zeros_like(gsend)
+    for q in range(t):
+        gsend[q, 0:1, :] = gain_sum[0:1, q * chan : (q + 1) * chan]
+
+    def gain_copy(o, slot):
+        to = lax.rem(tp + o, t)
+        return pltpu.make_async_remote_copy(
+            src_ref=gsend.at[to],
+            dst_ref=gtake.at[slot],
+            send_sem=gs_.at[o],
+            recv_sem=gr_.at[slot],
+            device_id=(seq, to),
+            device_id_type=MESH,
+        )
+
+    def gain_go(o, c):
+        gain_copy(o, tp).start()
+        return c
+
+    def gain_done(o, c):
+        gain_copy(o, lax.rem(tp + o, t)).wait_recv()
+        return c
+
+    def gain_sent(o, c):
+        gain_copy(o, tp).wait_send()
+        return c
+
+    lax.fori_loop(1, t, gain_go, 0)
+    gtake[tp] = gsend[tp]
     near()
     shard = width // n
     chips = n // 2
@@ -1247,15 +1298,25 @@
 
         @pl.when(r < 4)
         def _():
-            pump(16 + r)
+            pump(19 + r)
 
         return c
 
     lax.fori_loop(0, chips, slab, 0)
     for r in range(chips, 4):
-        pump(16 + r)
-    for copy in fetches[1:]:
-        copy.wait()
+        pump(19 + r)
+
+    done_z()
+    total = zslots2[0]
+    for k in range(1, t):
+        total = total + zslots2[k]
+    dot_in[...] = jnp.transpose(total)[:, :1] / width
+    lax.fori_loop(1, t, gain_done, 0)
+    lax.fori_loop(1, t, gain_sent, 0)
+    gains = gtake[0]
+    for k in range(1, t):
+        gains = gains + gtake[k]
+    vecs[0:1, :] = gains[0:1]
 
     def ending(k, c):
         last(k)
@@ -1276,10 +1337,10 @@
 
 def closing(
     n, t, width,
-    gni_h, dw1_h, x_h, gres_h, invin, consts, vecs, ggain,
-    gin, allvec, sums,
-    acc, other, xc, gres, own, inbox, scaled, inner, zslots, vslots,
-    s_acc, m_core, s_own, s_x, sr, rr, sl, rl, zs, zr, vs, vr, ts, tr, *bufs,
+    lens, gni_h, dw1_h, x_h, gres_h, invin, dot_in, consts, vecs, ggain,
+    gin, vectors, rms, g_input, g_forget, g_outgate, g_output,
+    acc, other, xc, gres, own, inbox, vslots, allvec,
+    s_acc, m_core, s_own, s_x, sr, rr, sl, rl, vs, vr, ts, tr, *bufs,
 ):
     seq, tp = lax.axis_index("seq"), lax.axis_index("tp")
     rows, chan = gres.shape
@@ -1291,7 +1352,7 @@
     ]
     fetch.start()
     greet_all(n, t, seq, tp)
-    pieces, shard, cols = sums.shape
+    pieces, shard, cols = 2, g_input.shape[0], 2 * chan
 
     core = lax.rem(seq, 2)
 
@@ -1318,7 +1379,13 @@
     for j in range(pieces):
 
         def out(half, values, j=j):
-            sums[j, half * (shard // 2) : (half + 1) * (shard // 2), :] = values
+            at = slice(half * (shard // 2), (half + 1) * (shard // 2))
+            if j == 0:
+                g_input[at, :] = values[:, :chan]
+                g_forget[at, :] = values[:, chan:]
+            else:
+                g_outgate[at, :] = values[:, :chan]
+                g_output[:, at] = jnp.transpose(values[:, chan:])
 
         reduces.append(grid_reduce(n, seq, tp, j, acc.at[j], bufs, out))
 
@@ -1342,17 +1409,28 @@
     gain_in = consts[4:5, mine]
     vslots[seq] = vecs[...]
     vslots[seq, 3:4, :] = ggain[0:1, mine]
+    go_v, done_v = spread(n, seq, vslots, vs, vr, lambda k: (k, tp))
+    go_t, done_t = spread(t, tp, allvec, ts, tr, lambda k: (seq, k))
+    go_v()
+    for copy in fetches:
+        copy.wait()
 
     def finish(k, values):
         at = pl.ds(pl.multiple_of(k * step, step), step)
         hat = xc[at, :].astype(F32) * invin[at, :]
-        s = values * gain_in
-        scaled[at, :] = s
-        inner[at, :] = s * hat
-        vslots[seq, 0:1, :] += jnp.sum(values * hat, axis=0, keepdims=True)
+        gin[at, :] = gres[at, :] + invin[at, :] * (values * gain_in - hat * dot_in[at, :])
+
+    def vectors_on():
+        done_v()
+        total = vslots[0]
+        for k in range(1, n):
+            total = total + vslots[k]
+        allvec[tp] = total
+        go_t()
 
     turns, turn, last, drain = line_reduce_scatter(t, seq, tp, own, inbox, (sr, rr, sl, rl), finish)
     works = [
+        (1, vectors_on),
         (2, lambda: (stage1(0), start(1))),
         (5, lambda: stage1(1)),
         (6, lambda: stage2(0)),
@@ -1370,29 +1448,49 @@
         lax.fori_loop(slot * turns // slots, (slot + 1) * turns // slots, one, 0)
 
     loop_with(0, slots, turn_of, works)
-    for copy in fetches:
-        copy.wait()
+    done_t()
+    squares = jnp.zeros((8, 1), F32)
+    for k in range(t):
+        vectors[:, k * chan : (k + 1) * chan] = allvec[k]
+        squares = squares + jnp.sum(allvec[k], axis=1, keepdims=True)
+    count = (lens[0] + lens[1]).astype(F32) * width
+    rms[...] = jnp.broadcast_to(jnp.sqrt(squares / count), rms.shape)
 
     def ending(k, c):
         last(k)
         return c
 
     lax.fori_loop(0, SHARD_CHUNKS, ending, 0)
-    go_v, done_v = spread(n, seq, vslots, vs, vr, lambda k: (k, tp))
-    dot = sum_over_tp(row_sums(inner[...]), t, seq, tp, zslots, zs, zr, go_v) / width
-    done_v()
-    total = vslots[0]
-    for k in range(1, n):
-        total = total + vslots[k]
-    allvec[tp] = total
-    go_t, done_t = spread(t, tp, allvec, ts, tr, lambda k: (seq, k))
-    go_t()
-    gin[...] = gres[...] + invin[...] * (scaled[...] - xc[...].astype(F32) * invin[...] * dot)
-    done_t()
     drain()
     for j in range(pieces):
         swap(j).wait_send()
         reduces[j][3]()
+
+
+def emit(count, *refs):
+    sources, (vectors, roots) = refs[:count], refs[count : count + 2]
+    targets = refs[count + 2 : 2 * count + 2]
+    outs, stats = refs[2 * count + 2 : 2 * count + 6], refs[2 * count + 6]
+    held, sem = refs[2 * count + 7 : 3 * count + 7], refs[3 * count + 7]
+    loads = [
+        pltpu.make_async_copy(src, dst, sem.at[0, i])
+        for i, (src, dst) in enumerate(zip(sources, held))
+    ]
+    stores = [
+        pltpu.make_async_copy(src, dst, sem.at[1, i])
+        for i, (src, dst) in enumerate(zip(held, targets))
+    ]
+    for copy in loads:
+        copy.start()
+    for k, out in enumerate(outs):
+        out[...] = vectors[k, :]
+    for k in range(3):
+        stats[k] = roots[4 + k, 0]
+    for load, store in zip(loads, stores):
+        load.wait()
+        store.start()
+    for copy in stores:
+        copy.wait()
 
 
 def params(collective=None, limit=VMEM_LIMIT):
@@ -1420,18 +1518,6 @@
     def padded(w):
         return w if ffp == ff else jnp.pad(w, ((0, 0), (0, ffp - ff)))
 
-    total = lengths[0] + lengths[1]
-    bound = layer_index[0].astype(F32) / LAYERS
-    consts = jnp.stack(
-        [
-            forget_bias,
-            state_gain.astype(F32),
-            jnp.broadcast_to(bound, (width,)),
-            gain_mid.astype(F32),
-            gain_in.astype(F32),
-        ]
-        + [jnp.zeros((width,), F32)] * 3
-    )
     plane = shape((rows, chan), F32)
     plane16 = shape((rows, chan), BF)
     column = shape((rows, 1), F32)
@@ -1452,11 +1538,12 @@
 
     (
         ipre, fpre, opre, feff, states, gated, normed_in, nmid, mixed, w1, w2, invst, invmid, inv_in,
+        consts,
     ) = pl.pallas_call(
         functools.partial(mixer_forward, n, t, width),
-        out_shape=saved + [wide16, wide16, w1s, w2s, column, column, column],
-        in_specs=[SM] + [HB] * 8 + [VM],
-        out_specs=[HB] * 11 + [VM] * 3,
+        out_shape=saved + [wide16, wide16, w1s, w2s, column, column, column, shape((8, width), F32)],
+        in_specs=[SM] * 2 + [HB] * 4 + [VM] + [HB] * 3 + [VM] * 4,
+        out_specs=[HB] * 11 + [VM] * 4,
         scratch_shapes=[
             *vm(wide16, wide16, plane, plane, plane, groups(8), groups(8), plane16, wide16, w1s),
             *vm(groups(), plane),
@@ -1465,7 +1552,10 @@
             zslot,
             pltpu.VMEM((rows, width), BF),
             pltpu.VMEM((2, rows, width), BF),
-            DMA, DMA((7,)), DMA((4,)), DMA((CHUNKS,)), DMA((CHUNKS,)),
+            pltpu.VMEM((width // n, chan), BF),
+            pltpu.VMEM((width // n, ffp), BF),
+            pltpu.VMEM((ff, width // n), BF),
+            DMA, DMA, DMA((7,)), DMA((4,)), DMA((CHUNKS,)), DMA((CHUNKS,)),
             *small,
             *line_sems(CHUNKS),
             *gather_sems(n, 4),
@@ -1474,21 +1564,21 @@
         compiler_params=params(1),
         name="mixer_forward",
     )(
-        lengths, hidden_in, w_input, w_forget, w_outgate, w_output.T,
-        padded(w_gate), padded(w_up), padded(w_down.T), consts,
+        lengths, layer_index, hidden_in, w_input, w_forget, w_outgate, w_output,
+        padded(w_gate), padded(w_up), w_down, forget_bias, state_gain, gain_mid, gain_in,
     )
 
     shard, chips, tile, step = width // n, n // 2, rows // TILES, rows // CHUNKS
     piece = shape((shard, ffp), F32)
     ffs = shape((rows, ffp), BF)
-    gmix, gres, glu_part, ggain, sums2, down = pl.pallas_call(
+    gmix, gres, glu_part, ggain, sum_gate, sum_up, down = pl.pallas_call(
         functools.partial(feed_forward, n, t, width),
         out_shape=[
-            wide16, plane, shards16, shape((8, width), F32), shape((2, shard, ffp), F32),
+            wide16, plane, shards16, shape((8, width), F32), piece, piece,
             shape((width // 2, ffp), BF),
         ],
         in_specs=[HB] * 5 + [VM] * 2,
-        out_specs=[HB] * 3 + [VM] + [HB] * 2,
+        out_specs=[HB] * 3 + [VM] + [HB] * 3,
         scratch_shapes=[
             *vm(wide16, wide16, w2s, ffs, ffs, ffs),
             pltpu.VMEM((2, t, tile, chan), BF),
@@ -1513,13 +1603,14 @@
 
     shard_sems = [DMA((t, SHARD_CHUNKS))] * 4
     shard_bufs = [pltpu.VMEM((t, rows, chan), BF), pltpu.VMEM((t + 1, rows, chan), BF)]
-    gni_part, dw1, vecs, block_out, sum_down = pl.pallas_call(
+    gni_part, dw1, vecs, block_out, dot_in, sum_down = pl.pallas_call(
         functools.partial(mixer_backward, n, t, width),
         out_shape=[
-            shards16, shape((2, width // 2, 4 * chan), BF), shape((8, chan), F32), plane16, piece,
+            shards16, shape((2, width // 2, 4 * chan), BF), shape((8, chan), F32), plane16, column,
+            shape((ffp, shard), F32),
         ],
-        in_specs=[SM] + [HB] * 13 + [VM] * 2,
-        out_specs=[HB] * 2 + [VM] * 3,
+        in_specs=[SM] + [HB] * 13 + [VM] * 3,
+        out_specs=[HB] * 2 + [VM] * 4,
         scratch_shapes=[
             pltpu.VMEM((width // 2, ffp), BF),
             *vm(wide16, wide16),
@@ -1528,12 +1619,17 @@
             *vm(groups(), groups(), plane, shape((rows, 3 * chan), BF)),
             vslot,
             zslot,
-            *vm(plane16, plane16),
+            zslot,
+            pltpu.VMEM((8, width), F32),
+            pltpu.VMEM((t, 8, chan), F32),
+            pltpu.VMEM((t, 8, chan), F32),
+            *vm(wide16, plane16),
             *shard_bufs,
             *vm(shards16),
             pltpu.VMEM((2, 2, shard, 4 * chan), BF),
             DMA((12,)),
             *small,
+            DMA((t,)), DMA((t,)), DMA((t,)), DMA((t,)),
             DMA((3,)),
             *shard_sems,
             DMA((3,)), DMA((2,)), DMA,
@@ -1543,52 +1639,52 @@
         name="mixer_backward",
     )(
         lengths, glu_part, hidden_in, mixed, gmix, normed_in, w1, gated, states, feff, ipre, fpre, opre,
-        down, invst, consts,
+        down, invst, inv_in, consts,
     )
 
-    grad_in, allvec, sums1 = pl.pallas_call(
+    square = shape((shard, chan), F32)
+    grad_in, vectors, rms, g_input, g_forget, g_outgate, g_output = pl.pallas_call(
         functools.partial(closing, n, t, width),
-        out_shape=[plane, shape((t, 8, chan), F32), shape((2, shard, 2 * chan), F32)],
-        in_specs=[HB] * 4 + [VM] * 4,
-        out_specs=[VM] * 3,
+        out_shape=[
+            plane, shape((8, width), F32), shape((8, LANE), F32),
+            square, square, square, shape((chan, shard), F32),
+        ],
+        in_specs=[SM] + [HB] * 4 + [VM] * 5,
+        out_specs=[VM] * 7,
         scratch_shapes=[
             pltpu.VMEM((2, width // 2, 2 * chan), BF),
             pltpu.VMEM((2, width // 2, 2 * chan), BF),
             *vm(plane16, plane),
             *shard_bufs,
-            *vm(plane, plane),
-            zslot,
             vslot,
+            pltpu.VMEM((t, 8, chan), F32),
             DMA((2,)), DMA((2, 2)), DMA, DMA((2,)),
             *shard_sems,
-            DMA((t,)), DMA((t,)), DMA((n,)), DMA((n,)), DMA((t,)), DMA((t,)),
+            DMA((n,)), DMA((n,)), DMA((t,)), DMA((t,)),
             *grid_buffers(n, width, 2, 2 * chan),
         ],
         compiler_params=params(4),
         name="closing",
-    )(gni_part, dw1, hidden_in, gres, inv_in, consts, vecs, ggain)
-
-    def vector(r):
-        return allvec[:, r, :].reshape(width)
-
-    squares = jnp.stack([jnp.sum(allvec[:, r, :]) for r in (4, 5, 6)])
-    rms_stats = jnp.sqrt(squares / (total.astype(F32) * width))
-
+    )(lengths, gni_part, dw1, hidden_in, gres, inv_in, dot_in, consts, vecs, ggain)
+
+    arrays = (
+        block_out, grad_in, g_input, g_forget, g_outgate, g_output, sum_gate[:, :ff], sum_up[:, :ff],
+        sum_down[:ff],
+    )
+    count = len(arrays)
+    *copies, gain0, bias0, gain1, gain2, rms_stats = pl.pallas_call(
+        functools.partial(emit, count),
+        out_shape=[shape(a.shape, a.dtype) for a in arrays] + [shape((width,), F32)] * 4 + [shape((3,), F32)],
+        in_specs=[HB] * count + [VM, SM],
+        out_specs=[HB] * count + [VM] * 4 + [SM],
+        scratch_shapes=[pltpu.VMEM(a.shape, a.dtype) for a in arrays] + [DMA((2, count))],
+        compiler_params=params(),
+        name="emit",
+    )(*arrays, vectors, rms)
+    out, gin, g_input, g_forget, g_outgate, g_output, g_gate, g_up, g_down = copies
     return (
-        block_out,
-        grad_in,
-        vector(0),
-        sums1[0, :, :chan],
-        sums1[0, :, chan:],
-        vector(1),
-        sums1[1, :, :chan],
-        vector(2),
-        sums1[1, :, chan:].T,
-        vector(3),
-        sums2[0, :, :ff],
-        sums2[1, :, :ff],
-        sum_down[:, :ff].T,
-        rms_stats,
+        out, gin, gain0, g_input, g_forget, bias0, g_outgate, gain1, g_output, gain2,
+        g_gate, g_up, g_down, rms_stats,
     )
 
 

time: 416 us -> 390 us (0.938)
  local copies, waits for them, and re-layouts: 17.3 us -> 0 us
  other arithmetic: 7.02 us -> 0 us
    unnamed x14 -> x0, local copies, waits for them, and re-layouts: 10.8 us -> none
    pallas_call x0 -> x1, Pallas kernels: none -> 8.42 us  [on_device(): pl.pallas_call(functools.partial(emit, count), out_shape=[shape(a.shape,...]
    pallas_call x1, Pallas kernels: 71.5 us -> 64.5 us  [on_device(): pl.pallas_call(functools.partial(closing, n, t, width), out_shape=[plane,...]
    pallas_call x1, Pallas kernels: 111 us -> 106 us  [on_device(): pl.pallas_call(functools.partial(feed_forward, n, t, width), out_shape=[w...]
where the time goes in v5:
time: 390 us; the launch traced here: 389 us
  Pallas kernels  388 us (99%)
    pallas_call x1, Pallas kernels, on_device(): pl.pallas_call(functools.partial(mixer_forward, n, t, width), out_shape=s...  135 us
    pallas_call x1, Pallas kernels, on_device(): pl.pallas_call(functools.partial(feed_forward, n, t, width), out_shape=[w...  106 us
    pallas_call x1, Pallas kernels, on_device(): pl.pallas_call(functools.partial(mixer_backward, n, t, width), out_shape=...  74.3 us
    pallas_call x1, Pallas kernels, on_device(): pl.pallas_call(functools.partial(closing, n, t, width), out_shape=[plane,...  64.5 us
    pallas_call x1, Pallas kernels, on_device(): pl.pallas_call(functools.partial(emit, count), out_shape=[shape(a.shape,...  8.42 us

profile of v5, /device:TPU:0, one launch (start us, length us, event | category | flops | bytes accessed | tf_op | source)
XLA Modules:
  0.0 389.5 jit_solution(13384925232643912731)
XLA Ops:
  1.3 134.7 %mixer_forward.1 = (f32[768,512]{1,0:T(8,128)}, f32[768,512]{1,0:T(8,128)}, f32[768,512]{1,0:T(8,128)}, f32[4,776,128]{2,1,0:T(8,128)}, f32[4,776,128]{2,1,0:T(8...) custom-call(s32[2]{0:T(128)} %lens.5, ...), custom_call_target="tpu_custom_call" | custom-call | tf_op jit(solution)/shard_map/mixer_forward/pallas_call | solution.py:1542
  136.0 106.0 %feed_forward.1 = (bf16[768,2048]{1,0:T(8,128)(2,1)}, f32[768,512]{1,0:T(8,128)}, bf16[4,768,512]{2,1,0:T(8,128)(2,1)}, f32[8,2048]{1,0:T(8,128)}, f32[256,1408]...) custom-call(bf16[768,2048]{1,0:T(8,128)(2,1)} %get-tuple-element.63.nmid_h, bf16[768,2048]{1,0:T(8,128)(2,1)} %cot_h.1, ...), custom_call_target="tpu_custom_call" | custom-call | tf_op jit(solution)/shard_map/feed_forward/pallas_call | solution.py:1574
  242.1 74.3 %mixer_backward.1 = (bf16[4,768,512]{2,1,0:T(8,128)(2,1)}, bf16[2,1024,2048]{2,1,0:T(8,128)(2,1)}, f32[8,512]{1,0:T(8,128)}, bf16[768,512]{1,0:T(8,128)(2,1)}, f32[768,1]{1,0:T(8,128)}, /*index=5*/f32[1408,256]{1,0:T(8,128)}) custom-call(s32[2]{0:T(128)} %lens.5, bf16[4,768,512]{2,1,0:T(8,128)(2,1)} %get-tuple-element.68.glu_h, bf16[768,2048]{1,0:T(8,128)(2,1)} %x_h.7, ...), custom_call_target="tpu_custom_call" | custom-call | tf_op jit(solution)/shard_map/mixer_backward/pallas_call | solution.py:1606
  316.4 64.5 %closing.1 = (f32[768,512]{1,0:T(8,128)}, f32[8,2048]{1,0:T(8,128)}, f32[8,128]{1,0:T(8,128)}, f32[256,512]{1,0:T(8,128)}, f32[256,512]{1,0:T(8,128)}, /*index=5*/f32[256,512]{1,0:T(8,128)}, f32[512,256]{1,0:T(8,128)}) custom-call(s32[2]{0:T(128)} %lens.5, bf16[4,768,512]{2,1,0:T(8,128)(2,1)} %get-tuple-element.82.gni_h, ...), custom_call_target="tpu_custom_call" | custom-call | tf_op jit(solution)/shard_map/closing/pallas_call | solution.py:1646
  380.9 8.4 %emit.1 = (bf16[768,512]{1,0:T(8,128)(2,1)}, f32[768,512]{1,0:T(8,128)}, f32[256,512]{1,0:T(8,128)}, f32[256,512]{1,0:T(8,128)}, f32[256,512]{1,0:T(8,128)}, /*i...) custom-call(bf16[768,512]{1,0:T(8,128)(2,1)} %get-tuple-element.81.r, ...), custom_call_target="tpu_custom_call" | custom-call | tf_op jit(solution)/shard_map/emit/pallas_call | solution.py:1675

commit v6 on v5

--- a/solution.py
+++ b/solution.py
@@ -250,7 +250,7 @@
     return chunks + lag_in * (half - 1) + lag_turn + lag_out * (half - 1), turn, drain
 
 
-def line_reduce_scatter(t, seq, tp, own, inbox, sems, finish):
+def line_reduce_scatter(t, seq, tp, own, inbox, sems, finish, lead):
     s_r, r_r, s_l, r_l = sems
     rows = own.shape[1]
     chunks = SHARD_CHUNKS
@@ -286,7 +286,7 @@
         ).astype(BF)
 
     def right_turn(i):
-        k, j = i // (t - 1), lax.rem(i, t - 1)
+        j, k = i // chunks, lax.rem(i, chunks)
         q = t - 1 - j
 
         @pl.when((i >= 0) & (i < count) & (q > tp))
@@ -299,7 +299,7 @@
             rightward(q, k).start()
 
     def left_turn(i):
-        k, q = i // (t - 1), lax.rem(i, t - 1)
+        q, k = i // chunks, lax.rem(i, chunks)
 
         @pl.when((i >= 0) & (i < count) & (q < tp))
         def _():
@@ -310,9 +310,20 @@
 
             leftward(q, k).start()
 
+    def begin():
+        for i in range(lead):
+
+            @pl.when(tp == 0)
+            def _(i=i):
+                right_turn(i)
+
+            @pl.when(tp == t - 1)
+            def _(i=i):
+                left_turn(i)
+
     def turn(i):
-        right_turn(i - HOP_LAG * tp)
-        left_turn(i - HOP_LAG * (t - 1 - tp))
+        right_turn(i - jnp.where(tp == 0, -lead, HOP_LAG * tp))
+        left_turn(i - jnp.where(tp == t - 1, -lead, HOP_LAG * (t - 1 - tp)))
 
     def last(k):
         @pl.when(tp == 0)
@@ -338,8 +349,7 @@
 
     def drain():
         def sent(i, c):
-            k = i // (t - 1)
-            j = lax.rem(i, t - 1)
+            j, k = i // chunks, lax.rem(i, chunks)
 
             @pl.when(t - 1 - j > tp)
             def _():
@@ -353,7 +363,8 @@
 
         lax.fori_loop(0, count, sent, 0)
 
-    return count + HOP_LAG * (t - 2), turn, last, drain
+    turns = max((t - 1 - p) * chunks + (HOP_LAG * p if p else -lead) for p in range(t - 1))
+    return turns, begin, turn, last, drain
 
 
 def chip_grid(n):
@@ -1119,8 +1130,10 @@
         vecs[5:6, :] += jnp.sum(ok * values * values, axis=0, keepdims=True)
         vecs[6:7, :] += jnp.sum(ok * full * full, axis=0, keepdims=True)
 
-    turns, turn, last, drain = line_reduce_scatter(t, seq, tp, own, inbox, (sr, rr, sl, rl), finish)
-    slots = 23
+    turns, begin, turn, last, drain = line_reduce_scatter(
+        t, seq, tp, own, inbox, (sr, rr, sl, rl), finish, 0
+    )
+    slots = 12
 
     def pump(slot):
         def one(i, c):
@@ -1131,14 +1144,16 @@
 
     fetches[0].wait()
     pump(0)
-    pump(1)
     down.wait()
     far()
     for copy in inputs[:4]:
         copy.wait()
 
     def gates(i, c):
-        pump(2 + i)
+        @pl.when(i == 1)
+        def _():
+            pump(1)
+
         at = pl.ds(pl.multiple_of(i * tile, tile), tile)
         shifted = pl.ds(pl.multiple_of(i * tile + 8, 8), tile)
         g = nn(gmix[at, :], w1[:, 3 * chan :])
@@ -1154,7 +1169,7 @@
         return c
 
     lax.fori_loop(0, 3, gates, 0)
-    dot = sum_over_tp(row_sums(inner[...]), t, seq, tp, zslots, zs, zr, lambda: pump(5)) / width
+    dot = sum_over_tp(row_sums(inner[...]), t, seq, tp, zslots, zs, zr, lambda: (pump(2), pump(3))) / width
     inner[:, 0:1] = dot
 
     def leaving(i, c):
@@ -1166,7 +1181,7 @@
 
     lax.fori_loop(0, 3, leaving, 0)
     inputs[4].wait()
-    pump(6)
+    pump(4)
 
     length = rows // SEG
 
@@ -1190,14 +1205,15 @@
         block_p = p[s : s + 1] * block_p
     first = get(feff, slice(0, 1))
     arriving = carry_over_seq(
-        first * block_p, first * block_h, n, seq, tp, cslots, cs, cr, True, lambda: pump(7)
+        first * block_p, first * block_h, n, seq, tp, cslots, cs, cr, True, lambda: (pump(5), pump(6))
     )
     inputs[5].wait()
     inputs[6].wait()
     middle()
     bias_sum = jnp.zeros((1, chan), F32)
     for s in range(SEG - 1, -1, -1):
-        pump(15 - s)
+        if s in (5, 1):
+            pump(8 - s // 5)
         at = slice(s * length, (s + 1) * length)
         gs = get(weighted, at) + get(prod, at) * arriving
         arriving = h[s : s + 1] + p[s : s + 1] * arriving
@@ -1235,7 +1251,7 @@
         for k in range(LANE, width, LANE):
             short = short + product[:, k : k + LANE]
         inner[at, :LANE] = short
-        pump(16 + i)
+        pump(9 + i)
         return c
 
     lax.fori_loop(0, 3, spread_in, 0)
@@ -1295,16 +1311,9 @@
         keep(slot, 0, tn(normed[:, at], out3[...]).astype(BF))
         keep(slot, 3 * chan, tn(gmix[:, at], gated[...]).astype(BF))
         d_copy(r, slot).start()
-
-        @pl.when(r < 4)
-        def _():
-            pump(19 + r)
-
         return c
 
     lax.fori_loop(0, chips, slab, 0)
-    for r in range(chips, 4):
-        pump(19 + r)
 
     done_z()
     total = zslots2[0]
@@ -1428,17 +1437,19 @@
         allvec[tp] = total
         go_t()
 
-    turns, turn, last, drain = line_reduce_scatter(t, seq, tp, own, inbox, (sr, rr, sl, rl), finish)
+    turns, begin, turn, last, drain = line_reduce_scatter(
+        t, seq, tp, own, inbox, (sr, rr, sl, rl), finish, HOP_LAG
+    )
     works = [
-        (1, vectors_on),
-        (2, lambda: (stage1(0), start(1))),
-        (5, lambda: stage1(1)),
-        (6, lambda: stage2(0)),
-        (9, lambda: stage3(0)),
-        (10, lambda: stage2(1)),
-        (13, lambda: stage3(1)),
+        (0, lambda: (stage1(0), start(1), vectors_on())),
+        (2, lambda: stage1(1)),
+        (4, lambda: stage2(0)),
+        (6, lambda: stage3(0)),
+        (7, lambda: stage2(1)),
+        (9, lambda: stage3(1)),
     ]
-    slots = 16
+    slots = 10
+    begin()
 
     def turn_of(slot):
         def one(i, c):

time: 390 us -> 378 us (0.969)
  Pallas kernels: 388 us -> 376 us
    pallas_call x1, Pallas kernels: 74.3 us -> 66.4 us  [on_device(): pl.pallas_call(functools.partial(mixer_backward, n, t, width), out_shape=...]
    pallas_call x1, Pallas kernels: 64.5 us -> 60.1 us  [on_device(): pl.pallas_call(functools.partial(closing, n, t, width), out_shape=[plane,...]
where the time goes in v6:
time: 378 us; the launch traced here: 377 us
  Pallas kernels  376 us (99%)
    pallas_call x1, Pallas kernels, on_device(): pl.pallas_call(functools.partial(mixer_forward, n, t, width), out_shape=s...  135 us
    pallas_call x1, Pallas kernels, on_device(): pl.pallas_call(functools.partial(feed_forward, n, t, width), out_shape=[w...  106 us
    pallas_call x1, Pallas kernels, on_device(): pl.pallas_call(functools.partial(mixer_backward, n, t, width), out_shape=...  66.4 us
    pallas_call x1, Pallas kernels, on_device(): pl.pallas_call(functools.partial(closing, n, t, width), out_shape=[plane,...  60.1 us
    pallas_call x1, Pallas kernels, on_device(): pl.pallas_call(functools.partial(emit, count), out_shape=[shape(a.shape,...  8.42 us

profile of v6, /device:TPU:0, one launch (start us, length us, event | category | flops | bytes accessed | tf_op | source)
XLA Modules:
  0.0 377.2 jit_solution(15611852019337445756)
XLA Ops:
  1.3 134.7 %mixer_forward.1 = (f32[768,512]{1,0:T(8,128)}, f32[768,512]{1,0:T(8,128)}, f32[768,512]{1,0:T(8,128)}, f32[4,776,128]{2,1,0:T(8,128)}, f32[4,776,128]{2,1,0:T(8...) custom-call(s32[2]{0:T(128)} %lens.5, ...), custom_call_target="tpu_custom_call" | custom-call | tf_op jit(solution)/shard_map/mixer_forward/pallas_call | solution.py:1553
  136.0 106.0 %feed_forward.1 = (bf16[768,2048]{1,0:T(8,128)(2,1)}, f32[768,512]{1,0:T(8,128)}, bf16[4,768,512]{2,1,0:T(8,128)(2,1)}, f32[8,2048]{1,0:T(8,128)}, f32[256,1408]...) custom-call(bf16[768,2048]{1,0:T(8,128)(2,1)} %get-tuple-element.63.nmid_h, bf16[768,2048]{1,0:T(8,128)(2,1)} %cot_h.1, ...), custom_call_target="tpu_custom_call" | custom-call | tf_op jit(solution)/shard_map/feed_forward/pallas_call | solution.py:1585
  242.1 66.4 %mixer_backward.1 = (bf16[4,768,512]{2,1,0:T(8,128)(2,1)}, bf16[2,1024,2048]{2,1,0:T(8,128)(2,1)}, f32[8,512]{1,0:T(8,128)}, bf16[768,512]{1,0:T(8,128)(2,1)}, f32[768,1]{1,0:T(8,128)}, /*index=5*/f32[1408,256]{1,0:T(8,128)}) custom-call(s32[2]{0:T(128)} %lens.5, bf16[4,768,512]{2,1,0:T(8,128)(2,1)} %get-tuple-element.68.glu_h, bf16[768,2048]{1,0:T(8,128)(2,1)} %x_h.7, ...), custom_call_target="tpu_custom_call" | custom-call | tf_op jit(solution)/shard_map/mixer_backward/pallas_call | solution.py:1617
  308.4 60.1 %closing.1 = (f32[768,512]{1,0:T(8,128)}, f32[8,2048]{1,0:T(8,128)}, f32[8,128]{1,0:T(8,128)}, f32[256,512]{1,0:T(8,128)}, f32[256,512]{1,0:T(8,128)}, /*index=5*/f32[256,512]{1,0:T(8,128)}, f32[512,256]{1,0:T(8,128)}) custom-call(s32[2]{0:T(128)} %lens.5, bf16[4,768,512]{2,1,0:T(8,128)(2,1)} %get-tuple-element.82.gni_h, ...), custom_call_target="tpu_custom_call" | custom-call | tf_op jit(solution)/shard_map/closing/pallas_call | solution.py:1657
  368.6 8.4 %emit.1 = (bf16[768,512]{1,0:T(8,128)(2,1)}, f32[768,512]{1,0:T(8,128)}, f32[256,512]{1,0:T(8,128)}, f32[256,512]{1,0:T(8,128)}, f32[256,512]{1,0:T(8,128)}, /*i...) custom-call(bf16[768,512]{1,0:T(8,128)(2,1)} %get-tuple-element.81.r, ...), custom_call_target="tpu_custom_call" | custom-call | tf_op jit(solution)/shard_map/emit/pallas_call | solution.py:1686

commit v7 on v6

--- a/solution.py
+++ b/solution.py
@@ -826,7 +826,7 @@
     ]
 
     count, turn, drain = line_all_reduce(
-        t, seq, tp, rows, CHUNKS, partial, send, buf, (s_in, s_out, r_buf), finish, (0, 1, 3)
+        t, seq, tp, rows, CHUNKS, partial, send, buf, (s_in, s_out, r_buf), finish, (0, 1, 4)
     )
     loop_with(0, count, turn, turns)
     drain()
@@ -862,8 +862,8 @@
         pltpu.make_async_copy(cot_h, cot, s_a.at[1]),
     ]
     w_copies = [pltpu.make_async_copy(w2_h.at[j], pool.at[j], s_w.at[j]) for j in range(3)]
+    w_copies[0].start()
     act_copies[0].start()
-    w_copies[0].start()
     greet_all(n, t, seq, tp)
     for copy in (w_copies[1], act_copies[1], w_copies[2]):
         copy.start()

time: 378 us -> 378 us (level)
  no operation moved by 1% of the time
where the time goes in v7:
time: 378 us; the launch traced here: 377 us
  Pallas kernels  376 us (99%)
    pallas_call x1, Pallas kernels, on_device(): pl.pallas_call(functools.partial(mixer_forward, n, t, width), out_shape=s...  135 us
    pallas_call x1, Pallas kernels, on_device(): pl.pallas_call(functools.partial(feed_forward, n, t, width), out_shape=[w...  106 us
    pallas_call x1, Pallas kernels, on_device(): pl.pallas_call(functools.partial(mixer_backward, n, t, width), out_shape=...  66.4 us
    pallas_call x1, Pallas kernels, on_device(): pl.pallas_call(functools.partial(closing, n, t, width), out_shape=[plane,...  60.1 us
    pallas_call x1, Pallas kernels, on_device(): pl.pallas_call(functools.partial(emit, count), out_shape=[shape(a.shape,...  8.42 us

profile of v7, /device:TPU:0, one launch (start us, length us, event | category | flops | bytes accessed | tf_op | source)
XLA Modules:
  0.0 377.2 jit_solution(1286718216675424646)
XLA Ops:
  1.3 134.7 %mixer_forward.1 = (f32[768,512]{1,0:T(8,128)}, f32[768,512]{1,0:T(8,128)}, f32[768,512]{1,0:T(8,128)}, f32[4,776,128]{2,1,0:T(8,128)}, f32[4,776,128]{2,1,0:T(8...) custom-call(s32[2]{0:T(128)} %lens.5, ...), custom_call_target="tpu_custom_call" | custom-call | tf_op jit(solution)/shard_map/mixer_forward/pallas_call | solution.py:1553
  136.0 106.0 %feed_forward.1 = (bf16[768,2048]{1,0:T(8,128)(2,1)}, f32[768,512]{1,0:T(8,128)}, bf16[4,768,512]{2,1,0:T(8,128)(2,1)}, f32[8,2048]{1,0:T(8,128)}, f32[256,1408]...) custom-call(bf16[768,2048]{1,0:T(8,128)(2,1)} %get-tuple-element.63.nmid_h, bf16[768,2048]{1,0:T(8,128)(2,1)} %cot_h.1, ...), custom_call_target="tpu_custom_call" | custom-call | tf_op jit(solution)/shard_map/feed_forward/pallas_call | solution.py:1585
  242.0 66.4 %mixer_backward.1 = (bf16[4,768,512]{2,1,0:T(8,128)(2,1)}, bf16[2,1024,2048]{2,1,0:T(8,128)(2,1)}, f32[8,512]{1,0:T(8,128)}, bf16[768,512]{1,0:T(8,128)(2,1)}, f32[768,1]{1,0:T(8,128)}, /*index=5*/f32[1408,256]{1,0:T(8,128)}) custom-call(s32[2]{0:T(128)} %lens.5, bf16[4,768,512]{2,1,0:T(8,128)(2,1)} %get-tuple-element.68.glu_h, bf16[768,2048]{1,0:T(8,128)(2,1)} %x_h.7, ...), custom_call_target="tpu_custom_call" | custom-call | tf_op jit(solution)/shard_map/mixer_backward/pallas_call | solution.py:1617
  308.4 60.1 %closing.1 = (f32[768,512]{1,0:T(8,128)}, f32[8,2048]{1,0:T(8,128)}, f32[8,128]{1,0:T(8,128)}, f32[256,512]{1,0:T(8,128)}, f32[256,512]{1,0:T(8,128)}, /*index=5*/f32[256,512]{1,0:T(8,128)}, f32[512,256]{1,0:T(8,128)}) custom-call(s32[2]{0:T(128)} %lens.5, bf16[4,768,512]{2,1,0:T(8,128)(2,1)} %get-tuple-element.82.gni_h, ...), custom_call_target="tpu_custom_call" | custom-call | tf_op jit(solution)/shard_map/closing/pallas_call | solution.py:1657
  368.6 8.4 %emit.1 = (bf16[768,512]{1,0:T(8,128)(2,1)}, f32[768,512]{1,0:T(8,128)}, f32[256,512]{1,0:T(8,128)}, f32[256,512]{1,0:T(8,128)}, f32[256,512]{1,0:T(8,128)}, /*i...) custom-call(bf16[768,512]{1,0:T(8,128)(2,1)} %get-tuple-element.81.r, ...), custom_call_target="tpu_custom_call" | custom-call | tf_op jit(solution)/shard_map/emit/pallas_call | solution.py:1686

commit v8 on v6

--- a/solution.py
+++ b/solution.py
@@ -1131,7 +1131,7 @@
         vecs[6:7, :] += jnp.sum(ok * full * full, axis=0, keepdims=True)
 
     turns, begin, turn, last, drain = line_reduce_scatter(
-        t, seq, tp, own, inbox, (sr, rr, sl, rl), finish, 0
+        t, seq, tp, own, inbox, (sr, rr, sl, rl), finish, 1
     )
     slots = 12
 
@@ -1143,6 +1143,7 @@
         lax.fori_loop(slot * turns // slots, (slot + 1) * turns // slots, one, 0)
 
     fetches[0].wait()
+    begin()
     pump(0)
     down.wait()
     far()

time: 378 us -> 378 us (level)
  no operation moved by 1% of the time
where the time goes in v8:
time: 378 us
  Pallas kernels  376 us (99%)
    pallas_call x1, Pallas kernels, on_device(): pl.pallas_call(functools.partial(mixer_forward, n, t, width), out_shape=s...  135 us
    pallas_call x1, Pallas kernels, on_device(): pl.pallas_call(functools.partial(feed_forward, n, t, width), out_shape=[w...  106 us
    pallas_call x1, Pallas kernels, on_device(): pl.pallas_call(functools.partial(mixer_backward, n, t, width), out_shape=...  66.8 us
    pallas_call x1, Pallas kernels, on_device(): pl.pallas_call(functools.partial(closing, n, t, width), out_shape=[plane,...  60.1 us
    pallas_call x1, Pallas kernels, on_device(): pl.pallas_call(functools.partial(emit, count), out_shape=[shape(a.shape,...  8.42 us

profile of v8, /device:TPU:0, one launch (start us, length us, event | category | flops | bytes accessed | tf_op | source)
XLA Modules:
  0.0 377.6 jit_solution(6582407554153956213)
XLA Ops:
  1.3 134.7 %mixer_forward.1 = (f32[768,512]{1,0:T(8,128)}, f32[768,512]{1,0:T(8,128)}, f32[768,512]{1,0:T(8,128)}, f32[4,776,128]{2,1,0:T(8,128)}, f32[4,776,128]{2,1,0:T(8...) custom-call(s32[2]{0:T(128)} %lens.5, ...), custom_call_target="tpu_custom_call" | custom-call | tf_op jit(solution)/shard_map/mixer_forward/pallas_call | solution.py:1554
  136.0 106.0 %feed_forward.1 = (bf16[768,2048]{1,0:T(8,128)(2,1)}, f32[768,512]{1,0:T(8,128)}, bf16[4,768,512]{2,1,0:T(8,128)(2,1)}, f32[8,2048]{1,0:T(8,128)}, f32[256,1408]...) custom-call(bf16[768,2048]{1,0:T(8,128)(2,1)} %get-tuple-element.63.nmid_h, bf16[768,2048]{1,0:T(8,128)(2,1)} %cot_h.1, ...), custom_call_target="tpu_custom_call" | custom-call | tf_op jit(solution)/shard_map/feed_forward/pallas_call | solution.py:1586
  242.1 66.8 %mixer_backward.1 = (bf16[4,768,512]{2,1,0:T(8,128)(2,1)}, bf16[2,1024,2048]{2,1,0:T(8,128)(2,1)}, f32[8,512]{1,0:T(8,128)}, bf16[768,512]{1,0:T(8,128)(2,1)}, f32[768,1]{1,0:T(8,128)}, /*index=5*/f32[1408,256]{1,0:T(8,128)}) custom-call(s32[2]{0:T(128)} %lens.5, bf16[4,768,512]{2,1,0:T(8,128)(2,1)} %get-tuple-element.68.glu_h, bf16[768,2048]{1,0:T(8,128)(2,1)} %x_h.7, ...), custom_call_target="tpu_custom_call" | custom-call | tf_op jit(solution)/shard_map/mixer_backward/pallas_call | solution.py:1618
  308.9 60.1 %closing.1 = (f32[768,512]{1,0:T(8,128)}, f32[8,2048]{1,0:T(8,128)}, f32[8,128]{1,0:T(8,128)}, f32[256,512]{1,0:T(8,128)}, f32[256,512]{1,0:T(8,128)}, /*index=5*/f32[256,512]{1,0:T(8,128)}, f32[512,256]{1,0:T(8,128)}) custom-call(s32[2]{0:T(128)} %lens.5, bf16[4,768,512]{2,1,0:T(8,128)(2,1)} %get-tuple-element.82.gni_h, ...), custom_call_target="tpu_custom_call" | custom-call | tf_op jit(solution)/shard_map/closing/pallas_call | solution.py:1658
  369.0 8.4 %emit.1 = (bf16[768,512]{1,0:T(8,128)(2,1)}, f32[768,512]{1,0:T(8,128)}, f32[256,512]{1,0:T(8,128)}, f32[256,512]{1,0:T(8,128)}, f32[256,512]{1,0:T(8,128)}, /*i...) custom-call(bf16[768,512]{1,0:T(8,128)(2,1)} %get-tuple-element.81.r, ...), custom_call_target="tpu_custom_call" | custom-call | tf_op jit(solution)/shard_map/emit/pallas_call | solution.py:1687
